TPU v7x, 128 devices: a whole 4x4x4 slice. The times are simulated.
128 devices in a mesh: pipe: 4 (over x), ctx: 16 (over z, y), tp: 2 (over core).
Axes of the slice: x: 4, y: 4, z: 4, core: 2. Of those that a mesh axis runs over, the one named last changes fastest.
Arguments:
- queries: bfloat16 [4, 2048, 4096], P('pipe', 'ctx', 'tp'), may hold values from -12 to 12
- forget_logits: bfloat16 [4, 2048, 4096], P('pipe', 'ctx', 'tp'), may hold values from -1 to 12
- values: bfloat16 [4, 2048, 4096], P('pipe', 'ctx', 'tp'), may hold values from -48 to 48
- gates: bfloat16 [4, 2048, 4096], P('pipe', 'ctx', 'tp'), may hold values from -6 to 6
- output_grad: bfloat16 [4, 2048, 4096], P('pipe', 'ctx', 'tp'), may hold values from -6 to 6
- lower_bound: float32 [4, 4096], P('pipe', 'tp'), may hold values from 0.45 to 0.7
- norm_gain: float32 [4, 4096], P('pipe', 'tp'), may hold values from 0.5 to 2
Outputs:
- handed_query_grad: bfloat16 [4, 2048, 4096], P('pipe', 'ctx', 'tp')
- handed_logit_grad: bfloat16 [4, 2048, 4096], P('pipe', 'ctx', 'tp')
- handed_value_grad: bfloat16 [4, 2048, 4096], P('pipe', 'ctx', 'tp')
- handed_gate_grad: bfloat16 [4, 2048, 4096], P('pipe', 'ctx', 'tp')
All inputs are finite; a program needn't handle non-finite values.
Results may differ from a plain program's by a relative error of at most 0.0024.
Values may be sent and summed in bfloat16 or wider, within the bound.
No kernel may reach another device: no remote copies, remote signals or barrier semaphores. Data moves between devices by JAX's collectives and lax.ppermute only.
A program may use at most 128 MiB of HBM per device.

v0:
```python
import jax
import jax.numpy as jnp
from jax import lax
from jax.sharding import PartitionSpec as P

DK = 128
BLOCK = 128
HEAD_COLUMNS = 4096


exact_arithmetic_mode = lax.Precision.HIGHEST
epsilon = 1e-06


def passed_along(x, axis, by):
    size = lax.axis_size(axis)
    pairs = [(i, i + by) for i in range(size) if 0 <= i + by < size]
    return lax.ppermute(x, axis, pairs)


def carried_in(value, axis, join, neutral):
    count, mine = (lax.axis_size(axis), lax.axis_index(axis))
    pieces = lax.all_gather(value, axis)
    pieces = pieces[::-1]
    mine = count - 1 - mine
    running = jnp.full_like(value, 0) + jnp.asarray(neutral, value.dtype)

    def carried_turn(position, running):
        longer = join(running, pieces[position])
        return jnp.where(position < mine, longer, running)

    return lax.fori_loop(0, count - 1, carried_turn, running)


def passed_along_2(x, axis, by):
    size = lax.axis_size(axis)
    return lax.ppermute(x, axis, [(i, (i + by) % size) for i in range(size)])


def causal_mask(length):
    row_index = lax.broadcasted_iota(jnp.int32, (length, length), 0)
    col_index = lax.broadcasted_iota(jnp.int32, (length, length), 1)
    return row_index >= col_index


def state_update(incoming_memory, pieces):
    key_block, value_tile, log_forget = pieces
    running_total = jnp.cumsum(log_forget, axis=0)
    final_cumulative_forgetting = running_total[-1]
    lookup_vector_leftover = key_block * jnp.exp(final_cumulative_forgetting[None] - running_total)
    fresh_state = jnp.einsum(
        "ycw,yco->cwo", lookup_vector_leftover, value_tile, precision=exact_arithmetic_mode
    )
    return (jnp.exp(final_cumulative_forgetting)[:, :, None] * incoming_memory + fresh_state, None)


def grad_update(incoming_memory, pieces):
    query_block, log_forget, result_derivative_piece = pieces
    running_total = jnp.cumsum(log_forget, axis=0)
    final_cumulative_forgetting = running_total[-1]
    probe_vector_scaled = query_block * jnp.exp(running_total)
    fresh_state = jnp.einsum(
        "ygw,ygq->gwq",
        probe_vector_scaled,
        result_derivative_piece,
        precision=exact_arithmetic_mode,
    )
    return (jnp.exp(final_cumulative_forgetting)[:, :, None] * incoming_memory + fresh_state, None)


def block_forward(incoming_memory, pieces):
    query_block, key_block, value_tile, log_forget = pieces
    running_total = jnp.cumsum(log_forget, axis=0)
    final_cumulative_forgetting = running_total[-1]
    probe_vector_scaled = query_block * jnp.exp(running_total)
    key_rescaled = key_block * jnp.exp(-running_total)
    lookup_vector_leftover = key_block * jnp.exp(final_cumulative_forgetting[None] - running_total)
    similarity_weights = jnp.einsum(
        "thk,shk->hts", probe_vector_scaled, key_rescaled, precision=exact_arithmetic_mode
    )
    similarity_weights = jnp.where(causal_mask(query_block.shape[0])[None], similarity_weights, 0.0)
    within = jnp.einsum(
        "hts,shv->thv", similarity_weights, value_tile, precision=exact_arithmetic_mode
    )
    across_heads = jnp.einsum(
        "ubl,bli->ubi", probe_vector_scaled, incoming_memory, precision=exact_arithmetic_mode
    )
    fresh_state = jnp.einsum(
        "ycw,yco->cwo", lookup_vector_leftover, value_tile, precision=exact_arithmetic_mode
    )
    revised_memory = (
        jnp.exp(final_cumulative_forgetting)[:, :, None] * incoming_memory + fresh_state
    )
    return (revised_memory, (within + across_heads, incoming_memory))


def block_backward(incoming_memory, pieces):
    query_block, key_block, value_tile, log_forget, result_derivative_piece, initial_state = pieces
    running_total = jnp.cumsum(log_forget, axis=0)
    final_cumulative_forgetting = running_total[-1]
    probe_vector_scaled = query_block * jnp.exp(running_total)
    key_rescaled = key_block * jnp.exp(-running_total)
    lookup_vector_leftover = key_block * jnp.exp(final_cumulative_forgetting[None] - running_total)
    causal = causal_mask(query_block.shape[0])[None]
    similarity_weights = jnp.einsum(
        "thk,shk->hts", probe_vector_scaled, key_rescaled, precision=exact_arithmetic_mode
    )
    similarity_weights = jnp.where(causal, similarity_weights, 0.0)
    pair_products = jnp.einsum(
        "thv,shv->hts", result_derivative_piece, value_tile, precision=exact_arithmetic_mode
    )
    pair_products = jnp.where(causal, pair_products, 0.0)
    query_gradient = jnp.exp(running_total) * (
        jnp.einsum("ulm,muf->luf", pair_products, key_rescaled, precision=exact_arithmetic_mode)
        + jnp.einsum(
            "lxp,xup->lxu", result_derivative_piece, initial_state, precision=exact_arithmetic_mode
        )
    )
    key_gradient = jnp.exp(-running_total) * jnp.einsum(
        "dxb,xdc->bdc", pair_products, probe_vector_scaled, precision=exact_arithmetic_mode
    ) + jnp.exp(final_cumulative_forgetting[None] - running_total) * jnp.einsum(
        "zod,qzd->qzo", incoming_memory, value_tile, precision=exact_arithmetic_mode
    )
    content_derivative = jnp.einsum(
        "iay,aiz->yiz", similarity_weights, result_derivative_piece, precision=exact_arithmetic_mode
    ) + jnp.einsum(
        "oxa,rox->roa", incoming_memory, lookup_vector_leftover, precision=exact_arithmetic_mode
    )
    revised_memory = jnp.exp(final_cumulative_forgetting)[
        :, :, None
    ] * incoming_memory + jnp.einsum(
        "ygw,ygq->gwq",
        probe_vector_scaled,
        result_derivative_piece,
        precision=exact_arithmetic_mode,
    )
    return (revised_memory, (query_gradient, key_gradient, content_derivative))


def combine_forward(earlier, later):
    return (earlier[0] * later[0], later[0][:, :, None] * earlier[1] + later[1])


def combine_backward(earlier, later):
    return (earlier[0] * later[0], later[1] + later[0][:, :, None] * earlier[1])


def add_terms(earlier, later):
    return earlier + later


def forward_relay(local_pair, identity):
    position = lax.axis_index("ctx")

    def forward_turn(turn_index, prefix):
        combined = combine_forward(prefix, local_pair)
        received = passed_along((combined[0], combined[1]), "ctx", 1)
        first = position == 0
        return (
            jnp.where(first, identity[0], received[0]),
            jnp.where(first, identity[1], received[1]),
        )

    return lax.fori_loop(0, lax.axis_size("ctx") - 1, forward_turn, identity)


def backward_relay(local_pair, identity):
    position = lax.axis_index("ctx")
    last_index = lax.axis_size("ctx") - 1

    def backward_turn(turn_index, suffix):
        combined = combine_backward(suffix, local_pair)
        received = passed_along((combined[0], combined[1]), "ctx", -1)
        final = position == last_index
        return (
            jnp.where(final, identity[0], received[0]),
            jnp.where(final, identity[1], received[1]),
        )

    return lax.fori_loop(0, lax.axis_size("ctx") - 1, backward_turn, identity)


def body(queries, forget_logits, values, gates, output_grad, lower_bound, norm_gain):
    group = queries.shape[1]
    width = queries.shape[2]
    heads = width // DK
    blocks = group // BLOCK
    query_rows = queries[0].astype(jnp.float32)
    squashed = jax.nn.sigmoid(forget_logits[0].astype(jnp.float32))
    bound_row = lower_bound[0][None]
    forget = bound_row + (1.0 - bound_row) * squashed
    key_rows = 1.0 - forget
    log_forget = jnp.log(forget)

    def split_blocks(matrix):
        return matrix.reshape(blocks, BLOCK, heads, DK)

    query_blocks = split_blocks(query_rows)
    key_blocks = split_blocks(key_rows)
    value_blocks = split_blocks(values[0].astype(jnp.float32))
    forget_blocks = split_blocks(log_forget)
    zero_state = jnp.zeros((heads, DK, DK), jnp.float32)
    unit_decay = jnp.ones((heads, DK), jnp.float32)
    group_decay = jnp.exp(jnp.sum(log_forget, axis=0)).reshape(heads, DK)
    local_state, unused_state = lax.scan(
        state_update, zero_state, (key_blocks, value_blocks, forget_blocks)
    )
    before_decay, initial_state = forward_relay(
        (group_decay, local_state), (unit_decay, zero_state)
    )
    end_state, (attended_blocks, start_states) = lax.scan(
        block_forward, initial_state, (query_blocks, key_blocks, value_blocks, forget_blocks)
    )
    attended = attended_blocks.reshape(group, width)
    gate_rows = gates[0].astype(jnp.float32)
    grad_rows = output_grad[0].astype(jnp.float32)
    gain_row = norm_gain[0][None]
    norm_grad = grad_rows * jax.nn.silu(gate_rows)
    squares, weighted = lax.psum(
        (jnp.sum(attended * attended, axis=1), jnp.sum(gain_row * norm_grad * attended, axis=1)),
        "tp",
    )
    root = jnp.sqrt(squares / HEAD_COLUMNS + epsilon)[:, None]
    normed = attended / root * gain_row
    gated = jax.nn.sigmoid(gate_rows)
    gate_grad = grad_rows * normed * gated * (1.0 + gate_rows * (1.0 - gated))
    attended_grad = gain_row * norm_grad / root - attended * weighted[:, None] / (
        HEAD_COLUMNS * root**3
    )
    dout_blocks = split_blocks(attended_grad)
    local_grad, unused_grad = lax.scan(
        grad_update, zero_state, (query_blocks, forget_blocks, dout_blocks), reverse=True
    )
    after_decay, end_grad = backward_relay((group_decay, local_grad), (unit_decay, zero_state))
    first_grad, (query_parts, key_parts, value_parts) = lax.scan(
        block_backward,
        end_grad,
        (query_blocks, key_blocks, value_blocks, forget_blocks, dout_blocks, start_states),
        reverse=True,
    )
    query_gradient = query_parts.reshape(group, width)
    key_gradient = key_parts.reshape(group, width)
    content_derivative = value_parts.reshape(group, width)
    term_blocks = (query_rows * query_gradient - key_rows * key_gradient).reshape(
        blocks, BLOCK, width
    )
    upper = causal_mask(BLOCK).T.astype(jnp.float32)
    within_sums = jnp.einsum("ts,bsc->btc", upper, term_blocks, precision=exact_arithmetic_mode)
    block_totals = jnp.sum(term_blocks, axis=1)
    later_blocks = jnp.cumsum(block_totals[::-1], axis=0)[::-1] - block_totals
    group_total = jnp.sum(block_totals, axis=0)
    later_groups = carried_in(group_total, "ctx", add_terms, jnp.zeros_like(group_total))
    log_grad = (within_sums + later_blocks[:, None, :]).reshape(group, width) + later_groups[None]
    logit_grad = (
        (log_grad / forget - key_gradient) * (1.0 - bound_row) * squashed * (1.0 - squashed)
    )
    stacked = jnp.stack([query_gradient, logit_grad, content_derivative, gate_grad]).astype(
        jnp.bfloat16
    )[:, None]
    handed = passed_along_2(stacked, "pipe", -1)
    return (handed[0], handed[1], handed[2], handed[3])


def solution(mesh):
    return jax.shard_map(
        body,
        mesh=mesh,
        in_specs=(
            P("pipe", "ctx", "tp"),
            P("pipe", "ctx", "tp"),
            P("pipe", "ctx", "tp"),
            P("pipe", "ctx", "tp"),
            P("pipe", "ctx", "tp"),
            P("pipe", "tp"),
            P("pipe", "tp"),
        ),
        out_specs=(
            P("pipe", "ctx", "tp"),
            P("pipe", "ctx", "tp"),
            P("pipe", "ctx", "tp"),
            P("pipe", "ctx", "tp"),
        ),
        check_vma=False,
    )
```

profile of v0, /device:TPU:0, one launch (start us, length us, event | category | flops | bytes accessed | tf_op | source)
XLA Modules:
  0.0 978.9 jit_solution(5075687566118707265)
XLA Ops:
  30.2 408.1 %while.27 = (s32[]{:T(128)}, f32[16,128,128]{2,1,0:T(8,128)S(1)}, pred[]{:T(512)}, f32[2048]{0:T(1024)S(1)}, f32[16,128,128]{2,1,0:T(8,128)}, /*index=5*/s32[]{:T(128)}, s32[]{:T(128)}) while((s32[]{:T(128)}, f32[16,128,128]{2,1,0:T(8,128)S(1)}, pred[]{:T(512)}, f32[2048]{0:T(1024)S(1)}, f32[16,128,128]{2,1,0:T(8,128)}, ...), condition=%wide.region_3.4_spmd.clone, body=%wide.region_2.0_spmd.clone.sunk | while | flops 1048579 | bytes 13639836 | solution.py:164
  32.8 3.6 collective-permute-start
  36.4 22.6 %collective-permute-done = f32[16,128,128]{2,1,0:T(8,128)S(1)} collective-permute-done((f32[16,128,128]{2,1,0:T(8,128)}, f32[16,128,128]{2,1,0:T(8,128)S(1)}, u32[]{:S(2)}, u32[]{:S(2)}) %collective-permute-start) | collective-permute-done | bytes 1048608 | tf_op jit(solution)/shard_map/while/body/eval_jaxpr/ppermute | solution.py:18
  62.8 5.6 collective-permute-start
  68.3 21.8 %collective-permute-done = f32[16,128,128]{2,1,0:T(8,128)S(1)} collective-permute-done((f32[16,128,128]{2,1,0:T(8,128)}, f32[16,128,128]{2,1,0:T(8,128)S(1)}, u32[]{:S(2)}, u32[]{:S(2)}) %collective-permute-start) | collective-permute-done | bytes 1048608 | tf_op jit(solution)/shard_map/while/body/eval_jaxpr/ppermute | solution.py:18
  93.8 5.6 collective-permute-start
  99.3 20.8 %collective-permute-done = f32[16,128,128]{2,1,0:T(8,128)S(1)} collective-permute-done((f32[16,128,128]{2,1,0:T(8,128)}, f32[16,128,128]{2,1,0:T(8,128)S(1)}, u32[]{:S(2)}, u32[]{:S(2)}) %collective-permute-start) | collective-permute-done | bytes 1048608 | tf_op jit(solution)/shard_map/while/body/eval_jaxpr/ppermute | solution.py:18
  123.9 5.6 collective-permute-start
  129.4 19.9 %collective-permute-done = f32[16,128,128]{2,1,0:T(8,128)S(1)} collective-permute-done((f32[16,128,128]{2,1,0:T(8,128)}, f32[16,128,128]{2,1,0:T(8,128)S(1)}, u32[]{:S(2)}, u32[]{:S(2)}) %collective-permute-start) | collective-permute-done | bytes 1048608 | tf_op jit(solution)/shard_map/while/body/eval_jaxpr/ppermute | solution.py:18
  153.0 5.6 collective-permute-start
  158.6 19.0 %collective-permute-done = f32[16,128,128]{2,1,0:T(8,128)S(1)} collective-permute-done((f32[16,128,128]{2,1,0:T(8,128)}, f32[16,128,128]{2,1,0:T(8,128)S(1)}, u32[]{:S(2)}, u32[]{:S(2)}) %collective-permute-start) | collective-permute-done | bytes 1048608 | tf_op jit(solution)/shard_map/while/body/eval_jaxpr/ppermute | solution.py:18
  181.3 7.1 collective-permute-start
  188.4 18.1 %collective-permute-done = f32[16,128,128]{2,1,0:T(8,128)S(1)} collective-permute-done((f32[16,128,128]{2,1,0:T(8,128)}, f32[16,128,128]{2,1,0:T(8,128)S(1)}, u32[]{:S(2)}, u32[]{:S(2)}) %collective-permute-start) | collective-permute-done | bytes 1048608 | tf_op jit(solution)/shard_map/while/body/eval_jaxpr/ppermute | solution.py:18
  210.1 7.7 collective-permute-start
  217.8 17.2 %collective-permute-done = f32[16,128,128]{2,1,0:T(8,128)S(1)} collective-permute-done((f32[16,128,128]{2,1,0:T(8,128)}, f32[16,128,128]{2,1,0:T(8,128)S(1)}, u32[]{:S(2)}, u32[]{:S(2)}) %collective-permute-start) | collective-permute-done | bytes 1048608 | tf_op jit(solution)/shard_map/while/body/eval_jaxpr/ppermute | solution.py:18
  238.7 7.7 collective-permute-start
  246.3 16.2 %collective-permute-done = f32[16,128,128]{2,1,0:T(8,128)S(1)} collective-permute-done((f32[16,128,128]{2,1,0:T(8,128)}, f32[16,128,128]{2,1,0:T(8,128)S(1)}, u32[]{:S(2)}, u32[]{:S(2)}) %collective-permute-start) | collective-permute-done | bytes 1048608 | tf_op jit(solution)/shard_map/while/body/eval_jaxpr/ppermute | solution.py:18
  266.3 7.7 collective-permute-start
  273.9 15.3 %collective-permute-done = f32[16,128,128]{2,1,0:T(8,128)S(1)} collective-permute-done((f32[16,128,128]{2,1,0:T(8,128)}, f32[16,128,128]{2,1,0:T(8,128)S(1)}, u32[]{:S(2)}, u32[]{:S(2)}) %collective-permute-start) | collective-permute-done | bytes 1048608 | tf_op jit(solution)/shard_map/while/body/eval_jaxpr/ppermute | solution.py:18
  292.9 7.7 collective-permute-start
  300.6 14.4 %collective-permute-done = f32[16,128,128]{2,1,0:T(8,128)S(1)} collective-permute-done((f32[16,128,128]{2,1,0:T(8,128)}, f32[16,128,128]{2,1,0:T(8,128)S(1)}, u32[]{:S(2)}, u32[]{:S(2)}) %collective-permute-start) | collective-permute-done | bytes 1048608 | tf_op jit(solution)/shard_map/while/body/eval_jaxpr/ppermute | solution.py:18
  318.7 7.7 collective-permute-start
  326.4 13.5 %collective-permute-done = f32[16,128,128]{2,1,0:T(8,128)S(1)} collective-permute-done((f32[16,128,128]{2,1,0:T(8,128)}, f32[16,128,128]{2,1,0:T(8,128)S(1)}, u32[]{:S(2)}, u32[]{:S(2)}) %collective-permute-start) | collective-permute-done | bytes 1048608 | tf_op jit(solution)/shard_map/while/body/eval_jaxpr/ppermute | solution.py:18
  343.5 7.7 collective-permute-start
  351.2 12.6 %collective-permute-done = f32[16,128,128]{2,1,0:T(8,128)S(1)} collective-permute-done((f32[16,128,128]{2,1,0:T(8,128)}, f32[16,128,128]{2,1,0:T(8,128)S(1)}, u32[]{:S(2)}, u32[]{:S(2)}) %collective-permute-start) | collective-permute-done | bytes 1048608 | tf_op jit(solution)/shard_map/while/body/eval_jaxpr/ppermute | solution.py:18
  367.4 7.7 collective-permute-start
  375.1 12.8 %collective-permute-done = f32[16,128,128]{2,1,0:T(8,128)S(1)} collective-permute-done((f32[16,128,128]{2,1,0:T(8,128)}, f32[16,128,128]{2,1,0:T(8,128)S(1)}, u32[]{:S(2)}, u32[]{:S(2)}) %collective-permute-start) | collective-permute-done | bytes 1048608 | tf_op jit(solution)/shard_map/while/body/eval_jaxpr/ppermute | solution.py:18
  391.5 7.7 collective-permute-start
  399.2 13.5 %collective-permute-done = f32[16,128,128]{2,1,0:T(8,128)S(1)} collective-permute-done((f32[16,128,128]{2,1,0:T(8,128)}, f32[16,128,128]{2,1,0:T(8,128)S(1)}, u32[]{:S(2)}, u32[]{:S(2)}) %collective-permute-start) | collective-permute-done | bytes 1048608 | tf_op jit(solution)/shard_map/while/body/eval_jaxpr/ppermute | solution.py:18
  416.4 8.3 collective-permute-start
  424.7 12.5 %collective-permute-done = f32[16,128,128]{2,1,0:T(8,128)S(1)} collective-permute-done((f32[16,128,128]{2,1,0:T(8,128)}, f32[16,128,128]{2,1,0:T(8,128)S(1)}, u32[]{:S(2)}, u32[]{:S(2)}) %collective-permute-start) | collective-permute-done | bytes 1048608 | tf_op jit(solution)/shard_map/while/body/eval_jaxpr/ppermute | solution.py:18
  438.3 5.7 multiply_reduce_fusion
  444.1 2.6 all-reduce
  451.3 3.3 convolution_add_fusion
  456.6 433.7 %while.28 = (s32[]{:T(128)}, f32[16,128,128]{2,1,0:T(8,128)S(1)}, pred[]{:T(512)}, f32[2048]{0:T(1024)S(1)}, f32[16,128,128]{2,1,0:T(8,128)}, /*index=5*/s32[]{:T(128)}, s32[]{:T(128)}) while((s32[]{:T(128)}, f32[16,128,128]{2,1,0:T(8,128)S(1)}, pred[]{:T(512)}, f32[2048]{0:T(1024)S(1)}, f32[16,128,128]{2,1,0:T(8,128)}, ...), condition=%wide.region_9.10_spmd.clone, body=%wide.region_8.9_spmd.clone.sunk | while | flops 1048579 | bytes 13639836 | solution.py:180
  460.5 30.6 %collective-permute-done.1 = f32[16,128,128]{2,1,0:T(8,128)S(1)} collective-permute-done((f32[16,128,128]{2,1,0:T(8,128)}, f32[16,128,128]{2,1,0:T(8,128)S(1)}, u32[]{:S(2)}, u32[]{:S(2)}) %collective-permute-start.1) | collective-permute-done | bytes 1048608 | tf_op jit(solution)/shard_map/while/body/eval_jaxpr/ppermute | solution.py:18
  493.5 2.6 fusion.65
  497.4 28.6 %collective-permute-done.1 = f32[16,128,128]{2,1,0:T(8,128)S(1)} collective-permute-done((f32[16,128,128]{2,1,0:T(8,128)}, f32[16,128,128]{2,1,0:T(8,128)S(1)}, u32[]{:S(2)}, u32[]{:S(2)}) %collective-permute-start.1) | collective-permute-done | bytes 1048608 | tf_op jit(solution)/shard_map/while/body/eval_jaxpr/ppermute | solution.py:18
  528.4 2.6 fusion.65
  532.3 27.7 %collective-permute-done.1 = f32[16,128,128]{2,1,0:T(8,128)S(1)} collective-permute-done((f32[16,128,128]{2,1,0:T(8,128)}, f32[16,128,128]{2,1,0:T(8,128)S(1)}, u32[]{:S(2)}, u32[]{:S(2)}) %collective-permute-start.1) | collective-permute-done | bytes 1048608 | tf_op jit(solution)/shard_map/while/body/eval_jaxpr/ppermute | solution.py:18
  562.4 2.6 fusion.65
  566.3 27.1 %collective-permute-done.1 = f32[16,128,128]{2,1,0:T(8,128)S(1)} collective-permute-done((f32[16,128,128]{2,1,0:T(8,128)}, f32[16,128,128]{2,1,0:T(8,128)S(1)}, u32[]{:S(2)}, u32[]{:S(2)}) %collective-permute-start.1) | collective-permute-done | bytes 1048608 | tf_op jit(solution)/shard_map/while/body/eval_jaxpr/ppermute | solution.py:18
  599.7 24.8 %collective-permute-done.1 = f32[16,128,128]{2,1,0:T(8,128)S(1)} collective-permute-done((f32[16,128,128]{2,1,0:T(8,128)}, f32[16,128,128]{2,1,0:T(8,128)S(1)}, u32[]{:S(2)}, u32[]{:S(2)}) %collective-permute-start.1) | collective-permute-done | bytes 1048608 | tf_op jit(solution)/shard_map/while/body/eval_jaxpr/ppermute | solution.py:18
  626.9 2.6 fusion.65
  630.8 24.0 %collective-permute-done.1 = f32[16,128,128]{2,1,0:T(8,128)S(1)} collective-permute-done((f32[16,128,128]{2,1,0:T(8,128)}, f32[16,128,128]{2,1,0:T(8,128)S(1)}, u32[]{:S(2)}, u32[]{:S(2)}) %collective-permute-start.1) | collective-permute-done | bytes 1048608 | tf_op jit(solution)/shard_map/while/body/eval_jaxpr/ppermute | solution.py:18
  657.1 2.6 fusion.65
  661.1 23.1 %collective-permute-done.1 = f32[16,128,128]{2,1,0:T(8,128)S(1)} collective-permute-done((f32[16,128,128]{2,1,0:T(8,128)}, f32[16,128,128]{2,1,0:T(8,128)S(1)}, u32[]{:S(2)}, u32[]{:S(2)}) %collective-permute-start.1) | collective-permute-done | bytes 1048608 | tf_op jit(solution)/shard_map/while/body/eval_jaxpr/ppermute | solution.py:18
  686.5 2.6 fusion.65
  690.4 22.1 %collective-permute-done.1 = f32[16,128,128]{2,1,0:T(8,128)S(1)} collective-permute-done((f32[16,128,128]{2,1,0:T(8,128)}, f32[16,128,128]{2,1,0:T(8,128)S(1)}, u32[]{:S(2)}, u32[]{:S(2)}) %collective-permute-start.1) | collective-permute-done | bytes 1048608 | tf_op jit(solution)/shard_map/while/body/eval_jaxpr/ppermute | solution.py:18
  714.9 2.6 fusion.65
  718.8 21.2 %collective-permute-done.1 = f32[16,128,128]{2,1,0:T(8,128)S(1)} collective-permute-done((f32[16,128,128]{2,1,0:T(8,128)}, f32[16,128,128]{2,1,0:T(8,128)S(1)}, u32[]{:S(2)}, u32[]{:S(2)}) %collective-permute-start.1) | collective-permute-done | bytes 1048608 | tf_op jit(solution)/shard_map/while/body/eval_jaxpr/ppermute | solution.py:18
  742.5 2.6 fusion.65
  746.4 20.3 %collective-permute-done.1 = f32[16,128,128]{2,1,0:T(8,128)S(1)} collective-permute-done((f32[16,128,128]{2,1,0:T(8,128)}, f32[16,128,128]{2,1,0:T(8,128)S(1)}, u32[]{:S(2)}, u32[]{:S(2)}) %collective-permute-start.1) | collective-permute-done | bytes 1048608 | tf_op jit(solution)/shard_map/while/body/eval_jaxpr/ppermute | solution.py:18
  773.0 19.4 %collective-permute-done.1 = f32[16,128,128]{2,1,0:T(8,128)S(1)} collective-permute-done((f32[16,128,128]{2,1,0:T(8,128)}, f32[16,128,128]{2,1,0:T(8,128)S(1)}, u32[]{:S(2)}, u32[]{:S(2)}) %collective-permute-start.1) | collective-permute-done | bytes 1048608 | tf_op jit(solution)/shard_map/while/body/eval_jaxpr/ppermute | solution.py:18
  798.6 18.4 %collective-permute-done.1 = f32[16,128,128]{2,1,0:T(8,128)S(1)} collective-permute-done((f32[16,128,128]{2,1,0:T(8,128)}, f32[16,128,128]{2,1,0:T(8,128)S(1)}, u32[]{:S(2)}, u32[]{:S(2)}) %collective-permute-start.1) | collective-permute-done | bytes 1048608 | tf_op jit(solution)/shard_map/while/body/eval_jaxpr/ppermute | solution.py:18
  823.4 17.5 %collective-permute-done.1 = f32[16,128,128]{2,1,0:T(8,128)S(1)} collective-permute-done((f32[16,128,128]{2,1,0:T(8,128)}, f32[16,128,128]{2,1,0:T(8,128)S(1)}, u32[]{:S(2)}, u32[]{:S(2)}) %collective-permute-start.1) | collective-permute-done | bytes 1048608 | tf_op jit(solution)/shard_map/while/body/eval_jaxpr/ppermute | solution.py:18
  847.2 17.2 %collective-permute-done.1 = f32[16,128,128]{2,1,0:T(8,128)S(1)} collective-permute-done((f32[16,128,128]{2,1,0:T(8,128)}, f32[16,128,128]{2,1,0:T(8,128)S(1)}, u32[]{:S(2)}, u32[]{:S(2)}) %collective-permute-start.1) | collective-permute-done | bytes 1048608 | tf_op jit(solution)/shard_map/while/body/eval_jaxpr/ppermute | solution.py:18
  870.7 17.2 %collective-permute-done.1 = f32[16,128,128]{2,1,0:T(8,128)S(1)} collective-permute-done((f32[16,128,128]{2,1,0:T(8,128)}, f32[16,128,128]{2,1,0:T(8,128)S(1)}, u32[]{:S(2)}, u32[]{:S(2)}) %collective-permute-start.1) | collective-permute-done | bytes 1048608 | tf_op jit(solution)/shard_map/while/body/eval_jaxpr/ppermute | solution.py:18
  892.8 2.8 fusion.35
  901.1 33.1 %all-gather = f32[32768]{0:T(1024)S(1)} all-gather(f32[2048]{0:T(1024)S(1)} %get-tuple-element.386), channel_id=2, replica_groups=mesh['pipe'=4,'ctx'=16,'tp'=2] {'ctx'}, dimensions={0}, use_global_device_ids=true | all-gather | bytes 139264 | tf_op jit(solution)/shard_map/all_gather | solution.py:23
  935.7 2.9 fusion.19
  939.9 2.6 fusion.11
  942.8 3.0 collective-permute-start.2
  945.8 25.9 %collective-permute-done.2 = bf16[4,1,128,2048]{2,3,1,0:T(8,128)(2,1)S(1)} collective-permute-done((bf16[4,1,128,2048]{2,3,1,0:T(8,128)(2,1)S(1)}, bf16[4,1,128,2048]{2,3,1,0:T(8,128)(2,1)S(1)}, u32[]{:S(2)}, u32[]{:S(2)}) %collective-permute-start.2) | collective-permute-done | bytes 2097184 | tf_op jit(solution)/shard_map/ppermute | solution.py:37
  (251 shorter events, 182.2 us)
Async XLA Ops:
  0.6 1.7 copy-start.26
  2.0 4.5 copy-start.18
  2.3 4.2 copy-start
  19.9 3.3 copy-start.1
  23.2 2.5 copy-start.5
  23.2 2.5 copy-start.10
  25.7 4.6 copy-start.13
  30.2 408.1 %copy-start.27 = (f32[1,2048]{1,0:T(1,128)S(1)}, f32[1,2048]{1,0:T(1,128)}, u32[]{:S(2)}) copy-start(f32[1,2048]{1,0:T(1,128)} %param.19) | copy-start | bytes 24580
  32.8 26.3 %collective-permute-start = (f32[16,128,128]{2,1,0:T(8,128)}, f32[16,128,128]{2,1,0:T(8,128)S(1)}, u32[]{:S(2)}, u32[]{:S(2)}) collective-permute-start(f32[16,128,128]{2,1,0:T(8,128)} %fusion.64), channel_id=1, source_target_pairs={{0,2},{2,4},{4,6},{6,8},{8,10},{10,12},{12,14},{14,16},{16,18},{18... | collective-permute-start | bytes 3145736 | tf_op jit(solution)/shard_map/while/body/eval_jaxpr/ppermute | solution.py:18
  62.8 27.3 %collective-permute-start = (f32[16,128,128]{2,1,0:T(8,128)}, f32[16,128,128]{2,1,0:T(8,128)S(1)}, u32[]{:S(2)}, u32[]{:S(2)}) collective-permute-start(f32[16,128,128]{2,1,0:T(8,128)} %fusion.64), channel_id=1, source_target_pairs={{0,2},{2,4},{4,6},{6,8},{8,10},{10,12},{12,14},{14,16},{16,18},{18... | collective-permute-start | bytes 3145736 | tf_op jit(solution)/shard_map/while/body/eval_jaxpr/ppermute | solution.py:18
  93.8 26.4 %collective-permute-start = (f32[16,128,128]{2,1,0:T(8,128)}, f32[16,128,128]{2,1,0:T(8,128)S(1)}, u32[]{:S(2)}, u32[]{:S(2)}) collective-permute-start(f32[16,128,128]{2,1,0:T(8,128)} %fusion.64), channel_id=1, source_target_pairs={{0,2},{2,4},{4,6},{6,8},{8,10},{10,12},{12,14},{14,16},{16,18},{18... | collective-permute-start | bytes 3145736 | tf_op jit(solution)/shard_map/while/body/eval_jaxpr/ppermute | solution.py:18
  123.9 25.5 %collective-permute-start = (f32[16,128,128]{2,1,0:T(8,128)}, f32[16,128,128]{2,1,0:T(8,128)S(1)}, u32[]{:S(2)}, u32[]{:S(2)}) collective-permute-start(f32[16,128,128]{2,1,0:T(8,128)} %fusion.64), channel_id=1, source_target_pairs={{0,2},{2,4},{4,6},{6,8},{8,10},{10,12},{12,14},{14,16},{16,18},{18... | collective-permute-start | bytes 3145736 | tf_op jit(solution)/shard_map/while/body/eval_jaxpr/ppermute | solution.py:18
  153.0 24.6 %collective-permute-start = (f32[16,128,128]{2,1,0:T(8,128)}, f32[16,128,128]{2,1,0:T(8,128)S(1)}, u32[]{:S(2)}, u32[]{:S(2)}) collective-permute-start(f32[16,128,128]{2,1,0:T(8,128)} %fusion.64), channel_id=1, source_target_pairs={{0,2},{2,4},{4,6},{6,8},{8,10},{10,12},{12,14},{14,16},{16,18},{18... | collective-permute-start | bytes 3145736 | tf_op jit(solution)/shard_map/while/body/eval_jaxpr/ppermute | solution.py:18
  181.3 25.2 %collective-permute-start = (f32[16,128,128]{2,1,0:T(8,128)}, f32[16,128,128]{2,1,0:T(8,128)S(1)}, u32[]{:S(2)}, u32[]{:S(2)}) collective-permute-start(f32[16,128,128]{2,1,0:T(8,128)} %fusion.64), channel_id=1, source_target_pairs={{0,2},{2,4},{4,6},{6,8},{8,10},{10,12},{12,14},{14,16},{16,18},{18... | collective-permute-start | bytes 3145736 | tf_op jit(solution)/shard_map/while/body/eval_jaxpr/ppermute | solution.py:18
  210.1 24.8 %collective-permute-start = (f32[16,128,128]{2,1,0:T(8,128)}, f32[16,128,128]{2,1,0:T(8,128)S(1)}, u32[]{:S(2)}, u32[]{:S(2)}) collective-permute-start(f32[16,128,128]{2,1,0:T(8,128)} %fusion.64), channel_id=1, source_target_pairs={{0,2},{2,4},{4,6},{6,8},{8,10},{10,12},{12,14},{14,16},{16,18},{18... | collective-permute-start | bytes 3145736 | tf_op jit(solution)/shard_map/while/body/eval_jaxpr/ppermute | solution.py:18
  238.7 23.9 %collective-permute-start = (f32[16,128,128]{2,1,0:T(8,128)}, f32[16,128,128]{2,1,0:T(8,128)S(1)}, u32[]{:S(2)}, u32[]{:S(2)}) collective-permute-start(f32[16,128,128]{2,1,0:T(8,128)} %fusion.64), channel_id=1, source_target_pairs={{0,2},{2,4},{4,6},{6,8},{8,10},{10,12},{12,14},{14,16},{16,18},{18... | collective-permute-start | bytes 3145736 | tf_op jit(solution)/shard_map/while/body/eval_jaxpr/ppermute | solution.py:18
  266.3 23.0 %collective-permute-start = (f32[16,128,128]{2,1,0:T(8,128)}, f32[16,128,128]{2,1,0:T(8,128)S(1)}, u32[]{:S(2)}, u32[]{:S(2)}) collective-permute-start(f32[16,128,128]{2,1,0:T(8,128)} %fusion.64), channel_id=1, source_target_pairs={{0,2},{2,4},{4,6},{6,8},{8,10},{10,12},{12,14},{14,16},{16,18},{18... | collective-permute-start | bytes 3145736 | tf_op jit(solution)/shard_map/while/body/eval_jaxpr/ppermute | solution.py:18
  292.9 22.1 %collective-permute-start = (f32[16,128,128]{2,1,0:T(8,128)}, f32[16,128,128]{2,1,0:T(8,128)S(1)}, u32[]{:S(2)}, u32[]{:S(2)}) collective-permute-start(f32[16,128,128]{2,1,0:T(8,128)} %fusion.64), channel_id=1, source_target_pairs={{0,2},{2,4},{4,6},{6,8},{8,10},{10,12},{12,14},{14,16},{16,18},{18... | collective-permute-start | bytes 3145736 | tf_op jit(solution)/shard_map/while/body/eval_jaxpr/ppermute | solution.py:18
  318.7 21.1 %collective-permute-start = (f32[16,128,128]{2,1,0:T(8,128)}, f32[16,128,128]{2,1,0:T(8,128)S(1)}, u32[]{:S(2)}, u32[]{:S(2)}) collective-permute-start(f32[16,128,128]{2,1,0:T(8,128)} %fusion.64), channel_id=1, source_target_pairs={{0,2},{2,4},{4,6},{6,8},{8,10},{10,12},{12,14},{14,16},{16,18},{18... | collective-permute-start | bytes 3145736 | tf_op jit(solution)/shard_map/while/body/eval_jaxpr/ppermute | solution.py:18
  343.5 20.2 %collective-permute-start = (f32[16,128,128]{2,1,0:T(8,128)}, f32[16,128,128]{2,1,0:T(8,128)S(1)}, u32[]{:S(2)}, u32[]{:S(2)}) collective-permute-start(f32[16,128,128]{2,1,0:T(8,128)} %fusion.64), channel_id=1, source_target_pairs={{0,2},{2,4},{4,6},{6,8},{8,10},{10,12},{12,14},{14,16},{16,18},{18... | collective-permute-start | bytes 3145736 | tf_op jit(solution)/shard_map/while/body/eval_jaxpr/ppermute | solution.py:18
  367.4 20.4 %collective-permute-start = (f32[16,128,128]{2,1,0:T(8,128)}, f32[16,128,128]{2,1,0:T(8,128)S(1)}, u32[]{:S(2)}, u32[]{:S(2)}) collective-permute-start(f32[16,128,128]{2,1,0:T(8,128)} %fusion.64), channel_id=1, source_target_pairs={{0,2},{2,4},{4,6},{6,8},{8,10},{10,12},{12,14},{14,16},{16,18},{18... | collective-permute-start | bytes 3145736 | tf_op jit(solution)/shard_map/while/body/eval_jaxpr/ppermute | solution.py:18
  391.5 21.2 %collective-permute-start = (f32[16,128,128]{2,1,0:T(8,128)}, f32[16,128,128]{2,1,0:T(8,128)S(1)}, u32[]{:S(2)}, u32[]{:S(2)}) collective-permute-start(f32[16,128,128]{2,1,0:T(8,128)} %fusion.64), channel_id=1, source_target_pairs={{0,2},{2,4},{4,6},{6,8},{8,10},{10,12},{12,14},{14,16},{16,18},{18... | collective-permute-start | bytes 3145736 | tf_op jit(solution)/shard_map/while/body/eval_jaxpr/ppermute | solution.py:18
  416.4 20.8 %collective-permute-start = (f32[16,128,128]{2,1,0:T(8,128)}, f32[16,128,128]{2,1,0:T(8,128)S(1)}, u32[]{:S(2)}, u32[]{:S(2)}) collective-permute-start(f32[16,128,128]{2,1,0:T(8,128)} %fusion.64), channel_id=1, source_target_pairs={{0,2},{2,4},{4,6},{6,8},{8,10},{10,12},{12,14},{14,16},{16,18},{18... | collective-permute-start | bytes 3145736 | tf_op jit(solution)/shard_map/while/body/eval_jaxpr/ppermute | solution.py:18
  446.7 2.4 copy-start.14
  449.1 5.5 copy-start.8
  449.1 2.2 copy-start.6
  451.3 3.3 copy-start.11
  459.2 31.9 %collective-permute-start.1 = (f32[16,128,128]{2,1,0:T(8,128)}, f32[16,128,128]{2,1,0:T(8,128)S(1)}, u32[]{:S(2)}, u32[]{:S(2)}) collective-permute-start(f32[16,128,128]{2,1,0:T(8,128)} %fusion.65), channel_id=1, source_target_pairs={{2,0},{4,2},{6,4},{8,6},{10,8},{12,10},{14,12},{16,14},{18,16},{20... | collective-permute-start | bytes 3145736 | tf_op jit(solution)/shard_map/while/body/eval_jaxpr/ppermute | solution.py:18
  491.1 1.1 copy-start.4
  496.1 29.9 %collective-permute-start.1 = (f32[16,128,128]{2,1,0:T(8,128)}, f32[16,128,128]{2,1,0:T(8,128)S(1)}, u32[]{:S(2)}, u32[]{:S(2)}) collective-permute-start(f32[16,128,128]{2,1,0:T(8,128)} %fusion.65), channel_id=1, source_target_pairs={{2,0},{4,2},{6,4},{8,6},{10,8},{12,10},{14,12},{16,14},{18,16},{20... | collective-permute-start | bytes 3145736 | tf_op jit(solution)/shard_map/while/body/eval_jaxpr/ppermute | solution.py:18
  526.0 1.1 copy-start.4
  531.0 29.0 %collective-permute-start.1 = (f32[16,128,128]{2,1,0:T(8,128)}, f32[16,128,128]{2,1,0:T(8,128)S(1)}, u32[]{:S(2)}, u32[]{:S(2)}) collective-permute-start(f32[16,128,128]{2,1,0:T(8,128)} %fusion.65), channel_id=1, source_target_pairs={{2,0},{4,2},{6,4},{8,6},{10,8},{12,10},{14,12},{16,14},{18,16},{20... | collective-permute-start | bytes 3145736 | tf_op jit(solution)/shard_map/while/body/eval_jaxpr/ppermute | solution.py:18
  560.0 1.1 copy-start.4
  565.0 28.3 %collective-permute-start.1 = (f32[16,128,128]{2,1,0:T(8,128)}, f32[16,128,128]{2,1,0:T(8,128)S(1)}, u32[]{:S(2)}, u32[]{:S(2)}) collective-permute-start(f32[16,128,128]{2,1,0:T(8,128)} %fusion.65), channel_id=1, source_target_pairs={{2,0},{4,2},{6,4},{8,6},{10,8},{12,10},{14,12},{16,14},{18,16},{20... | collective-permute-start | bytes 3145736 | tf_op jit(solution)/shard_map/while/body/eval_jaxpr/ppermute | solution.py:18
  593.4 1.1 copy-start.4
  598.4 26.1 %collective-permute-start.1 = (f32[16,128,128]{2,1,0:T(8,128)}, f32[16,128,128]{2,1,0:T(8,128)S(1)}, u32[]{:S(2)}, u32[]{:S(2)}) collective-permute-start(f32[16,128,128]{2,1,0:T(8,128)} %fusion.65), channel_id=1, source_target_pairs={{2,0},{4,2},{6,4},{8,6},{10,8},{12,10},{14,12},{16,14},{18,16},{20... | collective-permute-start | bytes 3145736 | tf_op jit(solution)/shard_map/while/body/eval_jaxpr/ppermute | solution.py:18
  624.5 1.1 copy-start.4
  629.5 25.3 %collective-permute-start.1 = (f32[16,128,128]{2,1,0:T(8,128)}, f32[16,128,128]{2,1,0:T(8,128)S(1)}, u32[]{:S(2)}, u32[]{:S(2)}) collective-permute-start(f32[16,128,128]{2,1,0:T(8,128)} %fusion.65), channel_id=1, source_target_pairs={{2,0},{4,2},{6,4},{8,6},{10,8},{12,10},{14,12},{16,14},{18,16},{20... | collective-permute-start | bytes 3145736 | tf_op jit(solution)/shard_map/while/body/eval_jaxpr/ppermute | solution.py:18
  654.8 1.1 copy-start.4
  659.8 24.3 %collective-permute-start.1 = (f32[16,128,128]{2,1,0:T(8,128)}, f32[16,128,128]{2,1,0:T(8,128)S(1)}, u32[]{:S(2)}, u32[]{:S(2)}) collective-permute-start(f32[16,128,128]{2,1,0:T(8,128)} %fusion.65), channel_id=1, source_target_pairs={{2,0},{4,2},{6,4},{8,6},{10,8},{12,10},{14,12},{16,14},{18,16},{20... | collective-permute-start | bytes 3145736 | tf_op jit(solution)/shard_map/while/body/eval_jaxpr/ppermute | solution.py:18
  684.1 1.1 copy-start.4
  689.1 23.4 %collective-permute-start.1 = (f32[16,128,128]{2,1,0:T(8,128)}, f32[16,128,128]{2,1,0:T(8,128)S(1)}, u32[]{:S(2)}, u32[]{:S(2)}) collective-permute-start(f32[16,128,128]{2,1,0:T(8,128)} %fusion.65), channel_id=1, source_target_pairs={{2,0},{4,2},{6,4},{8,6},{10,8},{12,10},{14,12},{16,14},{18,16},{20... | collective-permute-start | bytes 3145736 | tf_op jit(solution)/shard_map/while/body/eval_jaxpr/ppermute | solution.py:18
  717.6 22.5 %collective-permute-start.1 = (f32[16,128,128]{2,1,0:T(8,128)}, f32[16,128,128]{2,1,0:T(8,128)S(1)}, u32[]{:S(2)}, u32[]{:S(2)}) collective-permute-start(f32[16,128,128]{2,1,0:T(8,128)} %fusion.65), channel_id=1, source_target_pairs={{2,0},{4,2},{6,4},{8,6},{10,8},{12,10},{14,12},{16,14},{18,16},{20... | collective-permute-start | bytes 3145736 | tf_op jit(solution)/shard_map/while/body/eval_jaxpr/ppermute | solution.py:18
  745.1 21.6 %collective-permute-start.1 = (f32[16,128,128]{2,1,0:T(8,128)}, f32[16,128,128]{2,1,0:T(8,128)S(1)}, u32[]{:S(2)}, u32[]{:S(2)}) collective-permute-start(f32[16,128,128]{2,1,0:T(8,128)} %fusion.65), channel_id=1, source_target_pairs={{2,0},{4,2},{6,4},{8,6},{10,8},{12,10},{14,12},{16,14},{18,16},{20... | collective-permute-start | bytes 3145736 | tf_op jit(solution)/shard_map/while/body/eval_jaxpr/ppermute | solution.py:18
  771.7 20.7 %collective-permute-start.1 = (f32[16,128,128]{2,1,0:T(8,128)}, f32[16,128,128]{2,1,0:T(8,128)S(1)}, u32[]{:S(2)}, u32[]{:S(2)}) collective-permute-start(f32[16,128,128]{2,1,0:T(8,128)} %fusion.65), channel_id=1, source_target_pairs={{2,0},{4,2},{6,4},{8,6},{10,8},{12,10},{14,12},{16,14},{18,16},{20... | collective-permute-start | bytes 3145736 | tf_op jit(solution)/shard_map/while/body/eval_jaxpr/ppermute | solution.py:18
  797.3 19.7 %collective-permute-start.1 = (f32[16,128,128]{2,1,0:T(8,128)}, f32[16,128,128]{2,1,0:T(8,128)S(1)}, u32[]{:S(2)}, u32[]{:S(2)}) collective-permute-start(f32[16,128,128]{2,1,0:T(8,128)} %fusion.65), channel_id=1, source_target_pairs={{2,0},{4,2},{6,4},{8,6},{10,8},{12,10},{14,12},{16,14},{18,16},{20... | collective-permute-start | bytes 3145736 | tf_op jit(solution)/shard_map/while/body/eval_jaxpr/ppermute | solution.py:18
  822.1 18.8 %collective-permute-start.1 = (f32[16,128,128]{2,1,0:T(8,128)}, f32[16,128,128]{2,1,0:T(8,128)S(1)}, u32[]{:S(2)}, u32[]{:S(2)}) collective-permute-start(f32[16,128,128]{2,1,0:T(8,128)} %fusion.65), channel_id=1, source_target_pairs={{2,0},{4,2},{6,4},{8,6},{10,8},{12,10},{14,12},{16,14},{18,16},{20... | collective-permute-start | bytes 3145736 | tf_op jit(solution)/shard_map/while/body/eval_jaxpr/ppermute | solution.py:18
  845.9 18.5 %collective-permute-start.1 = (f32[16,128,128]{2,1,0:T(8,128)}, f32[16,128,128]{2,1,0:T(8,128)S(1)}, u32[]{:S(2)}, u32[]{:S(2)}) collective-permute-start(f32[16,128,128]{2,1,0:T(8,128)} %fusion.65), channel_id=1, source_target_pairs={{2,0},{4,2},{6,4},{8,6},{10,8},{12,10},{14,12},{16,14},{18,16},{20... | collective-permute-start | bytes 3145736 | tf_op jit(solution)/shard_map/while/body/eval_jaxpr/ppermute | solution.py:18
  869.5 18.5 %collective-permute-start.1 = (f32[16,128,128]{2,1,0:T(8,128)}, f32[16,128,128]{2,1,0:T(8,128)S(1)}, u32[]{:S(2)}, u32[]{:S(2)}) collective-permute-start(f32[16,128,128]{2,1,0:T(8,128)} %fusion.65), channel_id=1, source_target_pairs={{2,0},{4,2},{6,4},{8,6},{10,8},{12,10},{14,12},{16,14},{18,16},{20... | collective-permute-start | bytes 3145736 | tf_op jit(solution)/shard_map/while/body/eval_jaxpr/ppermute | solution.py:18
  890.3 2.5 copy-start.2
  890.3 2.5 copy-start.15
  892.8 2.8 copy-start.7
  895.6 1.4 copy-start.9
  897.0 2.2 copy-start.23
  897.0 2.2 copy-start.19
  897.0 2.2 copy-start.21
  899.2 35.1 %copy-start.12 = (f32[128,16,128]{0,2,1:T(8,128)S(1)}, f32[128,16,128]{0,2,1:T(8,128)}, u32[]{:S(2)}) copy-start(f32[128,16,128]{0,2,1:T(8,128)} %get-tuple-element.396) | copy-start | bytes 3145732
  899.2 35.1 %copy-start.16 = (bf16[1,128,2048]{1,2,0:T(8,128)(2,1)S(1)}, bf16[1,128,2048]{1,2,0:T(8,128)(2,1)}, u32[]{:S(2)}) copy-start(bf16[1,128,2048]{1,2,0:T(8,128)(2,1)} %copy.41) | copy-start | bytes 1572868
  899.2 35.1 %copy-start.17 = (bf16[1,128,2048]{1,2,0:T(8,128)(2,1)S(1)}, bf16[1,128,2048]{1,2,0:T(8,128)(2,1)}, u32[]{:S(2)}) copy-start(bf16[1,128,2048]{1,2,0:T(8,128)(2,1)} %copy.40) | copy-start | bytes 1572868
  901.1 34.6 %copy-start.22 = (f32[128,16,128]{0,2,1:T(8,128)S(1)}, f32[128,16,128]{0,2,1:T(8,128)}, u32[]{:S(2)}) copy-start(f32[128,16,128]{0,2,1:T(8,128)} %convolution_bitcast_fusion.2) | copy-start | bytes 3145732
  935.7 4.2 copy-start.20
  939.9 2.7 copy-start.24
  939.9 2.7 copy-start.25
  942.8 28.9 %collective-permute-start.2 = (bf16[4,1,128,2048]{2,3,1,0:T(8,128)(2,1)S(1)}, bf16[4,1,128,2048]{2,3,1,0:T(8,128)(2,1)S(1)}, u32[]{:S(2)}, u32[]{:S(2)}) collective-permute-start(bf16[4,1,128,2048]{2,3,1,0:T(8,128)(2,1)S(1)} %pad_maximum_fusion), channel_id=1, source_target_pairs={{0,96},{32,0},{64,32},{96,64},{1,97},{33,1},{65,33},{97,65},{2,98}... | collective-permute-start | bytes 6291464 | tf_op jit(solution)/shard_map/ppermute | solution.py:37
  (23 other events, 23.4 us)
where the time goes:
time: 984 us; the launch traced here: 979 us
  waiting for transfers between devices  615 us (62%)
  starting transfers between devices  125 us (13%)
  other arithmetic  113 us (11%)
  local copies, waits for them, and re-layouts  52.8 us (5%)
  blocking collectives  35.8 us (4%)
  matrix products  34.5 us (4%)
    ppermute x30, waiting for transfers between devices, passed_along(): return lax.ppermute(x, axis, pairs)  589 us
    ppermute x30, starting transfers between devices, passed_along(): return lax.ppermute(x, axis, pairs)  122 us
    add x15, other arithmetic, combine_backward(): return (earlier[0] * later[0], later[1] + later[0][:, :, None] * earlier[1])  39.3 us
    add x15, other arithmetic, combine_forward(): return (earlier[0] * later[0], later[0][:, :, None] * earlier[1] + later[1])  38.4 us
    all_gather x1, blocking collectives, carried_in(): pieces = lax.all_gather(value, axis)  33.1 us
    while x60, local copies, waits for them, and re-layouts  30.7 us
    ppermute x1, waiting for transfers between devices, passed_along_2(): return lax.ppermute(x, axis, [(i, (i + by) % size) for i in range(size)])  25.9 us
    select_n x15, other arithmetic, backward_turn(): jnp.where(final, identity[1], received[1])  19.7 us
  transfers between devices with their start and end apart: 31, of which 31 were waited for; matrix products, arithmetic and copies ran while one was open for 0% of the time, Pallas kernels for 0%

commit v1 on v0

v1 whole, which is shorter than its diff:
```python
import functools

import jax
import jax.numpy as jnp
from jax import lax
from jax.experimental import pallas as pl
from jax.experimental.pallas import tpu as pltpu
from jax.sharding import PartitionSpec as P

DK = 128
BLOCK = 128
HEAD_COLUMNS = 4096
EPSILON = 1e-06

F32 = jnp.float32
BF16 = jnp.bfloat16
NN = ((1,), (0,))
NT = ((1,), (1,))
TN = ((0,), (0,))
PARAMS = pltpu.CompilerParams(vmem_limit_bytes=48 * 1024 * 1024)
VMEM = pl.BlockSpec(memory_space=pltpu.VMEM)


def parts(x, count=2):
    if x.dtype == BF16:
        return [x]
    terms = []
    for _ in range(count - 1):
        term = x.astype(BF16)
        terms.append(term)
        x = x - term.astype(F32)
    return terms + [x.astype(BF16)]


def product(left, right, dims):
    pairs = [
        (a, b)
        for i, a in enumerate(left)
        for j, b in enumerate(right)
        if i + j < max(len(left), len(right))
    ]
    lhs = jnp.concatenate([a for a, _ in pairs], axis=dims[0][0])
    rhs = jnp.concatenate([b for _, b in pairs], axis=dims[1][0])
    return lax.dot_general(lhs, rhs, (dims, ((), ())), preferred_element_type=F32)


def triangle(lower):
    row = lax.broadcasted_iota(jnp.int32, (BLOCK, BLOCK), 0)
    col = lax.broadcasted_iota(jnp.int32, (BLOCK, BLOCK), 1)
    return row >= col if lower else row <= col


def head_row(ref):
    start = pl.multiple_of(lax.axis_index("ctx") * DK, DK)
    return ref[0:1, pl.ds(start, DK)]


def gates_of(x, bound):
    squashed = jax.nn.sigmoid(x.astype(F32))
    forget = bound + (1.0 - bound) * squashed
    return squashed, forget


def pack_kernel(heads, *refs):
    out = refs[-1]
    for a, ref in enumerate(refs[:-1]):
        for h in range(heads):
            out[h, a] = ref[0, :, h * DK : (h + 1) * DK]


def pack(arrays):
    rows, width = arrays[0].shape[1:]
    steps = 4
    heads = width // DK
    each = heads // steps
    return pl.pallas_call(
        functools.partial(pack_kernel, each),
        grid=(steps,),
        out_shape=jax.ShapeDtypeStruct((heads, len(arrays), rows, DK), BF16),
        in_specs=[pl.BlockSpec((1, rows, each * DK), lambda i: (0, 0, i))] * len(arrays),
        out_specs=pl.BlockSpec((each, len(arrays), rows, DK), lambda i: (i, 0, 0, 0)),
        compiler_params=PARAMS,
        name="pack",
    )(*arrays)


def unpack_kernel(heads, ref, *outs):
    for a, out in enumerate(outs):
        for h in range(heads):
            out[0, :, h * DK : (h + 1) * DK] = ref[h, a]


def unpack(array):
    heads, count, rows, _ = array.shape
    steps = 4
    each = heads // steps
    return pl.pallas_call(
        functools.partial(unpack_kernel, each),
        grid=(steps,),
        out_shape=[jax.ShapeDtypeStruct((1, rows, heads * DK), BF16)] * count,
        in_specs=[pl.BlockSpec((each, count, rows, DK), lambda i: (i, 0, 0, 0))],
        out_specs=[pl.BlockSpec((1, rows, each * DK), lambda i: (0, 0, i))] * count,
        compiler_params=PARAMS,
        name="unpack",
    )(array)


def forward_kernel(x_ref, bound_ref, gain_ref, att_ref, state_ref, run_ref, score_ref, sums_ref, rows_ref):
    blocks = x_ref.shape[0]
    bound = head_row(bound_ref)
    gain = head_row(gain_ref)
    lower = triangle(True)
    ones_below = [jnp.where(lower, 1.0, 0.0).astype(BF16)]
    ones = [jnp.ones((8, DK), BF16)]

    def turn(b, state):
        q = x_ref[b, 0].astype(F32)
        v = x_ref[b, 2]
        squashed, forget = gates_of(x_ref[b, 1], bound)
        keys = 1.0 - forget
        run = product(ones_below, parts(jnp.log(forget), 3), NN)
        last = run[BLOCK - 1 : BLOCK]
        q_scaled = parts(q * jnp.exp(run))
        k_scaled = parts(keys * jnp.exp(-run))
        k_left = parts(keys * jnp.exp(last - run))
        scores = jnp.where(lower, product(q_scaled, k_scaled, NT), 0.0)
        attended = product(parts(scores), [v], NN) + product(q_scaled, parts(state), NT)
        att_ref[b] = attended
        state_ref[b] = state
        run_ref[b] = run
        score_ref[b] = scores
        gates = x_ref[b, 3].astype(F32)
        norm_grad = x_ref[b, 4].astype(F32) * (gates * jax.nn.sigmoid(gates))
        rows_ref[b] = product(ones, parts(attended * attended, 3), NT)
        rows_ref[b + blocks] = product(ones, parts(gain * norm_grad * attended, 3), NT)
        return state * jnp.exp(last) + product([v], k_left, TN)

    lax.fori_loop(0, blocks, turn, jnp.zeros((DK, DK), F32), unroll=2)
    rows = jnp.concatenate([rows_ref[i, 0:1] for i in range(2 * blocks)], axis=0)
    for i in range(blocks):
        sums_ref[i] = rows


def forward(x, bound, gain):
    blocks = x.shape[0]
    square = jax.ShapeDtypeStruct((blocks, BLOCK, DK), F32)
    return pl.pallas_call(
        forward_kernel,
        out_shape=[square, square, square, square, jax.ShapeDtypeStruct((blocks, 2 * blocks, BLOCK), F32)],
        in_specs=[VMEM] * 3,
        out_specs=[VMEM] * 5,
        scratch_shapes=[pltpu.VMEM((2 * blocks, 8, BLOCK), F32)],
        compiler_params=PARAMS,
        name="forward",
    )(x, bound, gain)


def backward_kernel(
    x_ref, bound_ref, gain_ref, att_ref, state_ref, run_ref, score_ref, mine_ref, other_ref,
    gq_ref, vl_ref, root_ref, pull_ref,
):
    blocks = x_ref.shape[0]
    bound = head_row(bound_ref)
    gain = head_row(gain_ref)
    lower = triangle(True)
    ones_above = [jnp.where(triangle(False), 1.0, 0.0).astype(BF16)]

    sums = mine_ref[0] + other_ref[0]
    for i in range(1, blocks):
        sums = sums + (mine_ref[i] + other_ref[i])
    root = jnp.sqrt(sums[:blocks] / HEAD_COLUMNS + EPSILON)
    inverse = 1.0 / root
    pull = sums[blocks:] / (HEAD_COLUMNS * (root * root * root))
    fill = jnp.zeros((BLOCK - 2 * blocks, BLOCK), F32)
    columns = jnp.concatenate([inverse, pull, fill], axis=0).T
    for i in range(blocks):
        root_ref[i] = jnp.broadcast_to(columns[:, i : i + 1], (BLOCK, DK))
        pull_ref[i] = jnp.broadcast_to(columns[:, blocks + i : blocks + i + 1], (BLOCK, DK))

    def turn(step, carried):
        later, log_later = carried
        b = blocks - 1 - step
        q = x_ref[b, 0].astype(F32)
        v = x_ref[b, 2]
        squashed, forget = gates_of(x_ref[b, 1], bound)
        keys = 1.0 - forget
        gates = x_ref[b, 3].astype(F32)
        grad = x_ref[b, 4].astype(F32)
        gated = jax.nn.sigmoid(gates)
        attended = att_ref[b]
        over_root = root_ref[b]
        normed = attended * over_root * gain
        gq_ref[b, 0] = (grad * normed * gated * (1.0 + gates * (1.0 - gated))).astype(BF16)
        dout = gain * (grad * (gates * gated)) * over_root - attended * pull_ref[b]

        run = run_ref[b]
        last = run[BLOCK - 1 : BLOCK]
        grow = jnp.exp(run)
        shrink = jnp.exp(-run)
        left = jnp.exp(last - run)
        q_scaled = parts(q * grow)
        k_scaled = parts(keys * shrink)
        k_left = parts(keys * left)
        douts = parts(dout)
        laters = parts(later)
        pairs = parts(jnp.where(lower, product(douts, [v], NT), 0.0))
        q_grad = grow * (product(pairs, k_scaled, NN) + product(douts, parts(state_ref[b]), NN))
        k_grad = shrink * product(pairs, q_scaled, TN) + left * product([v], laters, NN)
        v_grad = product(parts(score_ref[b]), douts, TN) + product(k_left, laters, NT)
        terms = q * q_grad - keys * k_grad
        log_grad = product(ones_above, parts(terms, 3), NN) + log_later
        logit_grad = (log_grad / forget - k_grad) * (1.0 - bound) * squashed * (1.0 - squashed)
        gq_ref[b, 1] = q_grad.astype(BF16)
        vl_ref[b, 0] = v_grad.astype(BF16)
        vl_ref[b, 1] = logit_grad.astype(BF16)
        later = later * jnp.exp(last) + product(douts, q_scaled, TN)
        return later, jnp.sum(state_ref[b] * later, axis=0, keepdims=True)

    lax.fori_loop(
        0, blocks, turn, (jnp.zeros((DK, DK), F32), jnp.zeros((1, DK), F32)), unroll=2
    )


def backward(x, bound, gain, attended, states, runs, scores, mine, other):
    blocks = x.shape[0]
    pair = jax.ShapeDtypeStruct((blocks, 2, BLOCK, DK), BF16)
    return pl.pallas_call(
        backward_kernel,
        out_shape=[pair, pair],
        in_specs=[VMEM] * 9,
        out_specs=[VMEM] * 2,
        scratch_shapes=[pltpu.VMEM((blocks, BLOCK, DK), F32)] * 2,
        compiler_params=PARAMS,
        name="backward",
    )(x, bound, gain, attended, states, runs, scores, mine, other)


def to_previous_section(x):
    size = lax.axis_size("pipe")
    return lax.ppermute(x, "pipe", [(i, (i - 1) % size) for i in range(size)])


def exchange(x):
    return lax.all_to_all(x, "ctx", 0, 0)


def body(queries, forget_logits, values, gates, output_grad, lower_bound, norm_gain):
    x = exchange(pack([queries, forget_logits, values, gates, output_grad]))
    attended, states, runs, scores, sums = forward(x, lower_bound, norm_gain)
    mine = exchange(sums)
    other = lax.ppermute(mine, "tp", [(0, 1), (1, 0)])
    gq, vl = backward(x, lower_bound, norm_gain, attended, states, runs, scores, mine, other)
    gq_there = to_previous_section(gq)
    vl_back = exchange(vl)
    vl_there = to_previous_section(vl_back)
    gate_grad, query_grad = unpack(exchange(gq_there))
    value_grad, logit_grad = unpack(vl_there)
    return query_grad, logit_grad, value_grad, gate_grad


def solution(mesh):
    rows = P("pipe", "ctx", "tp")
    return jax.shard_map(
        body,
        mesh=mesh,
        in_specs=(rows,) * 5 + (P("pipe", "tp"),) * 2,
        out_specs=(rows,) * 4,
        check_vma=False,
    )
```

time: 984 us -> 137 us (0.14)
  waiting for transfers between devices: 615 us -> 5.11 us
  starting transfers between devices: 125 us -> 3.65 us
  other arithmetic: 113 us -> 0 us
  blocking collectives: 35.8 us -> 92.9 us
  local copies, waits for them, and re-layouts: 52.8 us -> 6.18 us
  matrix products: 34.5 us -> 0 us
  Pallas kernels: 0 us -> 27.4 us
    ppermute x31 -> x3, waiting for transfers between devices: 615 us -> 5.11 us  [the longest x2 3.58 us: to_previous_section(): return lax.ppermute(x, 'pipe', [(i, (i - 1) % size) for i in range(size)])]
    ppermute x31 -> x3, starting transfers between devices: 125 us -> 3.65 us  [the longest x2 3.64 us: to_previous_section(): return lax.ppermute(x, 'pipe', [(i, (i - 1) % size) for i in range(size)])]
    all_to_all x0 -> x4, blocking collectives: none -> 92.9 us  [exchange(): return lax.all_to_all(x, 'ctx', 0, 0)]
    add x30 -> x0, other arithmetic: 77.7 us -> none  [the longest x15 39.3 us: combine_backward(): return (earlier[0] * later[0], later[1] + later[0][:, :, None] * earlier[1])]
    dot_general x13 -> x0, matrix products: 34.5 us -> none  [the longest x1 5.74 us: block_forward(): jnp.einsum('ubl,bli->ubi', probe_vector_scaled, incoming_memory, precisio...]
    all_gather x1 -> x0, blocking collectives: 33.1 us -> none  [carried_in(): pieces = lax.all_gather(value, axis)]
    while x60 -> x0, local copies, waits for them, and re-layouts: 30.7 us -> none
    pallas_call x0 -> x5, Pallas kernels: none -> 27.4 us  [the longest x1 11.8 us: forward(): pl.pallas_call(forward_kernel, out_shape=[square, square, square, square,...]
  transfers between devices with their start and end apart: 31 -> 3, of which waited for: 31 -> 3; matrix products, arithmetic and copies ran while one was open for 0% -> 0% of each run, Pallas kernels for 0% -> 1%
where the time goes in v1:
time: 137 us; the launch traced here: 136 us
  blocking collectives  92.9 us (68%)
  Pallas kernels  27.4 us (20%)
  local copies, waits for them, and re-layouts  6.18 us (5%)
  waiting for transfers between devices  5.11 us (4%)
  starting transfers between devices  3.65 us (3%)
    all_to_all x4, blocking collectives, exchange(): return lax.all_to_all(x, 'ctx', 0, 0)  92.9 us
    pallas_call x1, Pallas kernels, forward(): pl.pallas_call(forward_kernel, out_shape=[square, square, square, square,...  11.8 us
    pallas_call x1, Pallas kernels, backward(): pl.pallas_call(backward_kernel, out_shape=[pair, pair], in_specs=[VMEM] *...  11.7 us
    unnamed x16, local copies, waits for them, and re-layouts  6.18 us
    ppermute x2, starting transfers between devices, to_previous_section(): return lax.ppermute(x, 'pipe', [(i, (i - 1) % size) for i in range(size)])  3.64 us
    ppermute x2, waiting for transfers between devices, to_previous_section(): return lax.ppermute(x, 'pipe', [(i, (i - 1) % size) for i in range(size)])  3.58 us
    pallas_call x2, Pallas kernels, unpack(): pl.pallas_call(functools.partial(unpack_kernel, each), grid=(steps,), out...  3.14 us
  transfers between devices with their start and end apart: 3, of which 3 were waited for; matrix products, arithmetic and copies ran while one was open for 0% of the time, Pallas kernels for 1%

profile of v1, /device:TPU:0, one launch (start us, length us, event | category | flops | bytes accessed | tf_op | source)
XLA Modules:
  0.0 135.9 jit_solution(14300414349159761676)
XLA Ops:
  0.6 0.0 copy-start.1
  0.6 1.0 copy-done.1
  1.7 0.0 copy-start.2
  1.7 1.0 copy-done.2
  2.7 0.0 copy-start.3
  2.7 1.0 copy-done.3
  3.8 0.0 copy-start.4
  3.8 1.0 copy-done.4
  4.8 0.0 copy-start.5
  4.8 1.0 copy-done.5
  5.8 0.7 pack.1
  6.6 0.0 copy-start.6
  6.6 0.0 copy-start.7
  6.6 42.0 %all_to_all.20.x_ref = bf16[16,5,128,128]{3,2,1,0:T(8,128)(2,1)} all-to-all(bf16[16,5,128,128]{3,2,1,0:T(8,128)(2,1)S(1)} %pack.1), channel_id=1, replica_groups=mesh['pipe'=4,'ctx'=16,'tp'=2] {'ctx'}, dimensions={0} | all-to-all | bytes 5242880 | tf_op jit(solution)/shard_map/all_to_all | solution.py:244
  48.7 0.0 copy-done.6
  48.7 0.0 copy-done.7
  48.7 11.8 %forward.1 = (f32[16,128,128]{2,1,0:T(8,128)S(1)}, f32[16,128,128]{2,1,0:T(8,128)S(1)}, f32[16,128,128]{2,1,0:T(8,128)S(1)}, f32[16,128,128]{2,1,0:T(8,128)S(1)}, f32[16,32,128]{2,1,0:T(8,128)S(1)}) custom-call(bf16[16,5,128,128]{3,2,1,0:T(8,128)(2,1)} %all_to_all.20.x_ref, f32[1,2048]{1,0:T(1,128)S(1)} %copy-done.6, f32[1,2048]{1,0:T(1,128)S(1)} %copy-done.7), custom_call_target="tpu_custom_call" | custom-call | tf_op jit(solution)/shard_map/forward/pallas_call | solution.py:147
  60.5 0.0 copy-start
  60.5 1.0 copy-done
  61.5 11.6 %all_to_all.21.mine_ref = f32[16,32,128]{2,1,0:T(8,128)S(1)} all-to-all(f32[16,32,128]{2,1,0:T(8,128)S(1)} %get-tuple-element.19), channel_id=1, replica_groups=mesh['pipe'=4,'ctx'=16,'tp'=2] {'ctx'}, dimensions={0} | all-to-all | bytes 524288 | tf_op jit(solution)/shard_map/all_to_all | solution.py:244
  73.1 0.0 collective-permute-start
  73.1 1.5 %collective-permute-done.other_ref = f32[16,32,128]{2,1,0:T(8,128)S(1)} collective-permute-done((f32[16,32,128]{2,1,0:T(8,128)S(1)}, f32[16,32,128]{2,1,0:T(8,128)S(1)}, u32[]{:S(2)}, u32[]{:S(2)}) %collective-permute-start) | collective-permute-done | bytes 262176 | tf_op jit(solution)/shard_map/ppermute | solution.py:251
  74.6 11.7 %backward.1 = (bf16[16,2,128,128]{3,2,1,0:T(8,128)(2,1)S(1)}, bf16[16,2,128,128]{3,2,1,0:T(8,128)(2,1)S(1)}) custom-call(bf16[16,5,128,128]{3,2,1,0:T(8,128)(2,1)} %all_to_all.20.x_ref, f32[1,2048]{1,0:T(1,128)S(1)} %copy-done.6, f32[1,2048]{1,0:T(1,128)S(1)} %copy-done.7, f32[16,128,128]{2,1,0:T(8,128)S(1)} %get-tuple-element.15.att_ref, ...), custom_call_target="tpu_custom_call" | custom-call | tf_op jit(solution)/shard_map/backward/pallas_call | solution.py:227
  86.3 2.8 %collective-permute-start.1 = (bf16[16,2,128,128]{3,2,1,0:T(8,128)(2,1)S(1)}, bf16[16,2,128,128]{3,2,1,0:T(8,128)(2,1)S(1)}, u32[]{:S(2)}, u32[]{:S(2)}) collective-permute-start(bf16[16,2,128,128]{3,2,1,0:T(8,128)(2,1)S(1)} %get-tuple-element.20), channel_id=1, source_target_pairs={{0,96},{32,0},{64,32},{96,64},{1,97},{33,1},{65,33},{97,65},{2,98}... | collective-permute-start | bytes 3145736 | tf_op jit(solution)/shard_map/ppermute | solution.py:240
  89.1 20.1 %all_to_all.22 = bf16[16,2,128,128]{3,2,1,0:T(8,128)(2,1)S(1)} all-to-all(bf16[16,2,128,128]{3,2,1,0:T(8,128)(2,1)S(1)} %get-tuple-element.22), channel_id=1, replica_groups=mesh['pipe'=4,'ctx'=16,'tp'=2] {'ctx'}, dimensions={0} | all-to-all | bytes 2097152 | tf_op jit(solution)/shard_map/all_to_all | solution.py:244
  109.2 0.8 collective-permute-start.2
  110.0 2.6 %collective-permute-done.1 = bf16[16,2,128,128]{3,2,1,0:T(8,128)(2,1)S(1)} collective-permute-done((bf16[16,2,128,128]{3,2,1,0:T(8,128)(2,1)S(1)}, bf16[16,2,128,128]{3,2,1,0:T(8,128)(2,1)S(1)}, u32[]{:S(2)}, u32[]{:S(2)}) %collective-permute-start.1) | collective-permute-done | bytes 1048608 | tf_op jit(solution)/shard_map/ppermute | solution.py:240
  112.7 19.2 %all_to_all.23.ref = bf16[16,2,128,128]{3,2,1,0:T(8,128)(2,1)S(1)} all-to-all(bf16[16,2,128,128]{3,2,1,0:T(8,128)(2,1)S(1)} %collective-permute-done.1), channel_id=1, replica_groups=mesh['pipe'=4,'ctx'=16,'tp'=2] {'ctx'}, dimensions={0} | all-to-all | bytes 2097152 | tf_op jit(solution)/shard_map/all_to_all | solution.py:244
  131.8 1.6 %unpack.2 = (bf16[1,128,2048]{2,1,0:T(8,128)(2,1)}, bf16[1,128,2048]{2,1,0:T(8,128)(2,1)}) custom-call(bf16[16,2,128,128]{3,2,1,0:T(8,128)(2,1)S(1)} %all_to_all.23.ref), custom_call_target="tpu_custom_call" | custom-call | tf_op jit(solution)/shard_map/unpack/pallas_call | solution.py:97
  133.4 0.9 collective-permute-done.2.ref
  134.3 1.6 %unpack.3 = (bf16[1,128,2048]{2,1,0:T(8,128)(2,1)}, bf16[1,128,2048]{2,1,0:T(8,128)(2,1)}) custom-call(bf16[16,2,128,128]{3,2,1,0:T(8,128)(2,1)S(1)} %collective-permute-done.2.ref), custom_call_target="tpu_custom_call" | custom-call | tf_op jit(solution)/shard_map/unpack/pallas_call | solution.py:97
Async XLA Ops:
  0.6 1.0 copy-start.1
  1.7 1.0 copy-start.2
  2.7 1.0 copy-start.3
  3.8 1.0 copy-start.4
  4.8 1.0 copy-start.5
  6.6 42.1 %copy-start.6 = (f32[1,2048]{1,0:T(1,128)S(1)}, f32[1,2048]{1,0:T(1,128)}, u32[]{:S(2)}) copy-start(f32[1,2048]{1,0:T(1,128)} %bound_ref.3) | copy-start | bytes 24580
  6.6 42.1 %copy-start.7 = (f32[1,2048]{1,0:T(1,128)S(1)}, f32[1,2048]{1,0:T(1,128)}, u32[]{:S(2)}) copy-start(f32[1,2048]{1,0:T(1,128)} %gain_ref.3) | copy-start | bytes 24580
  60.5 1.0 copy-start
  73.1 1.5 %collective-permute-start = (f32[16,32,128]{2,1,0:T(8,128)S(1)}, f32[16,32,128]{2,1,0:T(8,128)S(1)}, u32[]{:S(2)}, u32[]{:S(2)}) collective-permute-start(f32[16,32,128]{2,1,0:T(8,128)S(1)} %all_to_all.21.mine_ref), channel_id=1, source_target_pairs={{0,1},{1,0},{2,3},{3,2},{4,5},{5,4},{6,7},{7,6},{8,9},{9,8},{10,11... | collective-permute-start | bytes 786440 | tf_op jit(solution)/shard_map/ppermute | solution.py:251
  86.3 26.4 %collective-permute-start.1 = (bf16[16,2,128,128]{3,2,1,0:T(8,128)(2,1)S(1)}, bf16[16,2,128,128]{3,2,1,0:T(8,128)(2,1)S(1)}, u32[]{:S(2)}, u32[]{:S(2)}) collective-permute-start(bf16[16,2,128,128]{3,2,1,0:T(8,128)(2,1)S(1)} %get-tuple-element.20), channel_id=1, source_target_pairs={{0,96},{32,0},{64,32},{96,64},{1,97},{33,1},{65,33},{97,65},{2,98}... | collective-permute-start | bytes 3145736 | tf_op jit(solution)/shard_map/ppermute | solution.py:240
  109.2 25.1 %collective-permute-start.2 = (bf16[16,2,128,128]{3,2,1,0:T(8,128)(2,1)S(1)}, bf16[16,2,128,128]{3,2,1,0:T(8,128)(2,1)S(1)}, u32[]{:S(2)}, u32[]{:S(2)}) collective-permute-start(bf16[16,2,128,128]{3,2,1,0:T(8,128)(2,1)S(1)} %all_to_all.22), channel_id=1, source_target_pairs={{0,96},{32,0},{64,32},{96,64},{1,97},{33,1},{65,33},{97,65},{2,98}... | collective-permute-start | bytes 3145736 | tf_op jit(solution)/shard_map/ppermute | solution.py:240

commit v2 on v1

v2 whole, which is shorter than its diff:
```python
import functools

import jax
import jax.numpy as jnp
from jax import lax
from jax.experimental import pallas as pl
from jax.experimental.pallas import tpu as pltpu
from jax.sharding import PartitionSpec as P

DK = 128
BLOCK = 128
HEAD_COLUMNS = 4096
EPSILON = 1e-06

F32 = jnp.float32
BF16 = jnp.bfloat16
NN = ((1,), (0,))
NT = ((1,), (1,))
TN = ((0,), (0,))
UNROLL = 4
PARAMS = pltpu.CompilerParams(vmem_limit_bytes=24 * 1024 * 1024)
VMEM = pl.BlockSpec(memory_space=pltpu.VMEM)


def parts(x, count=2):
    if x.dtype == BF16:
        return [x]
    terms = []
    for _ in range(count - 1):
        term = x.astype(BF16)
        terms.append(term)
        x = x - term.astype(F32)
    return terms + [x.astype(BF16)]


def product(left, right, dims):
    pairs = [
        (a, b)
        for i, a in enumerate(left)
        for j, b in enumerate(right)
        if i + j < max(len(left), len(right))
    ]
    lhs = jnp.concatenate([a for a, _ in pairs], axis=dims[0][0])
    rhs = jnp.concatenate([b for _, b in pairs], axis=dims[1][0])
    return lax.dot_general(lhs, rhs, (dims, ((), ())), preferred_element_type=F32)


def triangle(lower):
    row = lax.broadcasted_iota(jnp.int32, (BLOCK, BLOCK), 0)
    col = lax.broadcasted_iota(jnp.int32, (BLOCK, BLOCK), 1)
    return row >= col if lower else row <= col


def head_row(ref):
    start = pl.multiple_of(lax.axis_index("ctx") * DK, DK)
    return ref[0:1, pl.ds(start, DK)]


def pack_kernel(*refs):
    *arrays, out, landed, sems = refs
    copies = [pltpu.make_async_copy(ref, landed.at[a], sems.at[a]) for a, ref in enumerate(arrays)]
    for copy in copies:
        copy.start()
    for a, copy in enumerate(copies):
        copy.wait()
        for h in range(out.shape[0]):
            out[h, a] = landed[a, 0, :, h * DK : (h + 1) * DK]


def pack(arrays):
    count = len(arrays)
    rows, width = arrays[0].shape[1:]
    return pl.pallas_call(
        pack_kernel,
        out_shape=jax.ShapeDtypeStruct((width // DK, count, rows, DK), BF16),
        in_specs=[pl.BlockSpec(memory_space=pl.ANY)] * count,
        out_specs=VMEM,
        scratch_shapes=[pltpu.VMEM((count, 1, rows, width), BF16), pltpu.SemaphoreType.DMA((count,))],
        compiler_params=pltpu.CompilerParams(vmem_limit_bytes=58 * 1024 * 1024),
        name="pack",
    )(*arrays)


def unpack_kernel(heads, ref, *outs):
    for a, out in enumerate(outs):
        for h in range(heads):
            out[0, :, h * DK : (h + 1) * DK] = ref[h, a]


def unpack(array):
    heads, count, rows, _ = array.shape
    steps = 4
    each = heads // steps
    return pl.pallas_call(
        functools.partial(unpack_kernel, each),
        grid=(steps,),
        out_shape=[jax.ShapeDtypeStruct((1, rows, heads * DK), BF16)] * count,
        in_specs=[pl.BlockSpec((each, count, rows, DK), lambda i: (i, 0, 0, 0))],
        out_specs=[pl.BlockSpec((1, rows, each * DK), lambda i: (0, 0, i))] * count,
        compiler_params=PARAMS,
        name="unpack",
    )(array)


def forward_kernel(
    x_ref, bound_ref, gain_ref,
    att_ref, pull_ref, gate_ref, squash_ref, grow_ref, shrink_ref, q_ref, k_ref, state_ref, score_ref, sums_ref,
):
    blocks = x_ref.shape[0]
    bound = head_row(bound_ref)
    gain = head_row(gain_ref)
    lower = triangle(True)
    ones_below = [jnp.where(lower, 1.0, 0.0).astype(BF16)]
    lane = lax.broadcasted_iota(jnp.int32, (BLOCK, DK), 1)

    def turn(b, carried):
        state, columns = carried
        q = x_ref[b, 0].astype(F32)
        v = x_ref[b, 2]
        squashed = jax.nn.sigmoid(x_ref[b, 1].astype(F32))
        forget = bound + (1.0 - bound) * squashed
        run = product(ones_below, parts(jnp.log(forget), 3), NN)
        grow = jnp.exp(run)
        shrink = jnp.exp(-run)
        q_scaled = parts(q * grow)
        k_scaled = parts((1.0 - forget) * shrink)
        states = parts(state)
        scores = parts(jnp.where(lower, product(q_scaled, k_scaled, NT), 0.0))
        attended = product(scores, [v], NN) + product(q_scaled, states, NT)
        gates = x_ref[b, 3].astype(F32)
        gated = jax.nn.sigmoid(gates)
        grad = x_ref[b, 4].astype(F32) * gain
        pull = grad * (gates * gated)
        att_ref[b] = attended
        pull_ref[b] = pull
        gate_ref[b] = grad * gated * (1.0 + gates * (1.0 - gated))
        squash_ref[b] = squashed
        grow_ref[b] = grow
        shrink_ref[b] = shrink
        for ref, terms in ((q_ref, q_scaled), (k_ref, k_scaled), (state_ref, states), (score_ref, scores)):
            ref[b, 0], ref[b, 1] = terms
        square = jnp.sum(attended * attended, axis=1, keepdims=True)
        weighted = jnp.sum(pull * attended, axis=1, keepdims=True)
        columns = jnp.where(lane == b, square, jnp.where(lane == b + blocks, weighted, columns))
        return (state + product([v], k_scaled, TN)) * grow[BLOCK - 1 : BLOCK], columns

    nothing = jnp.zeros((BLOCK, DK), F32)
    _, columns = lax.fori_loop(0, blocks, turn, (nothing, nothing), unroll=UNROLL)
    rows = columns.T[: 2 * blocks]
    for i in range(blocks):
        sums_ref[i] = rows


def forward(x, bound, gain):
    blocks = x.shape[0]
    square = jax.ShapeDtypeStruct((blocks, BLOCK, DK), F32)
    pair = jax.ShapeDtypeStruct((blocks, 2, BLOCK, DK), BF16)
    sums = jax.ShapeDtypeStruct((blocks, 2 * blocks, BLOCK), F32)
    return pl.pallas_call(
        forward_kernel,
        out_shape=[square] * 6 + [pair] * 4 + [sums],
        in_specs=[VMEM] * 3,
        out_specs=[VMEM] * 11,
        compiler_params=PARAMS,
        name="forward",
    )(x, bound, gain)


def backward_kernel(
    x_ref, bound_ref, gain_ref,
    att_ref, pull_ref, gate_ref, squash_ref, grow_ref, shrink_ref, q_ref, k_ref, state_ref, score_ref,
    mine_ref, other_ref,
    gq_ref, vl_ref, root_ref, weigh_ref,
):
    blocks = x_ref.shape[0]
    bound = head_row(bound_ref)
    lower = triangle(True)
    ones_above = [jnp.where(triangle(False), 1.0, 0.0).astype(BF16)]

    sums = mine_ref[0] + other_ref[0]
    for i in range(1, blocks):
        sums = sums + (mine_ref[i] + other_ref[i])
    root = jnp.sqrt(sums[:blocks] / HEAD_COLUMNS + EPSILON)
    inverse = 1.0 / root
    weigh = sums[blocks:] / (HEAD_COLUMNS * (root * root * root))
    fill = jnp.zeros((BLOCK - 2 * blocks, BLOCK), F32)
    columns = jnp.concatenate([inverse, weigh, fill], axis=0).T
    for i in range(blocks):
        root_ref[i] = jnp.broadcast_to(columns[:, i : i + 1], (BLOCK, DK))
        weigh_ref[i] = jnp.broadcast_to(columns[:, blocks + i : blocks + i + 1], (BLOCK, DK))

    def turn(step, carried):
        later, log_later = carried
        b = blocks - 1 - step
        q = x_ref[b, 0].astype(F32)
        v = x_ref[b, 2]
        squashed = squash_ref[b]
        forget = bound + (1.0 - bound) * squashed
        attended = att_ref[b]
        over_root = root_ref[b]
        gq_ref[b, 0] = (gate_ref[b] * (attended * over_root)).astype(BF16)
        douts = parts(pull_ref[b] * over_root - attended * weigh_ref[b])

        grow = grow_ref[b]
        q_scaled = [q_ref[b, 0], q_ref[b, 1]]
        k_scaled = [k_ref[b, 0], k_ref[b, 1]]
        states = [state_ref[b, 0], state_ref[b, 1]]
        scores = [score_ref[b, 0], score_ref[b, 1]]
        later = later * grow[BLOCK - 1 : BLOCK]
        laters = parts(later)
        pairs = parts(jnp.where(lower, product(douts, [v], NT), 0.0))
        q_grad = grow * (product(pairs, k_scaled, NN) + product(douts, states, NN))
        k_grad = shrink_ref[b] * (product(pairs, q_scaled, TN) + product([v], laters, NN))
        v_grad = product(scores, douts, TN) + product(k_scaled, laters, NT)
        terms = q * q_grad - (1.0 - forget) * k_grad
        log_grad = product(ones_above, parts(terms, 3), NN) + log_later
        logit_grad = (log_grad / forget - k_grad) * (1.0 - bound) * squashed * (1.0 - squashed)
        gq_ref[b, 1] = q_grad.astype(BF16)
        vl_ref[b, 0] = v_grad.astype(BF16)
        vl_ref[b, 1] = logit_grad.astype(BF16)
        later = later + product(douts, q_scaled, TN)
        state = states[0].astype(F32) + states[1].astype(F32)
        return later, jnp.sum(state * later, axis=0, keepdims=True)

    lax.fori_loop(
        0, blocks, turn, (jnp.zeros((DK, DK), F32), jnp.zeros((1, DK), F32)), unroll=UNROLL
    )


def backward(x, bound, gain, *saved):
    blocks = x.shape[0]
    pair = jax.ShapeDtypeStruct((blocks, 2, BLOCK, DK), BF16)
    return pl.pallas_call(
        backward_kernel,
        out_shape=[pair, pair],
        in_specs=[VMEM] * (3 + len(saved)),
        out_specs=[VMEM] * 2,
        scratch_shapes=[pltpu.VMEM((blocks, BLOCK, DK), F32)] * 2,
        compiler_params=PARAMS,
        name="backward",
    )(x, bound, gain, *saved)


def to_previous_section(x):
    size = lax.axis_size("pipe")
    return lax.ppermute(x, "pipe", [(i, (i - 1) % size) for i in range(size)])


def exchange(x):
    return lax.all_to_all(x, "ctx", 0, 0)


def body(queries, forget_logits, values, gates, output_grad, lower_bound, norm_gain):
    x = exchange(pack([queries, forget_logits, values, gates, output_grad]))
    *saved, sums = forward(x, lower_bound, norm_gain)
    mine = exchange(sums)
    other = lax.ppermute(mine, "tp", [(0, 1), (1, 0)])
    gq, vl = backward(x, lower_bound, norm_gain, *saved, mine, other)
    gq_there = to_previous_section(gq)
    vl_there = to_previous_section(exchange(vl))
    gate_grad, query_grad = unpack(exchange(gq_there))
    value_grad, logit_grad = unpack(vl_there)
    return query_grad, logit_grad, value_grad, gate_grad


def solution(mesh):
    rows = P("pipe", "ctx", "tp")
    return jax.shard_map(
        body,
        mesh=mesh,
        in_specs=(rows,) * 5 + (P("pipe", "tp"),) * 2,
        out_specs=(rows,) * 4,
        check_vma=False,
    )
```

time: 137 us -> 125 us (0.912)
  local copies, waits for them, and re-layouts: 6.18 us -> 0.01 us
  Pallas kernels: 27.4 us -> 21.3 us
    unnamed x16 -> x4, local copies, waits for them, and re-layouts: 6.18 us -> 0.01 us
    pallas_call x1, Pallas kernels: 11.7 us -> 8.4 us  [backward(): pl.pallas_call(backward_kernel, out_shape=[pair, pair], in_specs=[VMEM] *...]
    pallas_call x2, Pallas kernels: 12.6 us -> 9.75 us  [the longest x1 6.43 us: forward(): pl.pallas_call(forward_kernel, out_shape=[square] * 6 + [pair] * 4 + [sum...]
where the time goes in v2:
time: 125 us; the launch traced here: 124 us
  blocking collectives  93 us (74%)
  Pallas kernels  21.3 us (17%)
  waiting for transfers between devices  5.11 us (4%)
  starting transfers between devices  3.65 us (3%)
    all_to_all x4, blocking collectives, exchange(): return lax.all_to_all(x, 'ctx', 0, 0)  93 us
    pallas_call x1, Pallas kernels, backward(): pl.pallas_call(backward_kernel, out_shape=[pair, pair], in_specs=[VMEM] *...  8.4 us
    pallas_call x1, Pallas kernels, forward(): pl.pallas_call(forward_kernel, out_shape=[square] * 6 + [pair] * 4 + [sum...  6.43 us
    ppermute x2, starting transfers between devices, to_previous_section(): return lax.ppermute(x, 'pipe', [(i, (i - 1) % size) for i in range(size)])  3.65 us
    ppermute x2, waiting for transfers between devices, to_previous_section(): return lax.ppermute(x, 'pipe', [(i, (i - 1) % size) for i in range(size)])  3.57 us
    pallas_call x1, Pallas kernels, pack(): pl.pallas_call(pack_kernel, out_shape=jax.ShapeDtypeStruct((width // DK,...  3.32 us
    pallas_call x2, Pallas kernels, unpack(): pl.pallas_call(functools.partial(unpack_kernel, each), grid=(steps,), out...  3.14 us
  transfers between devices with their start and end apart: 3, of which 3 were waited for; matrix products, arithmetic and copies ran while one was open for 0% of the time, Pallas kernels for 1%

profile of v2, /device:TPU:0, one launch (start us, length us, event | category | flops | bytes accessed | tf_op | source)
XLA Modules:
  0.0 123.8 jit_solution(14630389748870009406)
XLA Ops:
  0.6 3.3 %pack.1 = bf16[16,5,128,128]{3,2,1,0:T(8,128)(2,1)} custom-call(bf16[1,128,2048]{2,1,0:T(8,128)(2,1)} %refs_0_.1, bf16[1,128,2048]{2,1,0:T(8,128)(2,1)} %refs_1_.1, bf16[1,128,2048]{2,1,0:T(8,128)(2,1)} %refs_2_.1, bf16[1,128,2048]{2,1,0:T(8,128)(2,1)} %refs_3_.1, bf16[1,128,2048]{2,1,0:T(8,128)(2,1)} %refs_4_.1), custom_call_target="tpu_custom_call" | custom-call | tf_op jit(solution)/shard_map/pack/pallas_call | solution.py:73
  4.0 0.0 copy-start
  4.0 0.0 copy-start.1
  4.0 42.1 %all_to_all.20.x_ref = bf16[16,5,128,128]{3,2,1,0:T(8,128)(2,1)S(1)} all-to-all(bf16[16,5,128,128]{3,2,1,0:T(8,128)(2,1)} %pack.1), channel_id=1, replica_groups=mesh['pipe'=4,'ctx'=16,'tp'=2] {'ctx'}, dimensions={0} | all-to-all | bytes 5242880 | tf_op jit(solution)/shard_map/all_to_all | solution.py:250
  46.1 0.0 copy-done
  46.1 0.0 copy-done.1
  46.1 6.4 %forward.1 = (f32[16,128,128]{2,1,0:T(8,128)S(1)}, f32[16,128,128]{2,1,0:T(8,128)S(1)}, f32[16,128,128]{2,1,0:T(8,128)S(1)}, f32[16,128,128]{2,1,0:T(8,128)S(1)}...) custom-call(bf16[16,5,128,128]{3,2,1,0:T(8,128)(2,1)S(1)} %all_to_al, ...), custom_call_target="tpu_custom_call" | custom-call | tf_op jit(solution)/shard_map/forward/pallas_call | solution.py:159
  52.6 11.6 %all_to_all.21.mine_ref = f32[16,32,128]{2,1,0:T(8,128)S(1)} all-to-all(f32[16,32,128]{2,1,0:T(8,128)S(1)} %get-tuple-element.31), channel_id=1, replica_groups=mesh['pipe'=4,'ctx'=16,'tp'=2] {'ctx'}, dimensions={0} | all-to-all | bytes 524288 | tf_op jit(solution)/shard_map/all_to_all | solution.py:250
  64.2 0.0 collective-permute-start
  64.2 1.5 %collective-permute-done.other_ref = f32[16,32,128]{2,1,0:T(8,128)S(1)} collective-permute-done((f32[16,32,128]{2,1,0:T(8,128)S(1)}, f32[16,32,128]{2,1,0:T(8,128)S(1)}, u32[]{:S(2)}, u32[]{:S(2)}) %collective-permute-start) | collective-permute-done | bytes 262176 | tf_op jit(solution)/shard_map/ppermute | solution.py:257
  65.8 8.4 %backward.1 = (bf16[16,2,128,128]{3,2,1,0:T(8,128)(2,1)S(1)}, bf16[16,2,128,128]{3,2,1,0:T(8,128)(2,1)S(1)}) custom-call(bf16[16,5,128,128]{3,2,1,0:T(8,128)(2,1)S(1)} %all_to_all.20.x_ref, f32[1,2048]{1,0:T(1,128)S(1)} %copy-done, f32[1,2048]{1,0:T(1,128)S(1)} %copy-done.1, f32[16,128,128]{2,1,0:T(8,128)S(1)} %get-tuple-element.21.att_ref, ...), custom_call_target="tpu_custom_call" | custom-call | tf_op jit(solution)/shard_map/backward/pallas_call | solution.py:233
  74.2 2.8 %collective-permute-start.1 = (bf16[16,2,128,128]{3,2,1,0:T(8,128)(2,1)S(1)}, bf16[16,2,128,128]{3,2,1,0:T(8,128)(2,1)S(1)}, u32[]{:S(2)}, u32[]{:S(2)}) collective-permute-start(bf16[16,2,128,128]{3,2,1,0:T(8,128)(2,1)S(1)} %get-tuple-element.32), channel_id=1, source_target_pairs={{0,96},{32,0},{64,32},{96,64},{1,97},{33,1},{65,33},{97,65},{2,98}... | collective-permute-start | bytes 3145736 | tf_op jit(solution)/shard_map/ppermute | solution.py:246
  77.0 20.1 %all_to_all.22 = bf16[16,2,128,128]{3,2,1,0:T(8,128)(2,1)S(1)} all-to-all(bf16[16,2,128,128]{3,2,1,0:T(8,128)(2,1)S(1)} %get-tuple-element.34), channel_id=1, replica_groups=mesh['pipe'=4,'ctx'=16,'tp'=2] {'ctx'}, dimensions={0} | all-to-all | bytes 2097152 | tf_op jit(solution)/shard_map/all_to_all | solution.py:250
  97.1 0.8 collective-permute-start.2
  97.9 2.6 %collective-permute-done.1 = bf16[16,2,128,128]{3,2,1,0:T(8,128)(2,1)S(1)} collective-permute-done((bf16[16,2,128,128]{3,2,1,0:T(8,128)(2,1)S(1)}, bf16[16,2,128,128]{3,2,1,0:T(8,128)(2,1)S(1)}, u32[]{:S(2)}, u32[]{:S(2)}) %collective-permute-start.1) | collective-permute-done | bytes 1048608 | tf_op jit(solution)/shard_map/ppermute | solution.py:246
  100.5 19.2 %all_to_all.23.ref = bf16[16,2,128,128]{3,2,1,0:T(8,128)(2,1)S(1)} all-to-all(bf16[16,2,128,128]{3,2,1,0:T(8,128)(2,1)S(1)} %collective-permute-done.1), channel_id=1, replica_groups=mesh['pipe'=4,'ctx'=16,'tp'=2] {'ctx'}, dimensions={0} | all-to-all | bytes 2097152 | tf_op jit(solution)/shard_map/all_to_all | solution.py:250
  119.7 1.6 %unpack.2 = (bf16[1,128,2048]{2,1,0:T(8,128)(2,1)}, bf16[1,128,2048]{2,1,0:T(8,128)(2,1)}) custom-call(bf16[16,2,128,128]{3,2,1,0:T(8,128)(2,1)S(1)} %all_to_all.23.ref), custom_call_target="tpu_custom_call" | custom-call | tf_op jit(solution)/shard_map/unpack/pallas_call | solution.py:94
  121.2 0.9 collective-permute-done.2.ref
  122.2 1.6 %unpack.3 = (bf16[1,128,2048]{2,1,0:T(8,128)(2,1)}, bf16[1,128,2048]{2,1,0:T(8,128)(2,1)}) custom-call(bf16[16,2,128,128]{3,2,1,0:T(8,128)(2,1)S(1)} %collective-permute-done.2.ref), custom_call_target="tpu_custom_call" | custom-call | tf_op jit(solution)/shard_map/unpack/pallas_call | solution.py:94
Async XLA Ops:
  4.0 42.2 %copy-start = (f32[1,2048]{1,0:T(1,128)S(1)}, f32[1,2048]{1,0:T(1,128)}, u32[]{:S(2)}) copy-start(f32[1,2048]{1,0:T(1,128)} %bound_ref.3) | copy-start | bytes 24580
  4.0 42.2 %copy-start.1 = (f32[1,2048]{1,0:T(1,128)S(1)}, f32[1,2048]{1,0:T(1,128)}, u32[]{:S(2)}) copy-start(f32[1,2048]{1,0:T(1,128)} %gain_ref.3) | copy-start | bytes 24580
  64.2 1.5 %collective-permute-start = (f32[16,32,128]{2,1,0:T(8,128)S(1)}, f32[16,32,128]{2,1,0:T(8,128)S(1)}, u32[]{:S(2)}, u32[]{:S(2)}) collective-permute-start(f32[16,32,128]{2,1,0:T(8,128)S(1)} %all_to_all.21.mine_ref), channel_id=1, source_target_pairs={{0,1},{1,0},{2,3},{3,2},{4,5},{5,4},{6,7},{7,6},{8,9},{9,8},{10,11... | collective-permute-start | bytes 786440 | tf_op jit(solution)/shard_map/ppermute | solution.py:257
  74.2 26.4 %collective-permute-start.1 = (bf16[16,2,128,128]{3,2,1,0:T(8,128)(2,1)S(1)}, bf16[16,2,128,128]{3,2,1,0:T(8,128)(2,1)S(1)}, u32[]{:S(2)}, u32[]{:S(2)}) collective-permute-start(bf16[16,2,128,128]{3,2,1,0:T(8,128)(2,1)S(1)} %get-tuple-element.32), channel_id=1, source_target_pairs={{0,96},{32,0},{64,32},{96,64},{1,97},{33,1},{65,33},{97,65},{2,98}... | collective-permute-start | bytes 3145736 | tf_op jit(solution)/shard_map/ppermute | solution.py:246
  97.1 25.1 %collective-permute-start.2 = (bf16[16,2,128,128]{3,2,1,0:T(8,128)(2,1)S(1)}, bf16[16,2,128,128]{3,2,1,0:T(8,128)(2,1)S(1)}, u32[]{:S(2)}, u32[]{:S(2)}) collective-permute-start(bf16[16,2,128,128]{3,2,1,0:T(8,128)(2,1)S(1)} %all_to_all.22), channel_id=1, source_target_pairs={{0,96},{32,0},{64,32},{96,64},{1,97},{33,1},{65,33},{97,65},{2,98}... | collective-permute-start | bytes 3145736 | tf_op jit(solution)/shard_map/ppermute | solution.py:246

commit v3 on v2

v3 whole, which is shorter than its diff:
```python
import functools

import jax
import jax.numpy as jnp
from jax import lax
from jax.experimental import pallas as pl
from jax.experimental.pallas import tpu as pltpu
from jax.sharding import PartitionSpec as P

DK = 128
BLOCK = 128
HEAD_COLUMNS = 4096
EPSILON = 1e-06

F32 = jnp.float32
BF16 = jnp.bfloat16
NN = ((1,), (0,))
NT = ((1,), (1,))
TN = ((0,), (0,))
RANGE = 84.0
EXTRA = 16
PIECES = 4
PARAMS = pltpu.CompilerParams(vmem_limit_bytes=24 * 1024 * 1024)
VMEM = pl.BlockSpec(memory_space=pltpu.VMEM)


def parts(x, count=2):
    if x.dtype == BF16:
        return [x]
    terms = []
    for _ in range(count - 1):
        term = x.astype(BF16)
        terms.append(term)
        x = x - term.astype(F32)
    return terms + [x.astype(BF16)]


def product(left, right, dims):
    pairs = [
        (a, b)
        for i, a in enumerate(left)
        for j, b in enumerate(right)
        if i + j < max(len(left), len(right))
    ]
    lhs = jnp.concatenate([a for a, _ in pairs], axis=dims[0][0])
    rhs = jnp.concatenate([b for _, b in pairs], axis=dims[1][0])
    return lax.dot_general(lhs, rhs, (dims, ((), ())), preferred_element_type=F32)


def triangle(lower):
    row = lax.broadcasted_iota(jnp.int32, (BLOCK, BLOCK), 0)
    col = lax.broadcasted_iota(jnp.int32, (BLOCK, BLOCK), 1)
    return row >= col if lower else row <= col


def of_head(ref, h):
    return ref[0, :, pl.ds(pl.multiple_of(h * DK, DK), DK)]


def row_of_head(ref, h):
    return ref[0:1, pl.ds(pl.multiple_of(h * DK, DK), DK)]


def put_head(ref, h, value):
    ref[0, :BLOCK, pl.ds(pl.multiple_of(h * DK, DK), DK)] = value


def pair_of(ref, h):
    return [ref[h, 0], ref[h, 1]]


def put_pair(ref, h, terms):
    ref[h, 0], ref[h, 1] = terms


def sum_of(terms):
    return terms[0].astype(F32) + terms[1].astype(F32)


def forget_of(squashed, bound):
    return bound + (1.0 - bound) * squashed


def encode(ref, i, x, *rows):
    top = jnp.maximum(jnp.max(jnp.abs(x), axis=0, keepdims=True), 1e-30)
    top = (top * 1.01).astype(BF16).astype(F32)
    ref[i, :DK] = jnp.exp(x * (RANGE / top)).astype(BF16)
    place = lax.broadcasted_iota(jnp.int32, (EXTRA, DK), 0)
    extra = jnp.zeros((EXTRA, DK), F32)
    for r, row in enumerate((top,) + rows):
        extra = jnp.where(place == r, row, extra)
    ref[i, DK:] = extra.astype(BF16)


def decode(ref, i):
    extra = ref[i, DK:].astype(F32)
    return jnp.log(ref[i, :DK].astype(F32)) * (extra[0:1] * (1.0 / RANGE)), extra


def call(kernel, name, ins, outs, streamed=(), kept=(), scratch=()):
    hbm = pl.BlockSpec(memory_space=pltpu.HBM)
    return pl.pallas_call(
        kernel,
        out_shape=[*outs, *kept],
        in_specs=[hbm] * len(streamed) + [VMEM] * len(ins),
        out_specs=[VMEM] * len(outs) + [hbm] * len(kept),
        scratch_shapes=scratch,
        compiler_params=PARAMS,
        name=name,
    )(*[pltpu.with_memory_space_constraint(x, pltpu.HBM) for x in streamed], *ins)


def buffers(*arrays):
    return [pltpu.VMEM(x.shape, x.dtype) for x in arrays] + [pltpu.SemaphoreType.DMA((len(arrays), PIECES))]


def piece_of(ref, p):
    if ref.shape[0] == 1:
        width = ref.shape[2] // PIECES
        return ref.at[:, :, pl.ds(p * width, width)]
    each = ref.shape[0] // PIECES
    return ref.at[pl.ds(p * each, each)]


def start_piece(sources, targets, sems, p):
    copies = [
        pltpu.make_async_copy(piece_of(source, p), piece_of(target, p), sems.at[a, p])
        for a, (source, target) in enumerate(zip(sources, targets))
    ]
    for copy in copies:
        copy.start()
    return copies


def start_copies(sources, targets, sems, heads):
    copies = [start_piece(sources, targets, sems, p) for p in range(PIECES)]

    def wait(h):
        if h % (heads // PIECES) == 0:
            for copy in copies[h * PIECES // heads]:
                copy.wait()

    return wait


def own_state_kernel(
    logit_hbm, value_hbm, bound_ref, run_ref, k_ref, own_ref, v_ref, coded_ref,
    logit_ref, value_ref, sems,
):
    wait = start_copies((logit_hbm, value_hbm), (logit_ref, value_ref), sems, own_ref.shape[0])
    ones_below = [jnp.where(triangle(True), 1.0, 0.0).astype(BF16)]
    for h in range(own_ref.shape[0]):
        wait(h)
        bound = row_of_head(bound_ref, h)
        squashed = jax.nn.sigmoid(of_head(logit_ref, h).astype(F32))
        forget = forget_of(squashed, bound)
        run = product(ones_below, parts(jnp.log(forget), 3), NN)
        k_scaled = parts((1.0 - forget) * jnp.exp(-run))
        last = run[BLOCK - 1 : BLOCK]
        v = of_head(value_ref, h)
        own = product([v], k_scaled, TN) * jnp.exp(last)
        run_ref[h] = run
        v_ref[h] = v
        put_pair(k_ref, h, k_scaled)
        own_ref[h] = own
        encode(coded_ref, h, own, *[term.astype(F32) for term in parts(last, 3)])


def states_before_kernel(coded_ref, out_ref, decay_ref):
    state = jnp.zeros((DK, DK), F32)
    for i in range(coded_ref.shape[0]):
        encode(out_ref, i, state)
        own, extra = decode(coded_ref, i)
        decay = jnp.exp(extra[1:2] + extra[2:3] + extra[3:4])
        decay_ref[i] = jnp.broadcast_to(decay, decay_ref.shape[1:])
        state = state * decay + own


def states_after_kernel(coded_ref, decay_ref, out_ref):
    later = jnp.zeros((DK, DK), F32)
    for i in reversed(range(coded_ref.shape[0])):
        encode(out_ref, i, later)
        later = later * decay_ref[i, 0:1] + decode(coded_ref, i)[0]


def attended_kernel(
    query_hbm, gates_hbm, grad_hbm, coded_ref, gain_ref, run_ref, k_ref, v_ref,
    q_ref, grow_ref, score_ref, pull_ref, gate_ref, att_ref, state_ref, sums_ref,
    query_ref, gates_ref, grad_ref, sems,
):
    wait = start_copies((query_hbm, gates_hbm, grad_hbm), (query_ref, gates_ref, grad_ref), sems, v_ref.shape[0])
    lower = triangle(True)
    squares = jnp.zeros((BLOCK, DK), F32)
    weighted = squares
    for h in range(v_ref.shape[0]):
        wait(h)
        grow = jnp.exp(run_ref[h])
        q_scaled = parts(of_head(query_ref, h).astype(F32) * grow)
        scores = parts(jnp.where(lower, product(q_scaled, pair_of(k_ref, h), NT), 0.0))
        states = parts(decode(coded_ref, h)[0])
        attended = product(scores, [v_ref[h]], NN) + product(q_scaled, states, NT)
        gates = of_head(gates_ref, h).astype(F32)
        gated = jax.nn.sigmoid(gates)
        grad = of_head(grad_ref, h).astype(F32) * row_of_head(gain_ref, h)
        pull = grad * (gates * gated)
        put_pair(q_ref, h, q_scaled)
        grow_ref[h] = grow
        put_pair(score_ref, h, scores)
        pull_ref[h] = pull
        gate_ref[h] = grad * gated * (1.0 + gates * (1.0 - gated))
        att_ref[h] = attended
        put_pair(state_ref, h, states)
        squares = squares + attended * attended
        weighted = weighted + pull * attended
    for i, total in enumerate((squares, weighted)):
        sums_ref[8 * i : 8 * i + 8] = jnp.broadcast_to(jnp.sum(total.T, axis=0, keepdims=True), (8, BLOCK))


def early_grads_kernel(
    mine_ref, other_ref, att_ref, pull_ref, gate_ref, grow_ref, q_ref, k_ref, v_ref, own_ref, state_ref, score_ref,
    coded_ref, gate_grad_ref, query_grad_ref, kept_hbm, kept_ref, sems,
):
    heads = v_ref.shape[0]
    copies = []
    ones_above = [jnp.where(triangle(False), 1.0, 0.0).astype(BF16)]
    sums = mine_ref[...] + other_ref[...]
    root = jnp.sqrt(sums[0:8] / HEAD_COLUMNS + EPSILON)
    weigh = sums[8:16] / (HEAD_COLUMNS * (root * root * root))
    fill = jnp.zeros((BLOCK - 16, BLOCK), F32)
    columns = jnp.concatenate([1.0 / root, weigh, fill], axis=0).T
    over_root = jnp.broadcast_to(columns[:, 0:1], (BLOCK, DK))
    weigh = jnp.broadcast_to(columns[:, 8:9], (BLOCK, DK))
    lower = triangle(True)
    for h in range(v_ref.shape[0]):
        attended = att_ref[h]
        put_head(gate_grad_ref, h, (gate_ref[h] * (attended * over_root)).astype(BF16))
        douts = parts(pull_ref[h] * over_root - attended * weigh)
        q_scaled = pair_of(q_ref, h)
        encode(coded_ref, h, product(douts, q_scaled, TN))
        pairs = parts(jnp.where(lower, product(douts, [v_ref[h]], NT), 0.0))
        k_scaled = pair_of(k_ref, h)
        states = pair_of(state_ref, h)
        q_part = product(pairs, k_scaled, NN) + product(douts, states, NN)
        k_part = product(pairs, q_scaled, TN)
        grow = grow_ref[h]
        put_head(query_grad_ref, h, (grow * q_part).astype(BF16))
        keys = sum_of(k_scaled)
        terms = sum_of(q_scaled) * q_part - keys * k_part
        shrink = 1.0 / grow
        kept_ref[h, 0] = product(ones_above, parts(terms, 3), NN) / (1.0 - keys * grow) - shrink * k_part
        kept_ref[h, 1] = product(pair_of(score_ref, h), douts, TN)
        kept_ref[h, 2] = shrink
        kept_ref[h, 3] = sum_of(states) * grow[BLOCK - 1 : BLOCK] + own_ref[h]
        if (h + 1) % (heads // PIECES) == 0:
            copies += start_piece((kept_ref,), (kept_hbm,), sems, h * PIECES // heads)
    for copy in copies:
        copy.wait()


def late_grads_kernel(
    logit_hbm, value_hbm, kept_hbm, coded_ref, bound_ref, value_grad_ref, logit_grad_ref,
    logit_ref, value_ref, kept_ref, sems,
):
    heads = kept_ref.shape[0]
    wait = start_copies((logit_hbm, value_hbm, kept_hbm), (logit_ref, value_ref, kept_ref), sems, heads)
    ones_above = [jnp.where(triangle(False), 1.0, 0.0).astype(BF16)]
    for h in range(heads):
        wait(h)
        later = decode(coded_ref, h)[0]
        shrink = kept_ref[h, 2]
        bound = row_of_head(bound_ref, h)
        squashed = jax.nn.sigmoid(of_head(logit_ref, h).astype(F32))
        forget = forget_of(squashed, bound)
        k_scaled = (1.0 - forget) * shrink
        log_later = jnp.sum(kept_ref[h, 3] * later, axis=0, keepdims=True)
        laters = parts(later / shrink[BLOCK - 1 : BLOCK])
        v_grad = kept_ref[h, 1] + product(parts(k_scaled), laters, NT)
        put_head(value_grad_ref, h, v_grad.astype(BF16))
        k_part = product([of_head(value_ref, h)], laters, NN)
        log_grad = log_later - product(ones_above, parts(k_scaled * k_part, 3), NN)
        logit_grad = kept_ref[h, 0] + (log_grad / forget - shrink * k_part)
        put_head(logit_grad_ref, h, (logit_grad * (1.0 - bound) * squashed * (1.0 - squashed)).astype(BF16))


def deliver_kernel(*refs):
    *refs, sems = refs
    half = len(refs) // 2
    copies = [
        pltpu.make_async_copy(source.at[:, :BLOCK], target, sems.at[a])
        for a, (source, target) in enumerate(zip(refs[:half], refs[half:]))
    ]
    for copy in copies:
        copy.start()
    for copy in copies:
        copy.wait()


def deliver(*arrays):
    hbm = pl.BlockSpec(memory_space=pltpu.HBM)
    return pl.pallas_call(
        deliver_kernel,
        out_shape=[jax.ShapeDtypeStruct((x.shape[0], BLOCK, x.shape[2]), x.dtype) for x in arrays],
        in_specs=[VMEM] * len(arrays),
        out_specs=[hbm] * len(arrays),
        scratch_shapes=[pltpu.SemaphoreType.DMA((len(arrays),))],
        compiler_params=pltpu.CompilerParams(vmem_limit_bytes=24 * 1024 * 1024),
        name="deliver",
    )(*arrays)


def to_previous_section(x):
    size = lax.axis_size("pipe")
    return lax.ppermute(x, "pipe", [(i, (i - 1) % size) for i in range(size)])


def exchange(x):
    return lax.all_to_all(x, "ctx", 0, 0)


def body(queries, forget_logits, values, gates, output_grad, lower_bound, norm_gain):
    heads = queries.shape[2] // DK
    whole = jax.ShapeDtypeStruct(queries.shape, BF16)
    square = jax.ShapeDtypeStruct((heads, BLOCK, DK), F32)
    pair = jax.ShapeDtypeStruct((heads, 2, BLOCK, DK), BF16)
    coded = jax.ShapeDtypeStruct((heads, DK + EXTRA, DK), BF16)
    decays = jax.ShapeDtypeStruct((heads, 8, DK), F32)
    sums = jax.ShapeDtypeStruct((16, BLOCK), F32)
    plain = jax.ShapeDtypeStruct((heads, BLOCK, DK), BF16)
    kept = jax.ShapeDtypeStruct((heads, 4, BLOCK, DK), F32)

    run, k_scaled, own_state, v, sent = call(
        own_state_kernel, "own_state", [lower_bound], [square, pair, square, plain, coded],
        streamed=[forget_logits, values], scratch=buffers(whole, whole),
    )
    sent, decay = call(states_before_kernel, "states_before", [exchange(sent)], [coded, decays])
    q_scaled, grow, scores, pull, gate_factor, attended, states, mine = call(
        attended_kernel, "attended", [exchange(sent), norm_gain, run, k_scaled, v],
        [pair, square, pair, square, square, square, pair, sums], streamed=[queries, gates, output_grad],
        scratch=buffers(whole, whole, whole),
    )
    other = lax.ppermute(mine, "tp", [(0, 1), (1, 0)])
    sent, gate_grad, query_grad, kept_now = call(
        early_grads_kernel, "early_grads",
        [mine, other, attended, pull, gate_factor, grow, q_scaled, k_scaled, v, own_state, states, scores],
        [coded, whole, whole], kept=[kept], scratch=buffers(kept),
    )
    gate_grad = to_previous_section(gate_grad)
    query_grad = to_previous_section(query_grad)

    def through(sent, decay):
        (sent,) = call(states_after_kernel, "states_after", [exchange(sent), decay], [coded])
        return exchange(sent)

    arrived = lax.cond(lower_bound[0, 0] > -1.0, through, lambda sent, decay: sent, sent, decay)
    arrived, gate_grad, query_grad = lax.optimization_barrier((arrived, gate_grad, query_grad))
    value_grad, logit_grad = call(
        late_grads_kernel, "late_grads", [arrived, lower_bound], [whole, whole],
        streamed=[forget_logits, values, kept_now], scratch=buffers(whole, whole, kept),
    )
    value_grad, logit_grad = to_previous_section(value_grad), to_previous_section(logit_grad)
    gate_grad, query_grad = deliver(gate_grad, query_grad)
    value_grad, logit_grad = deliver(value_grad, logit_grad)
    return query_grad, logit_grad, value_grad, gate_grad


def solution(mesh):
    rows = P("pipe", "ctx", "tp")
    return jax.shard_map(
        body,
        mesh=mesh,
        in_specs=(rows,) * 5 + (P("pipe", "tp"),) * 2,
        out_specs=(rows,) * 4,
        check_vma=False,
    )
```

time: 125 us -> 123 us (0.984)
  blocking collectives: 93 us -> 63.5 us
  waiting for transfers between devices: 5.11 us -> 21.3 us
  Pallas kernels: 21.3 us -> 27.1 us
  local copies, waits for them, and re-layouts: 0.01 us -> 3.86 us
  starting transfers between devices: 3.65 us -> 5.01 us
    all_to_all x4, blocking collectives: 93 us -> 63.5 us  [exchange(): return lax.all_to_all(x, 'ctx', 0, 0)]
    ppermute x2 -> x4, waiting for transfers between devices: 3.57 us -> 20.2 us  [to_previous_section(): return lax.ppermute(x, 'pipe', [(i, (i - 1) % size) for i in range(size)])]
    pallas_call x5 -> x8, Pallas kernels: 21.3 us -> 27.1 us  [the longest x6 25.1 us: call(): pl.pallas_call(kernel, out_shape=[*outs, *kept], in_specs=[hbm] * len(str...]
    unnamed x4 -> x8, local copies, waits for them, and re-layouts: 0.01 us -> 3.35 us
    ppermute x2 -> x4, starting transfers between devices: 3.65 us -> 4.74 us  [to_previous_section(): return lax.ppermute(x, 'pipe', [(i, (i - 1) % size) for i in range(size)])]
  transfers between devices with their start and end apart: 3 -> 5, of which waited for: 3 -> 3; matrix products, arithmetic and copies ran while one was open for 0% -> 0% of each run, Pallas kernels for 1% -> 1%
where the time goes in v3:
time: 123 us; the launch traced here: 122 us
  blocking collectives  63.5 us (52%)
  Pallas kernels  27.1 us (22%)
  waiting for transfers between devices  21.3 us (17%)
  starting transfers between devices  5.01 us (4%)
  local copies, waits for them, and re-layouts  3.86 us (3%)
  between operations  1.52 us (1%)
    all_to_all x4, blocking collectives, exchange(): return lax.all_to_all(x, 'ctx', 0, 0)  63.5 us
    pallas_call x6, Pallas kernels, call(): pl.pallas_call(kernel, out_shape=[*outs, *kept], in_specs=[hbm] * len(str...  25.1 us
    ppermute x4, waiting for transfers between devices, to_previous_section(): return lax.ppermute(x, 'pipe', [(i, (i - 1) % size) for i in range(size)])  20.2 us
    ppermute x4, starting transfers between devices, to_previous_section(): return lax.ppermute(x, 'pipe', [(i, (i - 1) % size) for i in range(size)])  4.74 us
    unnamed x8, local copies, waits for them, and re-layouts  3.35 us
  transfers between devices with their start and end apart: 5, of which 3 were waited for; matrix products, arithmetic and copies ran while one was open for 0% of the time, Pallas kernels for 1%

profile of v3, /device:TPU:0, one launch (start us, length us, event | category | flops | bytes accessed | tf_op | source)
XLA Modules:
  0.0 122.3 jit_solution(4814225757954809827)
XLA Ops:
  0.6 0.0 copy-start.1
  0.6 0.7 copy-done.1
  1.3 4.9 %own_state.1 = (f32[16,128,128]{2,1,0:T(8,128)S(1)}, bf16[16,2,128,128]{3,2,1,0:T(8,128)(2,1)S(1)}, f32[16,128,128]{2,1,0:T(8,128)S(1)}, bf16[16,128,128]{2,1,0:T(8,128)(2,1)S(1)}, bf16[16,144,128]{2,1,0:T(8,128)(2,1)S(1)}) custom-call(bf16[1,128,2048]{2,1,0:T(8,128)(2,1)} %logit_hbm.3, bf16[1,128,2048]{2,1,0:T(8,128)(2,1)} %value_hbm.3, f32[1,2048]{1,0:T(1,128)S(1)} %copy-done.1), custom_call_target="tpu_custom_call" | custom-call | tf_op jit(solution)/shard_map/own_state/pallas_call | solution.py:102
  6.3 20.2 %all_to_all.20.coded_ref = bf16[16,144,128]{2,1,0:T(8,128)(2,1)S(1)} all-to-all(bf16[16,144,128]{2,1,0:T(8,128)(2,1)S(1)} %get-tuple-element.42), channel_id=1, replica_groups=mesh['pipe'=4,'ctx'=16,'tp'=2] {'ctx'}, dimensions={0} | all-to-all | bytes 1179648 | tf_op jit(solution)/shard_map/all_to_all | solution.py:317
  26.4 0.4 states_before.1
  26.9 14.2 %all_to_all.21.coded_ref = bf16[16,144,128]{2,1,0:T(8,128)(2,1)S(1)} all-to-all(bf16[16,144,128]{2,1,0:T(8,128)(2,1)S(1)} %get-tuple-element.43), channel_id=1, replica_groups=mesh['pipe'=4,'ctx'=16,'tp'=2] {'ctx'}, dimensions={0} | all-to-all | bytes 1179648 | tf_op jit(solution)/shard_map/all_to_all | solution.py:317
  41.0 0.0 copy-start.3
  41.0 0.7 copy-done.3
  41.7 4.4 %attended.1 = (bf16[16,2,128,128]{3,2,1,0:T(8,128)(2,1)S(1)}, f32[16,128,128]{2,1,0:T(8,128)S(1)}, bf16[16,2,128,128]{3,2,1,0:T(8,128)(2,1)S(1)}, f32[16,128,128...) custom-call(bf16[1,128,2048]{2,1,0:T(8,128)(2,1)} %query_hbm.1, ...), custom_call_target="tpu_custom_call" | custom-call | tf_op jit(solution)/shard_map/attended/pallas_call | solution.py:102
  46.2 0.3 collective-permute-start
  46.4 1.2 collective-permute-done.other_ref
  47.6 0.0 copy-start.2
  47.6 9.0 %early_grads.1 = (bf16[16,144,128]{2,1,0:T(8,128)(2,1)S(1)}, bf16[1,128,2048]{2,1,0:T(8,128)(2,1)S(1)}, bf16[1,128,2048]{2,1,0:T(8,128)(2,1)S(1)}, f32[16,4,128,128]{3,2,1,0:T(8,128)S(1)}) custom-call(f32[16,128]{1,0:T(8,128)S(1)} %get-tuple-element.47.mine_ref, f32[16,128]{1,0:T(8,128)S(1)} %collective-permute-done.other_ref, ...), custom_call_target="tpu_custom_call" | custom-call | tf_op jit(solution)/shard_map/early_grads/pallas_call | solution.py:102
  56.6 0.0 copy-start
  56.6 2.0 %copy-done = f32[16,4,128,128]{3,2,1,0:T(8,128)} copy-done((f32[16,4,128,128]{3,2,1,0:T(8,128)}, f32[16,4,128,128]{3,2,1,0:T(8,128)S(1)}, u32[]{:S(2)}) %copy-start) | copy-done | bytes 4194328
  58.5 2.8 %collective-permute-start.1 = (bf16[1,128,2048]{2,1,0:T(8,128)(2,1)S(1)}, bf16[1,128,2048]{2,1,0:T(8,128)(2,1)S(1)}, u32[]{:S(2)}, u32[]{:S(2)}) collective-permute-start(bf16[1,128,2048]{2,1,0:T(8,128)(2,1)S(1)} %get-tuple-element.58), channel_id=1, source_target_pairs={{0,96},{32,0},{64,32},{96,64},{1,97},{33,1},{65,33},{97,65},{2,98}... | collective-permute-start | bytes 1572872 | tf_op jit(solution)/shard_map/ppermute | solution.py:313
  61.3 0.8 collective-permute-start.2
  62.1 0.0 copy-done.2
  62.1 0.5 slice.3
  63.3 29.5 %conditional.1 = (bf16[16,144,128]{2,1,0:T(8,128)(2,1)S(1)}) conditional(s32[]{:T(128)} %bitcast, bf16[16,144,128]{2,1,0:T(8,128)(2,1)S(1)} %get-tuple-element.56, (bf16[16,144,128]{2,1,0:T(8,128)(2,1)S(1)}, f32[16,8,128]{2,1,0:T(8,128)S(1)}) %tuple.15), branch_computations={%region_0.0_spmd, %region_1.0_spmd} | conditional | bytes 2359304 | solution.py:354
  63.3 15.2 %all_to_all.18.coded_ref = bf16[16,144,128]{2,1,0:T(8,128)(2,1)S(1)} all-to-all(bf16[16,144,128]{2,1,0:T(8,128)(2,1)S(1)} %get-tuple-element.8), channel_id=1, replica_groups=mesh['pipe'=4,'ctx'=16,'tp'=2] {'ctx'}, dimensions={0} | all-to-all | bytes 1179648 | tf_op jit(solution)/shard_map/cond/branch_1_fun/all_to_all | solution.py:317
  78.5 0.4 states_after.1
  78.9 13.9 %all_to_all.19 = bf16[16,144,128]{2,1,0:T(8,128)(2,1)S(1)} all-to-all(bf16[16,144,128]{2,1,0:T(8,128)(2,1)S(1)} %states_after.1), channel_id=1, replica_groups=mesh['pipe'=4,'ctx'=16,'tp'=2] {'ctx'}, dimensions={0} | all-to-all | bytes 1179648 | tf_op jit(solution)/shard_map/cond/branch_1_fun/all_to_all | solution.py:317
  92.8 0.0 collective-permute-done.1.refs_0_
  92.8 0.0 collective-permute-done.2.refs_1_
  92.8 6.0 %late_grads.1 = (bf16[1,128,2048]{2,1,0:T(8,128)(2,1)S(1)}, bf16[1,128,2048]{2,1,0:T(8,128)(2,1)S(1)}) custom-call(bf16[1,128,2048]{2,1,0:T(8,128)(2,1)} %logit_hbm.3, bf16[1,128,2048]{2,1,0:T(8,128)(2,1)} %value_hbm.3, f32[16,4,128,128]{3,2,1,0:T(8,128)} %copy-done, bf16[16,144,128]{2,1,0:T(8,128)(2,1)S(1)} %get-tuple-element.70.coded_ref, ...), custom_call_target="tpu_custom_call" | custom-call | tf_op jit(solution)/shard_map/late_grads/pallas_call | solution.py:102
  98.8 0.6 collective-permute-start.3
  99.4 0.5 collective-permute-start.4
  100.0 1.0 deliver.2
  101.0 12.8 %collective-permute-done.3.refs_0_ = bf16[1,128,2048]{2,1,0:T(8,128)(2,1)S(1)} collective-permute-done((bf16[1,128,2048]{2,1,0:T(8,128)(2,1)S(1)}, bf16[1,128,2048]{2,1,0:T(8,128)(2,1)S(1)}, u32[]{:S(2)}, u32[]{:S(2)}) %collective-permute-start.3) | collective-permute-done | bytes 524320 | tf_op jit(solution)/shard_map/ppermute | solution.py:313
  113.7 7.4 %collective-permute-done.4.refs_1_ = bf16[1,128,2048]{2,1,0:T(8,128)(2,1)S(1)} collective-permute-done((bf16[1,128,2048]{2,1,0:T(8,128)(2,1)S(1)}, bf16[1,128,2048]{2,1,0:T(8,128)(2,1)S(1)}, u32[]{:S(2)}, u32[]{:S(2)}) %collective-permute-start.4) | collective-permute-done | bytes 524320 | tf_op jit(solution)/shard_map/ppermute | solution.py:313
  121.1 1.0 deliver.3
Async XLA Ops:
  0.6 0.7 copy-start.1
  41.0 0.7 copy-start.3
  46.2 1.4 %collective-permute-start = (f32[16,128]{1,0:T(8,128)S(1)}, f32[16,128]{1,0:T(8,128)S(1)}, u32[]{:S(2)}, u32[]{:S(2)}) collective-permute-start(f32[16,128]{1,0:T(8,128)S(1)} %get-tuple-element.47.mine_ref), channel_id=1, source_target_pairs={{0,1},{1,0},{2,3},{3,2},{4,5},{5,4},{6,7},{7,6},{8,9},{9,8},{10,11... | collective-permute-start | bytes 24584 | tf_op jit(solution)/shard_map/ppermute | solution.py:341
  47.6 14.5 %copy-start.2 = (f32[1,2048]{1,0:T(1,128)S(1)}, f32[1,2048]{1,0:T(1,128)}, u32[]{:S(2)}) copy-start(f32[1,2048]{1,0:T(1,128)} %bound_ref.3) | copy-start | bytes 24580
  56.6 2.0 %copy-start = (f32[16,4,128,128]{3,2,1,0:T(8,128)}, f32[16,4,128,128]{3,2,1,0:T(8,128)S(1)}, u32[]{:S(2)}) copy-start(f32[16,4,128,128]{3,2,1,0:T(8,128)S(1)} %get-tuple-element.63.kept_hbm) | copy-start | bytes 12582916
  58.5 34.3 %collective-permute-start.1 = (bf16[1,128,2048]{2,1,0:T(8,128)(2,1)S(1)}, bf16[1,128,2048]{2,1,0:T(8,128)(2,1)S(1)}, u32[]{:S(2)}, u32[]{:S(2)}) collective-permute-start(bf16[1,128,2048]{2,1,0:T(8,128)(2,1)S(1)} %get-tuple-element.58), channel_id=1, source_target_pairs={{0,96},{32,0},{64,32},{96,64},{1,97},{33,1},{65,33},{97,65},{2,98}... | collective-permute-start | bytes 1572872 | tf_op jit(solution)/shard_map/ppermute | solution.py:313
  61.3 31.5 %collective-permute-start.2 = (bf16[1,128,2048]{2,1,0:T(8,128)(2,1)S(1)}, bf16[1,128,2048]{2,1,0:T(8,128)(2,1)S(1)}, u32[]{:S(2)}, u32[]{:S(2)}) collective-permute-start(bf16[1,128,2048]{2,1,0:T(8,128)(2,1)S(1)} %get-tuple-element.59), channel_id=1, source_target_pairs={{0,96},{32,0},{64,32},{96,64},{1,97},{33,1},{65,33},{97,65},{2,98}... | collective-permute-start | bytes 1572872 | tf_op jit(solution)/shard_map/ppermute | solution.py:313
  98.8 14.9 %collective-permute-start.3 = (bf16[1,128,2048]{2,1,0:T(8,128)(2,1)S(1)}, bf16[1,128,2048]{2,1,0:T(8,128)(2,1)S(1)}, u32[]{:S(2)}, u32[]{:S(2)}) collective-permute-start(bf16[1,128,2048]{2,1,0:T(8,128)(2,1)S(1)} %get-tuple-element.65), channel_id=1, source_target_pairs={{0,96},{32,0},{64,32},{96,64},{1,97},{33,1},{65,33},{97,65},{2,98}... | collective-permute-start | bytes 1572872 | tf_op jit(solution)/shard_map/ppermute | solution.py:313
  99.4 21.7 %collective-permute-start.4 = (bf16[1,128,2048]{2,1,0:T(8,128)(2,1)S(1)}, bf16[1,128,2048]{2,1,0:T(8,128)(2,1)S(1)}, u32[]{:S(2)}, u32[]{:S(2)}) collective-permute-start(bf16[1,128,2048]{2,1,0:T(8,128)(2,1)S(1)} %get-tuple-element.66), channel_id=1, source_target_pairs={{0,96},{32,0},{64,32},{96,64},{1,97},{33,1},{65,33},{97,65},{2,98}... | collective-permute-start | bytes 1572872 | tf_op jit(solution)/shard_map/ppermute | solution.py:313

commit v4 on v3

v4 whole, which is shorter than its diff:
```python
import functools

import jax
import jax.numpy as jnp
from jax import lax
from jax.experimental import pallas as pl
from jax.experimental.pallas import tpu as pltpu
from jax.sharding import PartitionSpec as P

DK = 128
BLOCK = 128
HEAD_COLUMNS = 4096
EPSILON = 1e-06

F32 = jnp.float32
BF16 = jnp.bfloat16
NN = ((1,), (0,))
NT = ((1,), (1,))
TN = ((0,), (0,))
RANGE = 84.0
EXTRA = 16
PIECES = 4
GROUP = 4
SHARES = (3, 4, 1)
PARAMS = pltpu.CompilerParams(vmem_limit_bytes=24 * 1024 * 1024)
VMEM = pl.BlockSpec(memory_space=pltpu.VMEM)
SMEM = pl.BlockSpec(memory_space=pltpu.SMEM)


def parts(x, count=2):
    if x.dtype == BF16:
        return [x]
    terms = []
    for _ in range(count - 1):
        term = x.astype(BF16)
        terms.append(term)
        x = x - term.astype(F32)
    return terms + [x.astype(BF16)]


def product(left, right, dims):
    pairs = [
        (a, b)
        for i, a in enumerate(left)
        for j, b in enumerate(right)
        if i + j < max(len(left), len(right))
    ]
    lhs = jnp.concatenate([a for a, _ in pairs], axis=dims[0][0])
    rhs = jnp.concatenate([b for _, b in pairs], axis=dims[1][0])
    return lax.dot_general(lhs, rhs, (dims, ((), ())), preferred_element_type=F32)


def triangle(lower):
    row = lax.broadcasted_iota(jnp.int32, (BLOCK, BLOCK), 0)
    col = lax.broadcasted_iota(jnp.int32, (BLOCK, BLOCK), 1)
    return row >= col if lower else row <= col


def of_head(ref, h):
    return ref[0, :, pl.ds(pl.multiple_of(h * DK, DK), DK)]


def put_head(ref, h, value, index=0):
    ref[index, :, pl.ds(pl.multiple_of(h * DK, DK), DK)] = value


def pair_of(ref, h):
    return [ref[h, 0], ref[h, 1]]


def put_pair(ref, h, terms):
    ref[h, 0], ref[h, 1] = terms


def sum_of(terms):
    return terms[0].astype(F32) + terms[1].astype(F32)


def forget_of(squashed, bound):
    return bound + (1.0 - bound) * squashed


def encode(ref, i, x, *rows):
    top = jnp.maximum(jnp.max(jnp.abs(x), axis=0, keepdims=True), 1e-36)
    top = (top * 1.01).astype(BF16).astype(F32)
    ref[i, :DK] = jnp.exp(x * (RANGE / top)).astype(BF16)
    place = lax.broadcasted_iota(jnp.int32, (EXTRA, DK), 0)
    extra = jnp.zeros((EXTRA, DK), F32)
    for r, row in enumerate((top,) + rows):
        extra = jnp.where(place == r, row, extra)
    ref[i, DK:] = extra.astype(BF16)


def decode(ref, i):
    extra = ref[i, DK:].astype(F32)
    return jnp.log(ref[i, :DK].astype(F32)) * (extra[0:1] * (1.0 / RANGE)), extra


def call(kernel, name, ins, outs, streamed=(), kept=(), scratch=()):
    hbm = pl.BlockSpec(memory_space=pltpu.HBM)
    return pl.pallas_call(
        kernel,
        out_shape=[*outs, *[pltpu.HBM(x.shape, x.dtype) for x in kept]],
        in_specs=[hbm] * len(streamed) + [VMEM] * len(ins),
        out_specs=[SMEM if x.ndim == 1 else VMEM for x in outs] + [hbm] * len(kept),
        scratch_shapes=scratch,
        compiler_params=PARAMS,
        name=name,
    )(*[pltpu.with_memory_space_constraint(x, pltpu.HBM) for x in streamed], *ins)


def buffers(*arrays):
    return [pltpu.VMEM(x.shape, x.dtype) for x in arrays] + [pltpu.SemaphoreType.DMA((len(arrays), PIECES))]


def piece_of(ref, p):
    if ref.shape[0] == 1:
        width = ref.shape[2] // PIECES
        return ref.at[:, :, pl.ds(p * width, width)]
    each = ref.shape[0] // PIECES
    return ref.at[pl.ds(p * each, each)]


def start_piece(sources, targets, sems, p):
    copies = [
        pltpu.make_async_copy(piece_of(source, p), piece_of(target, p), sems.at[a, p])
        for a, (source, target) in enumerate(zip(sources, targets))
    ]
    for copy in copies:
        copy.start()
    return copies


def start_copies(sources, targets, sems, heads):
    copies = [start_piece(sources, targets, sems, p) for p in range(PIECES)]

    def wait(h):
        if h % (heads // PIECES) == 0:
            for copy in copies[h * PIECES // heads]:
                copy.wait()

    return wait


def together(turn, heads, wait=None, after=None):
    for first in range(0, heads, GROUP):
        for h in range(first, first + GROUP):
            if wait is not None:
                wait(h)
        turns = [turn(h) for h in range(first, first + GROUP)]
        while turns:
            turns = [t for t in turns if next(t, None) is not None]
        if after is not None:
            for h in range(first, first + GROUP):
                after(h)


def own_state_kernel(
    logit_hbm, value_hbm, bound_hbm, run_ref, k_ref, own_ref, v_ref, coded_ref,
    logit_ref, value_ref, bound_ref, sems,
):
    wait = start_copies(
        (logit_hbm, value_hbm, bound_hbm), (logit_ref, value_ref, bound_ref), sems, own_ref.shape[0]
    )
    ones_below = [jnp.where(triangle(True), 1.0, 0.0).astype(BF16)]
    for h in range(own_ref.shape[0]):
        wait(h)
        bound = of_head(bound_ref, h)
        squashed = jax.nn.sigmoid(of_head(logit_ref, h).astype(F32))
        forget = forget_of(squashed, bound)
        run = product(ones_below, parts(jnp.log(forget), 2), NN)
        k_scaled = parts((1.0 - forget) * jnp.exp(-run))
        last = run[BLOCK - 1 : BLOCK]
        v = of_head(value_ref, h)
        own = product([v], k_scaled, TN)
        run_ref[h] = run
        v_ref[h] = v
        put_pair(k_ref, h, k_scaled)
        own_ref[h] = own
        encode(coded_ref, h, own * jnp.exp(last), *[term.astype(F32) for term in parts(last, 3)])


def states_before_kernel(coded_ref, out_ref, decay_ref):
    state = jnp.zeros((DK, DK), F32)
    for i in range(coded_ref.shape[0]):
        encode(out_ref, i, state)
        own, extra = decode(coded_ref, i)
        decay = jnp.exp(extra[1:2] + extra[2:3] + extra[3:4])
        decay_ref[i] = jnp.broadcast_to(decay, decay_ref.shape[1:])
        state = state * decay + own


def states_after_kernel(coded_ref, decay_ref, out_ref):
    later = jnp.zeros((DK, DK), F32)
    for i in reversed(range(coded_ref.shape[0])):
        later = later * decay_ref[i, 0:1]
        encode(out_ref, i, later)
        later = later + decode(coded_ref, i)[0]


def attended_kernel(
    query_hbm, gates_hbm, grad_hbm, gain_hbm, coded_ref, run_ref, k_ref, v_ref,
    q_ref, score_ref, pull_ref, gate_ref, att_ref, state_ref, sums_ref, go_ref,
    query_ref, gates_ref, grad_ref, gain_ref, sems,
):
    wait = start_copies(
        (query_hbm, gates_hbm, grad_hbm, gain_hbm), (query_ref, gates_ref, grad_ref, gain_ref), sems, v_ref.shape[0]
    )
    lower = triangle(True)
    go_ref[0] = 1
    totals = [jnp.zeros((BLOCK, DK), F32)] * 2

    def turn(h):
        q_scaled = parts(of_head(query_ref, h).astype(F32) * jnp.exp(run_ref[h]))
        put_pair(q_ref, h, q_scaled)
        yield True
        scores = product(q_scaled, pair_of(k_ref, h), NT)
        states = parts(decode(coded_ref, h)[0])
        put_pair(state_ref, h, states)
        yield True
        scores = parts(jnp.where(lower, scores, 0.0))
        put_pair(score_ref, h, scores)
        yield True
        attended = product(scores, [v_ref[h]], NN) + product(q_scaled, states, NT)
        gates = of_head(gates_ref, h).astype(F32)
        gated = jax.nn.sigmoid(gates)
        grad = of_head(grad_ref, h).astype(F32) * of_head(gain_ref, h)
        pull = grad * (gates * gated)
        pull_ref[h] = pull
        gate_ref[h] = grad * gated * (1.0 + gates * (1.0 - gated))
        yield True
        att_ref[h] = attended
        totals[0] = totals[0] + attended * attended
        totals[1] = totals[1] + pull * attended

    together(turn, v_ref.shape[0], wait)
    for i, total in enumerate(totals):
        sums_ref[8 * i : 8 * i + 8] = jnp.broadcast_to(jnp.sum(total.T, axis=0, keepdims=True), (8, BLOCK))


def early_grads_kernel(
    mine_ref, other_ref, att_ref, pull_ref, gate_ref, run_ref, q_ref, k_ref, v_ref, own_ref, state_ref, score_ref,
    coded_ref, grads_ref, kept_hbm, value_part_hbm, k_hbm, kept_ref, value_part_ref, sems, k_sem,
):
    heads = v_ref.shape[0]
    copies = [pltpu.make_async_copy(k_ref, k_hbm, k_sem)]
    copies[0].start()
    ones_above = [jnp.where(triangle(False), 1.0, 0.0).astype(BF16)]
    sums = mine_ref[...] + other_ref[...]
    root = jnp.sqrt(sums[0:8] / HEAD_COLUMNS + EPSILON)
    weigh = sums[8:16] / (HEAD_COLUMNS * (root * root * root))
    fill = jnp.zeros((BLOCK - 16, BLOCK), F32)
    columns = jnp.concatenate([1.0 / root, weigh, fill], axis=0).T
    over_root = jnp.broadcast_to(columns[:, 0:1], (BLOCK, DK))
    weigh = jnp.broadcast_to(columns[:, 8:9], (BLOCK, DK))
    lower = triangle(True)

    def turn(h):
        attended = att_ref[h]
        put_head(grads_ref, h, (gate_ref[h] * (attended * over_root)).astype(BF16))
        douts = parts(pull_ref[h] * over_root - attended * weigh)
        q_scaled = pair_of(q_ref, h)
        yield True
        own = product(douts, q_scaled, TN)
        pairs = product(douts, [v_ref[h]], NT)
        yield True
        encode(coded_ref, h, own)
        pairs = parts(jnp.where(lower, pairs, 0.0))
        value_part_ref[h] = product(pair_of(score_ref, h), douts, TN)
        yield True
        k_scaled = pair_of(k_ref, h)
        states = pair_of(state_ref, h)
        q_part = product(pairs, k_scaled, NN) + product(douts, states, NN)
        k_part = product(pairs, q_scaled, TN)
        yield True
        grow = jnp.exp(run_ref[h])
        shrink = jnp.exp(-run_ref[h])
        put_head(grads_ref, h, (grow * q_part).astype(BF16), 1)
        keys = sum_of(k_scaled)
        terms = parts(sum_of(q_scaled) * q_part - keys * k_part, 2)
        kept_ref[h, 1] = shrink
        kept_ref[h, 2] = sum_of(states) + own_ref[h]
        yield True
        kept_ref[h, 0] = product(ones_above, terms, NN) - (1.0 - keys * grow) * (shrink * k_part)

    def after(h):
        if (h + 1) % (heads // PIECES) == 0:
            copies.extend(
                start_piece((kept_ref, value_part_ref), (kept_hbm, value_part_hbm), sems, h * PIECES // heads)
            )

    together(turn, heads, after=after)
    for copy in copies:
        copy.wait()


def value_grad_kernel(
    value_part_hbm, k_hbm, coded_ref, first_ref, second_ref, third_ref, value_part_ref, k_ref, sems
):
    heads = k_ref.shape[0]
    wait = start_copies((value_part_hbm, k_hbm), (value_part_ref, k_ref), sems, heads)
    for h in range(heads):
        wait(h)
        v_grad = value_part_ref[h] + product(pair_of(k_ref, h), parts(decode(coded_ref, h)[0]), NT)
        start = 0
        for ref in (first_ref, second_ref, third_ref):
            count = ref.shape[2] // DK
            if start <= h < start + count:
                put_head(ref, h - start, v_grad.astype(BF16))
            start += count


def logit_grad_kernel(
    logit_hbm, value_hbm, bound_hbm, kept_hbm, coded_ref, third_ref, logit_grad_ref,
    logit_ref, value_ref, bound_ref, kept_ref, sems,
):
    heads = kept_ref.shape[0]
    logit_grad_ref[0, :, heads * DK :] = third_ref[0]
    wait = start_copies(
        (logit_hbm, value_hbm, bound_hbm, kept_hbm), (logit_ref, value_ref, bound_ref, kept_ref), sems, heads
    )
    ones_above = [jnp.where(triangle(False), 1.0, 0.0).astype(BF16)]
    for h in range(heads):
        wait(h)
        later = decode(coded_ref, h)[0]
        shrink = kept_ref[h, 1]
        bound = of_head(bound_ref, h)
        squashed = jax.nn.sigmoid(of_head(logit_ref, h).astype(F32))
        forget = forget_of(squashed, bound)
        log_later = jnp.sum(kept_ref[h, 2] * later, axis=0, keepdims=True)
        k_part = shrink * product([of_head(value_ref, h)], parts(later), NN)
        log_grad = log_later - product(ones_above, parts((1.0 - forget) * k_part, 2), NN)
        logit_grad = (kept_ref[h, 0] + log_grad) / forget - k_part
        put_head(logit_grad_ref, h, (logit_grad * (1.0 - bound) * squashed * (1.0 - squashed)).astype(BF16))


def deliver_kernel(places, *refs):
    sources, targets, sems = refs[: len(places)], refs[len(places) : -1], refs[-1]
    copies = []
    for source, place in zip(sources, places):
        for index, column, width, target, start in place:
            copies.append(
                pltpu.make_async_copy(
                    source.at[pl.ds(index, 1), :, pl.ds(column, width)],
                    targets[target].at[:, :, pl.ds(start, width)],
                    sems.at[len(copies)],
                )
            )
            copies[-1].start()
    for copy in copies:
        copy.wait()


def deliver(arrays, places, outs):
    return pl.pallas_call(
        functools.partial(deliver_kernel, places),
        out_shape=outs,
        in_specs=[VMEM] * len(arrays),
        out_specs=[pl.BlockSpec(memory_space=pltpu.HBM)] * len(outs),
        scratch_shapes=[pltpu.SemaphoreType.DMA((sum(map(len, places)),))],
        compiler_params=PARAMS,
        name="deliver",
    )(*arrays)


def to_section(x, by):
    size = lax.axis_size("pipe")
    return lax.ppermute(x, "pipe", [(i, (i + by) % size) for i in range(size)])


def exchange(x):
    return lax.all_to_all(x, "ctx", 0, 0)


def body(queries, forget_logits, values, gates, output_grad, lower_bound, norm_gain):
    heads = queries.shape[2] // DK
    whole = jax.ShapeDtypeStruct(queries.shape, BF16)
    square = jax.ShapeDtypeStruct((heads, BLOCK, DK), F32)
    pair = jax.ShapeDtypeStruct((heads, 2, BLOCK, DK), BF16)
    coded = jax.ShapeDtypeStruct((heads, DK + EXTRA, DK), BF16)
    decays = jax.ShapeDtypeStruct((heads, 8, DK), F32)
    sums = jax.ShapeDtypeStruct((16, BLOCK), F32)
    plain = jax.ShapeDtypeStruct((heads, BLOCK, DK), BF16)
    columns = heads * DK
    around, ahead, beside = [columns * share // 8 for share in SHARES]
    first, second, third, rest = [
        jax.ShapeDtypeStruct((1, BLOCK, width), BF16) for width in (around, ahead, beside, columns + beside)
    ]
    kept = jax.ShapeDtypeStruct((heads, 3, BLOCK, DK), F32)
    flag = jax.ShapeDtypeStruct((1,), jnp.int32)

    both = jax.ShapeDtypeStruct((2, BLOCK, heads * DK), BF16)
    bound, gain = lower_bound[None], norm_gain[None]

    run, k_scaled, own_state, v, sent = call(
        own_state_kernel, "own_state", [], [square, pair, square, plain, coded],
        streamed=[forget_logits, values, bound], scratch=buffers(whole, whole, bound),
    )
    sent, decay = call(states_before_kernel, "states_before", [exchange(sent)], [coded, decays])
    q_scaled, scores, pull, gate_factor, attended, states, mine, go = call(
        attended_kernel, "attended", [exchange(sent), run, k_scaled, v],
        [pair, pair, square, square, square, pair, sums, flag], streamed=[queries, gates, output_grad, gain],
        scratch=buffers(whole, whole, whole, gain),
    )
    other = lax.ppermute(mine, "tp", [(0, 1), (1, 0)])
    sent, early, kept_now, value_part, k_kept = call(
        early_grads_kernel, "early_grads",
        [mine, other, attended, pull, gate_factor, run, q_scaled, k_scaled, v, own_state, states, scores],
        [coded, both], kept=[kept, square, pair], scratch=buffers(kept, square) + [pltpu.SemaphoreType.DMA],
    )
    early = to_section(early, -1)

    def through(sent, decay):
        (sent,) = call(states_after_kernel, "states_after", [exchange(sent), decay], [coded])
        return exchange(sent)

    arrived = lax.cond(go[0] > 0, through, lambda sent, decay: sent, sent, decay)
    arrived, early = lax.optimization_barrier((arrived, early))
    first, second, third = call(
        value_grad_kernel, "value_grad", [arrived], [first, second, third], streamed=[value_part, k_kept],
        scratch=buffers(square, pair),
    )
    first = to_section(first, 1)
    second = to_section(second, -1)
    (rest,) = call(
        logit_grad_kernel, "logit_grad", [arrived, third], [rest],
        streamed=[forget_logits, values, bound, kept_now], scratch=buffers(whole, whole, bound, kept),
    )
    rest, first, second = lax.optimization_barrier((rest, first, second))
    rest = to_section(rest, -1)
    for _ in range(lax.axis_size("pipe") - 2):
        first = to_section(first, 1)
    gate_grad, query_grad = deliver([early], [((0, 0, columns, 0, 0), (1, 0, columns, 1, 0))], [whole, whole])
    logit_grad, value_grad = deliver(
        [rest, first, second],
        [
            ((0, 0, columns, 0, 0), (0, columns, beside, 1, around + ahead)),
            ((0, 0, around, 1, 0),),
            ((0, 0, ahead, 1, around),),
        ],
        [whole, whole],
    )
    return query_grad, logit_grad, value_grad, gate_grad


def solution(mesh):
    rows = P("pipe", "ctx", "tp")
    return jax.shard_map(
        body,
        mesh=mesh,
        in_specs=(rows,) * 5 + (P("pipe", "tp"),) * 2,
        out_specs=(rows,) * 4,
        check_vma=False,
    )
```

time: 123 us -> 109 us (0.89)
  Pallas kernels: 27.1 us -> 19.9 us
  waiting for transfers between devices: 21.3 us -> 15.6 us
  local copies, waits for them, and re-layouts: 3.86 us -> 0 us
  starting transfers between devices: 5.01 us -> 7.76 us
    pallas_call x8 -> x9, Pallas kernels: 27.1 us -> 19.9 us  [the longest x7 17.9 us: call(): pl.pallas_call(kernel, out_shape=[*outs, *[pltpu.HBM(x.shape, x.dtype) fo...]
    ppermute x4 -> x6, waiting for transfers between devices: 20.2 us -> 14.4 us  [to_section(): return lax.ppermute(x, 'pipe', [(i, (i + by) % size) for i in range(size)])]
    unnamed x8 -> x0, local copies, waits for them, and re-layouts: 3.35 us -> none
    ppermute x4 -> x6, starting transfers between devices: 4.74 us -> 7.68 us  [to_section(): return lax.ppermute(x, 'pipe', [(i, (i + by) % size) for i in range(size)])]
  transfers between devices with their start and end apart: 5 -> 7, of which waited for: 3 -> 4; matrix products, arithmetic and copies ran while one was open for 0% -> 0% of each run, Pallas kernels for 1% -> 4%
where the time goes in v4:
time: 109 us
  blocking collectives  64.1 us (59%)
  Pallas kernels  19.9 us (18%)
  waiting for transfers between devices  15.6 us (14%)
  starting transfers between devices  7.76 us (7%)
  between operations  1.51 us (1%)
    all_to_all x4, blocking collectives, exchange(): return lax.all_to_all(x, 'ctx', 0, 0)  64.1 us
    pallas_call x7, Pallas kernels, call(): pl.pallas_call(kernel, out_shape=[*outs, *[pltpu.HBM(x.shape, x.dtype) fo...  17.9 us
    ppermute x6, waiting for transfers between devices, to_section(): return lax.ppermute(x, 'pipe', [(i, (i + by) % size) for i in range(size)])  14.4 us
    ppermute x6, starting transfers between devices, to_section(): return lax.ppermute(x, 'pipe', [(i, (i + by) % size) for i in range(size)])  7.68 us
  transfers between devices with their start and end apart: 7, of which 4 were waited for; matrix products, arithmetic and copies ran while one was open for 0% of the time, Pallas kernels for 4%

profile of v4, /device:TPU:0, one launch (start us, length us, event | category | flops | bytes accessed | tf_op | source)
XLA Modules:
  0.0 108.8 jit_solution(2204664158624240765)
XLA Ops:
  0.6 3.1 %own_state.1 = (f32[16,128,128]{2,1,0:T(8,128)S(1)}, bf16[16,2,128,128]{3,2,1,0:T(8,128)(2,1)S(1)}, f32[16,128,128]{2,1,0:T(8,128)S(1)}, bf16[16,128,128]{2,1,0:T(8,128)(2,1)S(1)}, bf16[16,144,128]{2,1,0:T(8,128)(2,1)S(1)}) custom-call(bf16[1,128,2048]{2,1,0:T(8,128)(2,1)} %logit_hbm.3, bf16[1,128,2048]{2,1,0:T(8,128)(2,1)} %value_hbm.3, f32[1,1,2048]{2,1,0:T(1,128)} %bitcast.3), custom_call_target="tpu_custom_call" | custom-call | tf_op jit(solution)/shard_map/own_state/pallas_call | solution.py:101
  3.7 20.2 %all_to_all.20.coded_ref = bf16[16,144,128]{2,1,0:T(8,128)(2,1)S(1)} all-to-all(bf16[16,144,128]{2,1,0:T(8,128)(2,1)S(1)} %get-tuple-element.46), channel_id=1, replica_groups=mesh['pipe'=4,'ctx'=16,'tp'=2] {'ctx'}, dimensions={0} | all-to-all | bytes 1179648 | tf_op jit(solution)/shard_map/all_to_all | solution.py:372
  23.9 0.4 states_before.1
  24.3 14.2 %all_to_all.21.coded_ref = bf16[16,144,128]{2,1,0:T(8,128)(2,1)S(1)} all-to-all(bf16[16,144,128]{2,1,0:T(8,128)(2,1)S(1)} %get-tuple-element.47), channel_id=1, replica_groups=mesh['pipe'=4,'ctx'=16,'tp'=2] {'ctx'}, dimensions={0} | all-to-all | bytes 1179648 | tf_op jit(solution)/shard_map/all_to_all | solution.py:372
  38.5 3.8 %attended.1 = (bf16[16,2,128,128]{3,2,1,0:T(8,128)(2,1)S(1)}, bf16[16,2,128,128]{3,2,1,0:T(8,128)(2,1)S(1)}, f32[16,128,128]{2,1,0:T(8,128)S(1)}, f32[16,128,128...) custom-call(bf16[1,128,2048]{2,1,0:T(8,128)(2,1)} %query_hbm.1, ...), custom_call_target="tpu_custom_call" | custom-call | tf_op jit(solution)/shard_map/attended/pallas_call | solution.py:101
  42.3 0.1 collective-permute-start
  42.3 1.2 %collective-permute-done.other_ref = f32[16,128]{1,0:T(8,128)S(1)} collective-permute-done((f32[16,128]{1,0:T(8,128)S(1)}, f32[16,128]{1,0:T(8,128)S(1)}, u32[]{:S(2)}, u32[]{:S(2)}) %collective-permute-start) | collective-permute-done | bytes 8224 | tf_op jit(solution)/shard_map/ppermute | solution.py:405
  43.5 4.6 %early_grads.1 = (bf16[16,144,128]{2,1,0:T(8,128)(2,1)S(1)}, bf16[2,128,2048]{2,1,0:T(8,128)(2,1)S(1)}, f32[16,3,128,128]{3,2,1,0:T(8,128)}, f32[16,128,128]{2,1,0:T(8,128)}, bf16[16,2,128,128]{3,2,1,0:T(8,128)(2,1)}) custom-call(f32[16,128]{1,0:T(8,128)S(1)} %get-tuple-element.52.mine_ref, f32[16,128]{1,0:T(8,128)S(1)} %collective-permute-done.other_ref, ...), custom_call_target="tpu_custom_call" | custom-call | tf_op jit(solution)/shard_map/early_grads/pallas_call | solution.py:101
  48.1 2.8 %collective-permute-start.1 = (bf16[2,128,2048]{2,1,0:T(8,128)(2,1)S(1)}, bf16[2,128,2048]{2,1,0:T(8,128)(2,1)S(1)}, u32[]{:S(2)}, u32[]{:S(2)}) collective-permute-start(bf16[2,128,2048]{2,1,0:T(8,128)(2,1)S(1)} %get-tuple-element.62), channel_id=1, source_target_pairs={{0,96},{32,0},{64,32},{96,64},{1,97},{33,1},{65,33},{97,65},{2,98}... | collective-permute-start | bytes 3145736 | tf_op jit(solution)/shard_map/ppermute | solution.py:368
  51.6 30.1 %conditional.1 = (bf16[16,144,128]{2,1,0:T(8,128)(2,1)S(1)}) conditional(s32[]{:T(128)} %bitcast.2, bf16[16,144,128]{2,1,0:T(8,128)(2,1)S(1)} %get-tuple-element.60, (bf16[16,144,128]{2,1,0:T(8,128)(2,1)S(1)}, f32[16,8,128]{2,1,0:T(8,128)S(1)}) %tuple.16), branch_computations={%region_0.0_spmd, %region_1.0_spmd} | conditional | bytes 2359304 | solution.py:417
  51.6 15.4 %all_to_all.18.coded_ref = bf16[16,144,128]{2,1,0:T(8,128)(2,1)S(1)} all-to-all(bf16[16,144,128]{2,1,0:T(8,128)(2,1)S(1)} %get-tuple-element.8), channel_id=1, replica_groups=mesh['pipe'=4,'ctx'=16,'tp'=2] {'ctx'}, dimensions={0} | all-to-all | bytes 1179648 | tf_op jit(solution)/shard_map/cond/branch_1_fun/all_to_all | solution.py:372
  67.1 0.4 states_after.1
  67.5 14.3 %all_to_all.19 = bf16[16,144,128]{2,1,0:T(8,128)(2,1)S(1)} all-to-all(bf16[16,144,128]{2,1,0:T(8,128)(2,1)S(1)} %states_after.1), channel_id=1, replica_groups=mesh['pipe'=4,'ctx'=16,'tp'=2] {'ctx'}, dimensions={0} | all-to-all | bytes 1179648 | tf_op jit(solution)/shard_map/cond/branch_1_fun/all_to_all | solution.py:372
  81.7 0.0 collective-permute-done.1.refs_0_
  81.7 2.4 %value_grad.1 = (bf16[1,128,768]{2,1,0:T(8,128)(2,1)S(1)}, bf16[1,128,1024]{2,1,0:T(8,128)(2,1)S(1)}, bf16[1,128,256]{2,1,0:T(8,128)(2,1)S(1)}) custom-call(f32[16,128,128]{2,1,0:T(8,128)} %get-tuple-element.67.value_part_hbm, bf16[16,2,128,128]{3,2,1,0:T(8,128)(2,1)} %get-tuple-element.68.k_hbm, bf16[16,144,128]{2,1,0:T(8,128)(2,1)S(1)} %get-tuple-element.78.coded_ref), custom_call_target="tpu_custom_call" | custom-call | tf_op jit(solution)/shard_map/value_grad/pallas_call | solution.py:101
  84.1 0.9 collective-permute-start.3
  85.0 1.2 %collective-permute-start.2 = (bf16[1,128,768]{2,1,0:T(8,128)(2,1)S(1)}, bf16[1,128,768]{2,1,0:T(8,128)(2,1)S(1)}, u32[]{:S(2)}, u32[]{:S(2)}) collective-permute-start(bf16[1,128,768]{2,1,0:T(8,128)(2,1)S(1)} %get-tuple-element.70), channel_id=1, source_target_pairs={{0,32},{32,64},{64,96},{96,0},{1,33},{33,65},{65,97},{97,1},{2,34}... | collective-permute-start | bytes 589832 | tf_op jit(solution)/shard_map/ppermute | solution.py:368
  86.2 3.2 %logit_grad.1 = bf16[1,128,2304]{2,1,0:T(8,128)(2,1)S(1)} custom-call(bf16[1,128,2048]{2,1,0:T(8,128)(2,1)} %logit_hbm.3, bf16[1,128,2048]{2,1,0:T(8,128)(2,1)} %value_hbm.3, f32[1,1,2048]{2,1,0:T(1,128)} %bitcast.4, f32[16,3,128,128]{3,2,1,0:T(8,128)} %get-tuple-element.65.kept_hbm, bf16[16,144,128]{2,1,0:T(8,128)(2,1)S(1)} %get-tuple-element.78.coded_ref, ...), custom_call_target="tpu_custom_call" | custom-call | tf_op jit(solution)/shard_map/logit_grad/pallas_call | solution.py:101
  89.5 2.4 %collective-permute-done.2 = bf16[1,128,768]{2,1,0:T(8,128)(2,1)S(1)} collective-permute-done((bf16[1,128,768]{2,1,0:T(8,128)(2,1)S(1)}, bf16[1,128,768]{2,1,0:T(8,128)(2,1)S(1)}, u32[]{:S(2)}, u32[]{:S(2)}) %collective-permute-start.2) | collective-permute-done | bytes 196640 | tf_op jit(solution)/shard_map/ppermute | solution.py:368
  91.9 0.0 collective-permute-done.3.refs_2_
  91.9 0.7 collective-permute-start.4
  92.6 1.3 %collective-permute-start.5 = (bf16[1,128,768]{2,1,0:T(8,128)(2,1)S(1)}, bf16[1,128,768]{2,1,0:T(8,128)(2,1)S(1)}, u32[]{:S(2)}, u32[]{:S(2)}) collective-permute-start(bf16[1,128,768]{2,1,0:T(8,128)(2,1)S(1)} %collective-permute-done.2), channel_id=1, source_target_pairs={{0,32},{32,64},{64,96},{96,0},{1,33},{33,65},{65,97},{97,1},{2,34}... | collective-permute-start | bytes 589832 | tf_op jit(solution)/shard_map/ppermute | solution.py:368
  94.0 6.8 %collective-permute-done.5 = bf16[1,128,768]{2,1,0:T(8,128)(2,1)S(1)} collective-permute-done((bf16[1,128,768]{2,1,0:T(8,128)(2,1)S(1)}, bf16[1,128,768]{2,1,0:T(8,128)(2,1)S(1)}, u32[]{:S(2)}, u32[]{:S(2)}) %collective-permute-start.5) | collective-permute-done | bytes 196640 | tf_op jit(solution)/shard_map/ppermute | solution.py:368
  100.8 0.7 collective-permute-start.6
  101.5 1.0 deliver.2
  102.5 5.2 %collective-permute-done.6.refs_1_ = bf16[1,128,768]{2,1,0:T(8,128)(2,1)S(1)} collective-permute-done((bf16[1,128,768]{2,1,0:T(8,128)(2,1)S(1)}, bf16[1,128,768]{2,1,0:T(8,128)(2,1)S(1)}, u32[]{:S(2)}, u32[]{:S(2)}) %collective-permute-start.6) | collective-permute-done | bytes 196640 | tf_op jit(solution)/shard_map/ppermute | solution.py:368
  107.7 0.0 collective-permute-done.4.refs_0_
  107.7 1.0 deliver.3
Async XLA Ops:
  42.3 1.3 %collective-permute-start = (f32[16,128]{1,0:T(8,128)S(1)}, f32[16,128]{1,0:T(8,128)S(1)}, u32[]{:S(2)}, u32[]{:S(2)}) collective-permute-start(f32[16,128]{1,0:T(8,128)S(1)} %get-tuple-element.52.mine_ref), channel_id=1, source_target_pairs={{0,1},{1,0},{2,3},{3,2},{4,5},{5,4},{6,7},{7,6},{8,9},{9,8},{10,11... | collective-permute-start | bytes 24584 | tf_op jit(solution)/shard_map/ppermute | solution.py:405
  48.1 33.6 %collective-permute-start.1 = (bf16[2,128,2048]{2,1,0:T(8,128)(2,1)S(1)}, bf16[2,128,2048]{2,1,0:T(8,128)(2,1)S(1)}, u32[]{:S(2)}, u32[]{:S(2)}) collective-permute-start(bf16[2,128,2048]{2,1,0:T(8,128)(2,1)S(1)} %get-tuple-element.62), channel_id=1, source_target_pairs={{0,96},{32,0},{64,32},{96,64},{1,97},{33,1},{65,33},{97,65},{2,98}... | collective-permute-start | bytes 3145736 | tf_op jit(solution)/shard_map/ppermute | solution.py:368
  84.1 7.8 %collective-permute-start.3 = (bf16[1,128,1024]{2,1,0:T(8,128)(2,1)S(1)}, bf16[1,128,1024]{2,1,0:T(8,128)(2,1)S(1)}, u32[]{:S(2)}, u32[]{:S(2)}) collective-permute-start(bf16[1,128,1024]{2,1,0:T(8,128)(2,1)S(1)} %get-tuple-element.71), channel_id=1, source_target_pairs={{0,96},{32,0},{64,32},{96,64},{1,97},{33,1},{65,33},{97,65},{2,98}... | collective-permute-start | bytes 786440 | tf_op jit(solution)/shard_map/ppermute | solution.py:368
  85.0 6.9 %collective-permute-start.2 = (bf16[1,128,768]{2,1,0:T(8,128)(2,1)S(1)}, bf16[1,128,768]{2,1,0:T(8,128)(2,1)S(1)}, u32[]{:S(2)}, u32[]{:S(2)}) collective-permute-start(bf16[1,128,768]{2,1,0:T(8,128)(2,1)S(1)} %get-tuple-element.70), channel_id=1, source_target_pairs={{0,32},{32,64},{64,96},{96,0},{1,33},{33,65},{65,97},{97,1},{2,34}... | collective-permute-start | bytes 589832 | tf_op jit(solution)/shard_map/ppermute | solution.py:368
  91.9 15.8 %collective-permute-start.4 = (bf16[1,128,2304]{2,1,0:T(8,128)(2,1)S(1)}, bf16[1,128,2304]{2,1,0:T(8,128)(2,1)S(1)}, u32[]{:S(2)}, u32[]{:S(2)}) collective-permute-start(bf16[1,128,2304]{2,1,0:T(8,128)(2,1)S(1)} %logit_grad.1), channel_id=1, source_target_pairs={{0,96},{32,0},{64,32},{96,64},{1,97},{33,1},{65,33},{97,65},{2,98}... | collective-permute-start | bytes 1769480 | tf_op jit(solution)/shard_map/ppermute | solution.py:368
  92.6 8.2 %collective-permute-start.5 = (bf16[1,128,768]{2,1,0:T(8,128)(2,1)S(1)}, bf16[1,128,768]{2,1,0:T(8,128)(2,1)S(1)}, u32[]{:S(2)}, u32[]{:S(2)}) collective-permute-start(bf16[1,128,768]{2,1,0:T(8,128)(2,1)S(1)} %collective-permute-done.2), channel_id=1, source_target_pairs={{0,32},{32,64},{64,96},{96,0},{1,33},{33,65},{65,97},{97,1},{2,34}... | collective-permute-start | bytes 589832 | tf_op jit(solution)/shard_map/ppermute | solution.py:368
  100.8 6.9 %collective-permute-start.6 = (bf16[1,128,768]{2,1,0:T(8,128)(2,1)S(1)}, bf16[1,128,768]{2,1,0:T(8,128)(2,1)S(1)}, u32[]{:S(2)}, u32[]{:S(2)}) collective-permute-start(bf16[1,128,768]{2,1,0:T(8,128)(2,1)S(1)} %collective-permute-done.5), channel_id=1, source_target_pairs={{0,32},{32,64},{64,96},{96,0},{1,33},{33,65},{65,97},{97,1},{2,34}... | collective-permute-start | bytes 589832 | tf_op jit(solution)/shard_map/ppermute | solution.py:368

commit v5 on v4

--- a/solution.py
+++ b/solution.py
@@ -19,12 +19,12 @@
 TN = ((0,), (0,))
 RANGE = 84.0
 EXTRA = 16
-PIECES = 4
+PIECES = 2
 GROUP = 4
+SPARE = 16
 SHARES = (3, 4, 1)
 PARAMS = pltpu.CompilerParams(vmem_limit_bytes=24 * 1024 * 1024)
 VMEM = pl.BlockSpec(memory_space=pltpu.VMEM)
-SMEM = pl.BlockSpec(memory_space=pltpu.SMEM)
 
 
 def parts(x, count=2):
@@ -61,7 +61,7 @@
 
 
 def put_head(ref, h, value, index=0):
-    ref[index, :, pl.ds(pl.multiple_of(h * DK, DK), DK)] = value
+    ref[index, :BLOCK, pl.ds(pl.multiple_of(h * DK, DK), DK)] = value
 
 
 def pair_of(ref, h):
@@ -102,28 +102,29 @@
         kernel,
         out_shape=[*outs, *[pltpu.HBM(x.shape, x.dtype) for x in kept]],
         in_specs=[hbm] * len(streamed) + [VMEM] * len(ins),
-        out_specs=[SMEM if x.ndim == 1 else VMEM for x in outs] + [hbm] * len(kept),
+        out_specs=[VMEM] * len(outs) + [hbm] * len(kept),
         scratch_shapes=scratch,
         compiler_params=PARAMS,
         name=name,
     )(*[pltpu.with_memory_space_constraint(x, pltpu.HBM) for x in streamed], *ins)
 
 
-def buffers(*arrays):
-    return [pltpu.VMEM(x.shape, x.dtype) for x in arrays] + [pltpu.SemaphoreType.DMA((len(arrays), PIECES))]
-
-
-def piece_of(ref, p):
+def buffers(*arrays, pieces=PIECES):
+    return [pltpu.VMEM(x.shape, x.dtype) for x in arrays] + [pltpu.SemaphoreType.DMA((len(arrays), pieces))]
+
+
+def piece_of(ref, p, pieces):
     if ref.shape[0] == 1:
-        width = ref.shape[2] // PIECES
+        width = ref.shape[2] // pieces
         return ref.at[:, :, pl.ds(p * width, width)]
-    each = ref.shape[0] // PIECES
+    each = ref.shape[0] // pieces
     return ref.at[pl.ds(p * each, each)]
 
 
 def start_piece(sources, targets, sems, p):
+    pieces = sems.shape[1]
     copies = [
-        pltpu.make_async_copy(piece_of(source, p), piece_of(target, p), sems.at[a, p])
+        pltpu.make_async_copy(piece_of(source, p, pieces), piece_of(target, p, pieces), sems.at[a, p])
         for a, (source, target) in enumerate(zip(sources, targets))
     ]
     for copy in copies:
@@ -200,14 +201,13 @@
 
 def attended_kernel(
     query_hbm, gates_hbm, grad_hbm, gain_hbm, coded_ref, run_ref, k_ref, v_ref,
-    q_ref, score_ref, pull_ref, gate_ref, att_ref, state_ref, sums_ref, go_ref,
+    q_ref, score_ref, pull_ref, gate_ref, att_ref, state_ref, sums_ref,
     query_ref, gates_ref, grad_ref, gain_ref, sems,
 ):
     wait = start_copies(
         (query_hbm, gates_hbm, grad_hbm, gain_hbm), (query_ref, gates_ref, grad_ref, gain_ref), sems, v_ref.shape[0]
     )
     lower = triangle(True)
-    go_ref[0] = 1
     totals = [jnp.zeros((BLOCK, DK), F32)] * 2
 
     def turn(h):
@@ -284,11 +284,13 @@
         kept_ref[h, 0] = product(ones_above, terms, NN) - (1.0 - keys * grow) * (shrink * k_part)
 
     def after(h):
-        if (h + 1) % (heads // PIECES) == 0:
+        pieces = sems.shape[1]
+        if (h + 1) % (heads // pieces) == 0:
             copies.extend(
-                start_piece((kept_ref, value_part_ref), (kept_hbm, value_part_hbm), sems, h * PIECES // heads)
+                start_piece((kept_ref, value_part_ref), (kept_hbm, value_part_hbm), sems, h * pieces // heads)
             )
 
+    grads_ref[:, BLOCK:] = jnp.zeros((2, SPARE, grads_ref.shape[2]), BF16)
     together(turn, heads, after=after)
     for copy in copies:
         copy.wait()
@@ -341,7 +343,7 @@
         for index, column, width, target, start in place:
             copies.append(
                 pltpu.make_async_copy(
-                    source.at[pl.ds(index, 1), :, pl.ds(column, width)],
+                    source.at[pl.ds(index, 1), pl.ds(0, BLOCK), pl.ds(column, width)],
                     targets[target].at[:, :, pl.ds(start, width)],
                     sems.at[len(copies)],
                 )
@@ -387,9 +389,8 @@
         jax.ShapeDtypeStruct((1, BLOCK, width), BF16) for width in (around, ahead, beside, columns + beside)
     ]
     kept = jax.ShapeDtypeStruct((heads, 3, BLOCK, DK), F32)
-    flag = jax.ShapeDtypeStruct((1,), jnp.int32)
-
-    both = jax.ShapeDtypeStruct((2, BLOCK, heads * DK), BF16)
+
+    both = jax.ShapeDtypeStruct((2, BLOCK + SPARE, heads * DK), BF16)
     bound, gain = lower_bound[None], norm_gain[None]
 
     run, k_scaled, own_state, v, sent = call(
@@ -397,24 +398,20 @@
         streamed=[forget_logits, values, bound], scratch=buffers(whole, whole, bound),
     )
     sent, decay = call(states_before_kernel, "states_before", [exchange(sent)], [coded, decays])
-    q_scaled, scores, pull, gate_factor, attended, states, mine, go = call(
+    q_scaled, scores, pull, gate_factor, attended, states, mine = call(
         attended_kernel, "attended", [exchange(sent), run, k_scaled, v],
-        [pair, pair, square, square, square, pair, sums, flag], streamed=[queries, gates, output_grad, gain],
+        [pair, pair, square, square, square, pair, sums], streamed=[queries, gates, output_grad, gain],
         scratch=buffers(whole, whole, whole, gain),
     )
     other = lax.ppermute(mine, "tp", [(0, 1), (1, 0)])
     sent, early, kept_now, value_part, k_kept = call(
         early_grads_kernel, "early_grads",
         [mine, other, attended, pull, gate_factor, run, q_scaled, k_scaled, v, own_state, states, scores],
-        [coded, both], kept=[kept, square, pair], scratch=buffers(kept, square) + [pltpu.SemaphoreType.DMA],
+        [coded, both], kept=[kept, square, pair], scratch=buffers(kept, square, pieces=4) + [pltpu.SemaphoreType.DMA],
     )
     early = to_section(early, -1)
-
-    def through(sent, decay):
-        (sent,) = call(states_after_kernel, "states_after", [exchange(sent), decay], [coded])
-        return exchange(sent)
-
-    arrived = lax.cond(go[0] > 0, through, lambda sent, decay: sent, sent, decay)
+    (sent,) = call(states_after_kernel, "states_after", [exchange(sent), decay], [coded])
+    arrived = exchange(sent)
     arrived, early = lax.optimization_barrier((arrived, early))
     first, second, third = call(
         value_grad_kernel, "value_grad", [arrived], [first, second, third], streamed=[value_part, k_kept],

time: 109 us -> 107 us (0.982)
  Pallas kernels: 19.9 us -> 18.1 us
    pallas_call x7, Pallas kernels: 17.9 us -> 16.1 us  [call(): pl.pallas_call(kernel, out_shape=[*outs, *[pltpu.HBM(x.shape, x.dtype) fo...]
where the time goes in v5:
time: 107 us; the launch traced here: 106 us
  blocking collectives  64.1 us (60%)
  Pallas kernels  18.1 us (17%)
  waiting for transfers between devices  15.4 us (14%)
  starting transfers between devices  8.02 us (7%)
    all_to_all x4, blocking collectives, exchange(): return lax.all_to_all(x, 'ctx', 0, 0)  64.1 us
    pallas_call x7, Pallas kernels, call(): pl.pallas_call(kernel, out_shape=[*outs, *[pltpu.HBM(x.shape, x.dtype) fo...  16.1 us
    ppermute x6, waiting for transfers between devices, to_section(): return lax.ppermute(x, 'pipe', [(i, (i + by) % size) for i in range(size)])  14.3 us
    ppermute x6, starting transfers between devices, to_section(): return lax.ppermute(x, 'pipe', [(i, (i + by) % size) for i in range(size)])  7.93 us
  transfers between devices with their start and end apart: 7, of which 4 were waited for; matrix products, arithmetic and copies ran while one was open for 0% of the time, Pallas kernels for 4%

profile of v5, /device:TPU:0, one launch (start us, length us, event | category | flops | bytes accessed | tf_op | source)
XLA Modules:
  0.0 106.4 jit_solution(8630540220124091851)
XLA Ops:
  0.6 2.4 %own_state.1 = (f32[16,128,128]{2,1,0:T(8,128)S(1)}, bf16[16,2,128,128]{3,2,1,0:T(8,128)(2,1)S(1)}, f32[16,128,128]{2,1,0:T(8,128)S(1)}, bf16[16,128,128]{2,1,0:T(8,128)(2,1)S(1)}, bf16[16,144,128]{2,1,0:T(8,128)(2,1)S(1)}) custom-call(bf16[1,128,2048]{2,1,0:T(8,128)(2,1)} %logit_hbm.3, bf16[1,128,2048]{2,1,0:T(8,128)(2,1)} %value_hbm.3, f32[1,1,2048]{2,1,0:T(1,128)} %bitcast.2), custom_call_target="tpu_custom_call" | custom-call | tf_op jit(solution)/shard_map/own_state/pallas_call | solution.py:101
  3.0 20.2 %all_to_all.20.coded_ref = bf16[16,144,128]{2,1,0:T(8,128)(2,1)S(1)} all-to-all(bf16[16,144,128]{2,1,0:T(8,128)(2,1)S(1)} %get-tuple-element.35), channel_id=1, replica_groups=mesh['pipe'=4,'ctx'=16,'tp'=2] {'ctx'}, dimensions={0} | all-to-all | bytes 1179648 | tf_op jit(solution)/shard_map/all_to_all | solution.py:374
  23.2 0.4 states_before.1
  23.6 14.2 %all_to_all.21.coded_ref = bf16[16,144,128]{2,1,0:T(8,128)(2,1)S(1)} all-to-all(bf16[16,144,128]{2,1,0:T(8,128)(2,1)S(1)} %get-tuple-element.36), channel_id=1, replica_groups=mesh['pipe'=4,'ctx'=16,'tp'=2] {'ctx'}, dimensions={0} | all-to-all | bytes 1179648 | tf_op jit(solution)/shard_map/all_to_all | solution.py:374
  37.8 3.1 %attended.1 = (bf16[16,2,128,128]{3,2,1,0:T(8,128)(2,1)S(1)}, bf16[16,2,128,128]{3,2,1,0:T(8,128)(2,1)S(1)}, f32[16,128,128]{2,1,0:T(8,128)S(1)}, f32[16,128,128...) custom-call(bf16[1,128,2048]{2,1,0:T(8,128)(2,1)} %query_hbm.1, ...), custom_call_target="tpu_custom_call" | custom-call | tf_op jit(solution)/shard_map/attended/pallas_call | solution.py:101
  40.9 0.1 collective-permute-start
  41.0 1.2 %collective-permute-done.other_ref = f32[16,128]{1,0:T(8,128)S(1)} collective-permute-done((f32[16,128]{1,0:T(8,128)S(1)}, f32[16,128]{1,0:T(8,128)S(1)}, u32[]{:S(2)}, u32[]{:S(2)}) %collective-permute-start) | collective-permute-done | bytes 8224 | tf_op jit(solution)/shard_map/ppermute | solution.py:406
  42.1 4.6 %early_grads.1 = (bf16[16,144,128]{2,1,0:T(8,128)(2,1)S(1)}, bf16[2,144,2048]{2,1,0:T(8,128)(2,1)S(1)}, f32[16,3,128,128]{3,2,1,0:T(8,128)}, f32[16,128,128]{2,1,0:T(8,128)}, bf16[16,2,128,128]{3,2,1,0:T(8,128)(2,1)}) custom-call(f32[16,128]{1,0:T(8,128)S(1)} %get-tuple-element.40.mine_ref, f32[16,128]{1,0:T(8,128)S(1)} %collective-permute-done.other_ref, ...), custom_call_target="tpu_custom_call" | custom-call | tf_op jit(solution)/shard_map/early_grads/pallas_call | solution.py:101
  46.7 2.8 %collective-permute-start.1 = (bf16[2,144,2048]{2,1,0:T(8,128)(2,1)S(1)}, bf16[2,144,2048]{2,1,0:T(8,128)(2,1)S(1)}, u32[]{:S(2)}, u32[]{:S(2)}) collective-permute-start(bf16[2,144,2048]{2,1,0:T(8,128)(2,1)S(1)} %get-tuple-element.50), channel_id=1, source_target_pairs={{0,96},{32,0},{64,32},{96,64},{1,97},{33,1},{65,33},{97,65},{2,98}... | collective-permute-start | bytes 3538952 | tf_op jit(solution)/shard_map/ppermute | solution.py:370
  49.5 15.4 %all_to_all.22.coded_ref = bf16[16,144,128]{2,1,0:T(8,128)(2,1)S(1)} all-to-all(bf16[16,144,128]{2,1,0:T(8,128)(2,1)S(1)} %get-tuple-element.48), channel_id=1, replica_groups=mesh['pipe'=4,'ctx'=16,'tp'=2] {'ctx'}, dimensions={0} | all-to-all | bytes 1179648 | tf_op jit(solution)/shard_map/all_to_all | solution.py:374
  65.0 0.4 states_after.1
  65.4 14.3 %all_to_all.23.coded_ref = bf16[16,144,128]{2,1,0:T(8,128)(2,1)S(1)} all-to-all(bf16[16,144,128]{2,1,0:T(8,128)(2,1)S(1)} %states_after.1), channel_id=1, replica_groups=mesh['pipe'=4,'ctx'=16,'tp'=2] {'ctx'}, dimensions={0} | all-to-all | bytes 1179648 | tf_op jit(solution)/shard_map/all_to_all | solution.py:374
  79.7 0.0 collective-permute-done.1.refs_0_
  79.7 2.2 %value_grad.1 = (bf16[1,128,768]{2,1,0:T(8,128)(2,1)S(1)}, bf16[1,128,1024]{2,1,0:T(8,128)(2,1)S(1)}, bf16[1,128,256]{2,1,0:T(8,128)(2,1)S(1)}) custom-call(f32[16,128,128]{2,1,0:T(8,128)} %get-tuple-element.55.value_part_hbm, bf16[16,2,128,128]{3,2,1,0:T(8,128)(2,1)} %get-tuple-element.56.k_hbm, bf16[16,144,128]{2,1,0:T(8,128)(2,1)S(1)} %all_to_all.23.coded_ref), custom_call_target="tpu_custom_call" | custom-call | tf_op jit(solution)/shard_map/value_grad/pallas_call | solution.py:101
  81.9 0.9 collective-permute-start.3
  82.8 1.2 %collective-permute-start.2 = (bf16[1,128,768]{2,1,0:T(8,128)(2,1)S(1)}, bf16[1,128,768]{2,1,0:T(8,128)(2,1)S(1)}, u32[]{:S(2)}, u32[]{:S(2)}) collective-permute-start(bf16[1,128,768]{2,1,0:T(8,128)(2,1)S(1)} %get-tuple-element.58), channel_id=1, source_target_pairs={{0,32},{32,64},{64,96},{96,0},{1,33},{33,65},{65,97},{97,1},{2,34}... | collective-permute-start | bytes 589832 | tf_op jit(solution)/shard_map/ppermute | solution.py:370
  84.0 3.0 %logit_grad.1 = bf16[1,128,2304]{2,1,0:T(8,128)(2,1)S(1)} custom-call(bf16[1,128,2048]{2,1,0:T(8,128)(2,1)} %logit_hbm.3, bf16[1,128,2048]{2,1,0:T(8,128)(2,1)} %value_hbm.3, f32[1,1,2048]{2,1,0:T(1,128)} %bitcast.3, f32[16,3,128,128]{3,2,1,0:T(8,128)} %get-tuple-element.53.kept_hbm, bf16[16,144,128]{2,1,0:T(8,128)(2,1)S(1)} %all_to_all.23.coded_ref, ...), custom_call_target="tpu_custom_call" | custom-call | tf_op jit(solution)/shard_map/logit_grad/pallas_call | solution.py:101
  87.0 2.7 %collective-permute-done.2 = bf16[1,128,768]{2,1,0:T(8,128)(2,1)S(1)} collective-permute-done((bf16[1,128,768]{2,1,0:T(8,128)(2,1)S(1)}, bf16[1,128,768]{2,1,0:T(8,128)(2,1)S(1)}, u32[]{:S(2)}, u32[]{:S(2)}) %collective-permute-start.2) | collective-permute-done | bytes 196640 | tf_op jit(solution)/shard_map/ppermute | solution.py:370
  89.7 0.0 collective-permute-done.3.refs_2_
  89.7 0.7 collective-permute-start.4
  90.4 1.3 %collective-permute-start.5 = (bf16[1,128,768]{2,1,0:T(8,128)(2,1)S(1)}, bf16[1,128,768]{2,1,0:T(8,128)(2,1)S(1)}, u32[]{:S(2)}, u32[]{:S(2)}) collective-permute-start(bf16[1,128,768]{2,1,0:T(8,128)(2,1)S(1)} %collective-permute-done.2), channel_id=1, source_target_pairs={{0,32},{32,64},{64,96},{96,0},{1,33},{33,65},{65,97},{97,1},{2,34}... | collective-permute-start | bytes 589832 | tf_op jit(solution)/shard_map/ppermute | solution.py:370
  91.7 6.7 %collective-permute-done.5 = bf16[1,128,768]{2,1,0:T(8,128)(2,1)S(1)} collective-permute-done((bf16[1,128,768]{2,1,0:T(8,128)(2,1)S(1)}, bf16[1,128,768]{2,1,0:T(8,128)(2,1)S(1)}, u32[]{:S(2)}, u32[]{:S(2)}) %collective-permute-start.5) | collective-permute-done | bytes 196640 | tf_op jit(solution)/shard_map/ppermute | solution.py:370
  98.4 1.0 collective-permute-start.6
  99.4 1.0 deliver.2
  100.4 4.9 %collective-permute-done.6.refs_1_ = bf16[1,128,768]{2,1,0:T(8,128)(2,1)S(1)} collective-permute-done((bf16[1,128,768]{2,1,0:T(8,128)(2,1)S(1)}, bf16[1,128,768]{2,1,0:T(8,128)(2,1)S(1)}, u32[]{:S(2)}, u32[]{:S(2)}) %collective-permute-start.6) | collective-permute-done | bytes 196640 | tf_op jit(solution)/shard_map/ppermute | solution.py:370
  105.3 0.0 collective-permute-done.4.refs_0_
  105.3 1.0 deliver.3
Async XLA Ops:
  40.9 1.3 %collective-permute-start = (f32[16,128]{1,0:T(8,128)S(1)}, f32[16,128]{1,0:T(8,128)S(1)}, u32[]{:S(2)}, u32[]{:S(2)}) collective-permute-start(f32[16,128]{1,0:T(8,128)S(1)} %get-tuple-element.40.mine_ref), channel_id=1, source_target_pairs={{0,1},{1,0},{2,3},{3,2},{4,5},{5,4},{6,7},{7,6},{8,9},{9,8},{10,11... | collective-permute-start | bytes 24584 | tf_op jit(solution)/shard_map/ppermute | solution.py:406
  46.7 32.9 %collective-permute-start.1 = (bf16[2,144,2048]{2,1,0:T(8,128)(2,1)S(1)}, bf16[2,144,2048]{2,1,0:T(8,128)(2,1)S(1)}, u32[]{:S(2)}, u32[]{:S(2)}) collective-permute-start(bf16[2,144,2048]{2,1,0:T(8,128)(2,1)S(1)} %get-tuple-element.50), channel_id=1, source_target_pairs={{0,96},{32,0},{64,32},{96,64},{1,97},{33,1},{65,33},{97,65},{2,98}... | collective-permute-start | bytes 3538952 | tf_op jit(solution)/shard_map/ppermute | solution.py:370
  81.9 7.8 %collective-permute-start.3 = (bf16[1,128,1024]{2,1,0:T(8,128)(2,1)S(1)}, bf16[1,128,1024]{2,1,0:T(8,128)(2,1)S(1)}, u32[]{:S(2)}, u32[]{:S(2)}) collective-permute-start(bf16[1,128,1024]{2,1,0:T(8,128)(2,1)S(1)} %get-tuple-element.59), channel_id=1, source_target_pairs={{0,96},{32,0},{64,32},{96,64},{1,97},{33,1},{65,33},{97,65},{2,98}... | collective-permute-start | bytes 786440 | tf_op jit(solution)/shard_map/ppermute | solution.py:370
  82.8 6.9 %collective-permute-start.2 = (bf16[1,128,768]{2,1,0:T(8,128)(2,1)S(1)}, bf16[1,128,768]{2,1,0:T(8,128)(2,1)S(1)}, u32[]{:S(2)}, u32[]{:S(2)}) collective-permute-start(bf16[1,128,768]{2,1,0:T(8,128)(2,1)S(1)} %get-tuple-element.58), channel_id=1, source_target_pairs={{0,32},{32,64},{64,96},{96,0},{1,33},{33,65},{65,97},{97,1},{2,34}... | collective-permute-start | bytes 589832 | tf_op jit(solution)/shard_map/ppermute | solution.py:370
  89.7 15.6 %collective-permute-start.4 = (bf16[1,128,2304]{2,1,0:T(8,128)(2,1)S(1)}, bf16[1,128,2304]{2,1,0:T(8,128)(2,1)S(1)}, u32[]{:S(2)}, u32[]{:S(2)}) collective-permute-start(bf16[1,128,2304]{2,1,0:T(8,128)(2,1)S(1)} %logit_grad.1), channel_id=1, source_target_pairs={{0,96},{32,0},{64,32},{96,64},{1,97},{33,1},{65,33},{97,65},{2,98}... | collective-permute-start | bytes 1769480 | tf_op jit(solution)/shard_map/ppermute | solution.py:370
  90.4 8.0 %collective-permute-start.5 = (bf16[1,128,768]{2,1,0:T(8,128)(2,1)S(1)}, bf16[1,128,768]{2,1,0:T(8,128)(2,1)S(1)}, u32[]{:S(2)}, u32[]{:S(2)}) collective-permute-start(bf16[1,128,768]{2,1,0:T(8,128)(2,1)S(1)} %collective-permute-done.2), channel_id=1, source_target_pairs={{0,32},{32,64},{64,96},{96,0},{1,33},{33,65},{65,97},{97,1},{2,34}... | collective-permute-start | bytes 589832 | tf_op jit(solution)/shard_map/ppermute | solution.py:370
  98.4 6.9 %collective-permute-start.6 = (bf16[1,128,768]{2,1,0:T(8,128)(2,1)S(1)}, bf16[1,128,768]{2,1,0:T(8,128)(2,1)S(1)}, u32[]{:S(2)}, u32[]{:S(2)}) collective-permute-start(bf16[1,128,768]{2,1,0:T(8,128)(2,1)S(1)} %collective-permute-done.5), channel_id=1, source_target_pairs={{0,32},{32,64},{64,96},{96,0},{1,33},{33,65},{65,97},{97,1},{2,34}... | collective-permute-start | bytes 589832 | tf_op jit(solution)/shard_map/ppermute | solution.py:370

commit v6 on v5

--- a/solution.py
+++ b/solution.py
@@ -76,6 +76,10 @@
     return terms[0].astype(F32) + terms[1].astype(F32)
 
 
+def squash(logits):
+    return 1.0 / (1.0 + jnp.exp(-logits.astype(F32)))
+
+
 def forget_of(squashed, bound):
     return bound + (1.0 - bound) * squashed
 
@@ -167,7 +171,7 @@
     for h in range(own_ref.shape[0]):
         wait(h)
         bound = of_head(bound_ref, h)
-        squashed = jax.nn.sigmoid(of_head(logit_ref, h).astype(F32))
+        squashed = squash(of_head(logit_ref, h))
         forget = forget_of(squashed, bound)
         run = product(ones_below, parts(jnp.log(forget), 2), NN)
         k_scaled = parts((1.0 - forget) * jnp.exp(-run))
@@ -327,7 +331,7 @@
         later = decode(coded_ref, h)[0]
         shrink = kept_ref[h, 1]
         bound = of_head(bound_ref, h)
-        squashed = jax.nn.sigmoid(of_head(logit_ref, h).astype(F32))
+        squashed = squash(of_head(logit_ref, h))
         forget = forget_of(squashed, bound)
         log_later = jnp.sum(kept_ref[h, 2] * later, axis=0, keepdims=True)
         k_part = shrink * product([of_head(value_ref, h)], parts(later), NN)
@@ -423,7 +427,7 @@
         logit_grad_kernel, "logit_grad", [arrived, third], [rest],
         streamed=[forget_logits, values, bound, kept_now], scratch=buffers(whole, whole, bound, kept),
     )
-    rest, first, second = lax.optimization_barrier((rest, first, second))
+    first, second = lax.optimization_barrier((first, second))
     rest = to_section(rest, -1)
     for _ in range(lax.axis_size("pipe") - 2):
         first = to_section(first, 1)

time: 107 us -> 107 us (level)
  transfers between devices with their start and end apart: 7 -> 7, of which waited for: 4 -> 6; matrix products, arithmetic and copies ran while one was open for 0% -> 0% of each run, Pallas kernels for 4% -> 4%
where the time goes in v6:
time: 107 us; the launch traced here: 106 us
  blocking collectives  64.1 us (60%)
  Pallas kernels  18.2 us (17%)
  waiting for transfers between devices  15.5 us (14%)
  starting transfers between devices  7.55 us (7%)
    all_to_all x4, blocking collectives, exchange(): return lax.all_to_all(x, 'ctx', 0, 0)  64.1 us
    pallas_call x7, Pallas kernels, call(): pl.pallas_call(kernel, out_shape=[*outs, *[pltpu.HBM(x.shape, x.dtype) fo...  16.3 us
    ppermute x6, waiting for transfers between devices, to_section(): return lax.ppermute(x, 'pipe', [(i, (i + by) % size) for i in range(size)])  14.3 us
    ppermute x6, starting transfers between devices, to_section(): return lax.ppermute(x, 'pipe', [(i, (i + by) % size) for i in range(size)])  7.47 us
  transfers between devices with their start and end apart: 7, of which 6 were waited for; matrix products, arithmetic and copies ran while one was open for 0% of the time, Pallas kernels for 4%

profile of v6, /device:TPU:0, one launch (start us, length us, event | category | flops | bytes accessed | tf_op | source)
XLA Modules:
  0.0 106.2 jit_solution(3194079048335461533)
XLA Ops:
  0.6 2.5 %own_state.1 = (f32[16,128,128]{2,1,0:T(8,128)S(1)}, bf16[16,2,128,128]{3,2,1,0:T(8,128)(2,1)S(1)}, f32[16,128,128]{2,1,0:T(8,128)S(1)}, bf16[16,128,128]{2,1,0:T(8,128)(2,1)S(1)}, bf16[16,144,128]{2,1,0:T(8,128)(2,1)S(1)}) custom-call(bf16[1,128,2048]{2,1,0:T(8,128)(2,1)} %logit_hbm.3, bf16[1,128,2048]{2,1,0:T(8,128)(2,1)} %value_hbm.3, f32[1,1,2048]{2,1,0:T(1,128)} %bitcast.2), custom_call_target="tpu_custom_call" | custom-call | tf_op jit(solution)/shard_map/own_state/pallas_call | solution.py:105
  3.1 20.2 %all_to_all.20.coded_ref = bf16[16,144,128]{2,1,0:T(8,128)(2,1)S(1)} all-to-all(bf16[16,144,128]{2,1,0:T(8,128)(2,1)S(1)} %get-tuple-element.34), channel_id=1, replica_groups=mesh['pipe'=4,'ctx'=16,'tp'=2] {'ctx'}, dimensions={0} | all-to-all | bytes 1179648 | tf_op jit(solution)/shard_map/all_to_all | solution.py:378
  23.3 0.4 states_before.1
  23.7 14.2 %all_to_all.21.coded_ref = bf16[16,144,128]{2,1,0:T(8,128)(2,1)S(1)} all-to-all(bf16[16,144,128]{2,1,0:T(8,128)(2,1)S(1)} %get-tuple-element.35), channel_id=1, replica_groups=mesh['pipe'=4,'ctx'=16,'tp'=2] {'ctx'}, dimensions={0} | all-to-all | bytes 1179648 | tf_op jit(solution)/shard_map/all_to_all | solution.py:378
  37.9 3.1 %attended.1 = (bf16[16,2,128,128]{3,2,1,0:T(8,128)(2,1)S(1)}, bf16[16,2,128,128]{3,2,1,0:T(8,128)(2,1)S(1)}, f32[16,128,128]{2,1,0:T(8,128)S(1)}, f32[16,128,128...) custom-call(bf16[1,128,2048]{2,1,0:T(8,128)(2,1)} %query_hbm.1, ...), custom_call_target="tpu_custom_call" | custom-call | tf_op jit(solution)/shard_map/attended/pallas_call | solution.py:105
  41.0 0.1 collective-permute-start
  41.1 1.2 %collective-permute-done.other_ref = f32[16,128]{1,0:T(8,128)S(1)} collective-permute-done((f32[16,128]{1,0:T(8,128)S(1)}, f32[16,128]{1,0:T(8,128)S(1)}, u32[]{:S(2)}, u32[]{:S(2)}) %collective-permute-start) | collective-permute-done | bytes 8224 | tf_op jit(solution)/shard_map/ppermute | solution.py:410
  42.2 4.6 %early_grads.1 = (bf16[16,144,128]{2,1,0:T(8,128)(2,1)S(1)}, bf16[2,144,2048]{2,1,0:T(8,128)(2,1)S(1)}, f32[16,3,128,128]{3,2,1,0:T(8,128)}, f32[16,128,128]{2,1,0:T(8,128)}, bf16[16,2,128,128]{3,2,1,0:T(8,128)(2,1)}) custom-call(f32[16,128]{1,0:T(8,128)S(1)} %get-tuple-element.39.mine_ref, f32[16,128]{1,0:T(8,128)S(1)} %collective-permute-done.other_ref, ...), custom_call_target="tpu_custom_call" | custom-call | tf_op jit(solution)/shard_map/early_grads/pallas_call | solution.py:105
  46.8 2.8 %collective-permute-start.1 = (bf16[2,144,2048]{2,1,0:T(8,128)(2,1)S(1)}, bf16[2,144,2048]{2,1,0:T(8,128)(2,1)S(1)}, u32[]{:S(2)}, u32[]{:S(2)}) collective-permute-start(bf16[2,144,2048]{2,1,0:T(8,128)(2,1)S(1)} %get-tuple-element.49), channel_id=1, source_target_pairs={{0,96},{32,0},{64,32},{96,64},{1,97},{33,1},{65,33},{97,65},{2,98}... | collective-permute-start | bytes 3538952 | tf_op jit(solution)/shard_map/ppermute | solution.py:374
  49.6 15.4 %all_to_all.22.coded_ref = bf16[16,144,128]{2,1,0:T(8,128)(2,1)S(1)} all-to-all(bf16[16,144,128]{2,1,0:T(8,128)(2,1)S(1)} %get-tuple-element.47), channel_id=1, replica_groups=mesh['pipe'=4,'ctx'=16,'tp'=2] {'ctx'}, dimensions={0} | all-to-all | bytes 1179648 | tf_op jit(solution)/shard_map/all_to_all | solution.py:378
  65.1 0.4 states_after.1
  65.5 14.3 %all_to_all.23.coded_ref = bf16[16,144,128]{2,1,0:T(8,128)(2,1)S(1)} all-to-all(bf16[16,144,128]{2,1,0:T(8,128)(2,1)S(1)} %states_after.1), channel_id=1, replica_groups=mesh['pipe'=4,'ctx'=16,'tp'=2] {'ctx'}, dimensions={0} | all-to-all | bytes 1179648 | tf_op jit(solution)/shard_map/all_to_all | solution.py:378
  79.7 0.0 collective-permute-done.1.refs_0_
  79.7 2.2 %value_grad.1 = (bf16[1,128,768]{2,1,0:T(8,128)(2,1)S(1)}, bf16[1,128,1024]{2,1,0:T(8,128)(2,1)S(1)}, bf16[1,128,256]{2,1,0:T(8,128)(2,1)S(1)}) custom-call(f32[16,128,128]{2,1,0:T(8,128)} %get-tuple-element.54.value_part_hbm, bf16[16,2,128,128]{3,2,1,0:T(8,128)(2,1)} %get-tuple-element.55.k_hbm, bf16[16,144,128]{2,1,0:T(8,128)(2,1)S(1)} %all_to_all.23.coded_ref), custom_call_target="tpu_custom_call" | custom-call | tf_op jit(solution)/shard_map/value_grad/pallas_call | solution.py:105
  82.0 0.9 collective-permute-start.4
  82.9 1.2 %collective-permute-start.3 = (bf16[1,128,768]{2,1,0:T(8,128)(2,1)S(1)}, bf16[1,128,768]{2,1,0:T(8,128)(2,1)S(1)}, u32[]{:S(2)}, u32[]{:S(2)}) collective-permute-start(bf16[1,128,768]{2,1,0:T(8,128)(2,1)S(1)} %get-tuple-element.57), channel_id=1, source_target_pairs={{0,32},{32,64},{64,96},{96,0},{1,33},{33,65},{65,97},{97,1},{2,34}... | collective-permute-start | bytes 589832 | tf_op jit(solution)/shard_map/ppermute | solution.py:374
  84.1 3.1 %logit_grad.1 = bf16[1,128,2304]{2,1,0:T(8,128)(2,1)S(1)} custom-call(bf16[1,128,2048]{2,1,0:T(8,128)(2,1)} %logit_hbm.3, bf16[1,128,2048]{2,1,0:T(8,128)(2,1)} %value_hbm.3, f32[1,1,2048]{2,1,0:T(1,128)} %bitcast.3, f32[16,3,128,128]{3,2,1,0:T(8,128)} %get-tuple-element.52.kept_hbm, bf16[16,144,128]{2,1,0:T(8,128)(2,1)S(1)} %all_to_all.23.coded_ref, ...), custom_call_target="tpu_custom_call" | custom-call | tf_op jit(solution)/shard_map/logit_grad/pallas_call | solution.py:105
  87.2 2.1 %collective-permute-start.2 = (bf16[1,128,2304]{2,1,0:T(8,128)(2,1)S(1)}, bf16[1,128,2304]{2,1,0:T(8,128)(2,1)S(1)}, u32[]{:S(2)}, u32[]{:S(2)}) collective-permute-start(bf16[1,128,2304]{2,1,0:T(8,128)(2,1)S(1)} %logit_grad.1), channel_id=1, source_target_pairs={{0,96},{32,0},{64,32},{96,64},{1,97},{33,1},{65,33},{97,65},{2,98}... | collective-permute-start | bytes 1769480 | tf_op jit(solution)/shard_map/ppermute | solution.py:374
  89.3 0.5 collective-permute-done.3
  89.7 0.3 collective-permute-done.4.refs_2_
  90.0 0.4 collective-permute-start.5
  90.4 7.7 %collective-permute-done.5 = bf16[1,128,768]{2,1,0:T(8,128)(2,1)S(1)} collective-permute-done((bf16[1,128,768]{2,1,0:T(8,128)(2,1)S(1)}, bf16[1,128,768]{2,1,0:T(8,128)(2,1)S(1)}, u32[]{:S(2)}, u32[]{:S(2)}) %collective-permute-start.5) | collective-permute-done | bytes 196640 | tf_op jit(solution)/shard_map/ppermute | solution.py:374
  98.2 0.0 collective-permute-start.6
  98.2 1.0 deliver.2
  99.2 1.9 %collective-permute-done.2.refs_0_ = bf16[1,128,2304]{2,1,0:T(8,128)(2,1)S(1)} collective-permute-done((bf16[1,128,2304]{2,1,0:T(8,128)(2,1)S(1)}, bf16[1,128,2304]{2,1,0:T(8,128)(2,1)S(1)}, u32[]{:S(2)}, u32[]{:S(2)}) %collective-permute-start.2) | collective-permute-done | bytes 589856 | tf_op jit(solution)/shard_map/ppermute | solution.py:374
  101.0 4.0 %collective-permute-done.6.refs_1_ = bf16[1,128,768]{2,1,0:T(8,128)(2,1)S(1)} collective-permute-done((bf16[1,128,768]{2,1,0:T(8,128)(2,1)S(1)}, bf16[1,128,768]{2,1,0:T(8,128)(2,1)S(1)}, u32[]{:S(2)}, u32[]{:S(2)}) %collective-permute-start.6) | collective-permute-done | bytes 196640 | tf_op jit(solution)/shard_map/ppermute | solution.py:374
  105.1 1.0 deliver.3
Async XLA Ops:
  41.0 1.3 %collective-permute-start = (f32[16,128]{1,0:T(8,128)S(1)}, f32[16,128]{1,0:T(8,128)S(1)}, u32[]{:S(2)}, u32[]{:S(2)}) collective-permute-start(f32[16,128]{1,0:T(8,128)S(1)} %get-tuple-element.39.mine_ref), channel_id=1, source_target_pairs={{0,1},{1,0},{2,3},{3,2},{4,5},{5,4},{6,7},{7,6},{8,9},{9,8},{10,11... | collective-permute-start | bytes 24584 | tf_op jit(solution)/shard_map/ppermute | solution.py:410
  46.8 32.9 %collective-permute-start.1 = (bf16[2,144,2048]{2,1,0:T(8,128)(2,1)S(1)}, bf16[2,144,2048]{2,1,0:T(8,128)(2,1)S(1)}, u32[]{:S(2)}, u32[]{:S(2)}) collective-permute-start(bf16[2,144,2048]{2,1,0:T(8,128)(2,1)S(1)} %get-tuple-element.49), channel_id=1, source_target_pairs={{0,96},{32,0},{64,32},{96,64},{1,97},{33,1},{65,33},{97,65},{2,98}... | collective-permute-start | bytes 3538952 | tf_op jit(solution)/shard_map/ppermute | solution.py:374
  82.0 8.0 %collective-permute-start.4 = (bf16[1,128,1024]{2,1,0:T(8,128)(2,1)S(1)}, bf16[1,128,1024]{2,1,0:T(8,128)(2,1)S(1)}, u32[]{:S(2)}, u32[]{:S(2)}) collective-permute-start(bf16[1,128,1024]{2,1,0:T(8,128)(2,1)S(1)} %get-tuple-element.58), channel_id=1, source_target_pairs={{0,96},{32,0},{64,32},{96,64},{1,97},{33,1},{65,33},{97,65},{2,98}... | collective-permute-start | bytes 786440 | tf_op jit(solution)/shard_map/ppermute | solution.py:374
  82.9 6.9 %collective-permute-start.3 = (bf16[1,128,768]{2,1,0:T(8,128)(2,1)S(1)}, bf16[1,128,768]{2,1,0:T(8,128)(2,1)S(1)}, u32[]{:S(2)}, u32[]{:S(2)}) collective-permute-start(bf16[1,128,768]{2,1,0:T(8,128)(2,1)S(1)} %get-tuple-element.57), channel_id=1, source_target_pairs={{0,32},{32,64},{64,96},{96,0},{1,33},{33,65},{65,97},{97,1},{2,34}... | collective-permute-start | bytes 589832 | tf_op jit(solution)/shard_map/ppermute | solution.py:374
  87.2 13.9 %collective-permute-start.2 = (bf16[1,128,2304]{2,1,0:T(8,128)(2,1)S(1)}, bf16[1,128,2304]{2,1,0:T(8,128)(2,1)S(1)}, u32[]{:S(2)}, u32[]{:S(2)}) collective-permute-start(bf16[1,128,2304]{2,1,0:T(8,128)(2,1)S(1)} %logit_grad.1), channel_id=1, source_target_pairs={{0,96},{32,0},{64,32},{96,64},{1,97},{33,1},{65,33},{97,65},{2,98}... | collective-permute-start | bytes 1769480 | tf_op jit(solution)/shard_map/ppermute | solution.py:374
  90.0 8.2 %collective-permute-start.5 = (bf16[1,128,768]{2,1,0:T(8,128)(2,1)S(1)}, bf16[1,128,768]{2,1,0:T(8,128)(2,1)S(1)}, u32[]{:S(2)}, u32[]{:S(2)}) collective-permute-start(bf16[1,128,768]{2,1,0:T(8,128)(2,1)S(1)} %collective-permute-done.3), channel_id=1, source_target_pairs={{0,32},{32,64},{64,96},{96,0},{1,33},{33,65},{65,97},{97,1},{2,34}... | collective-permute-start | bytes 589832 | tf_op jit(solution)/shard_map/ppermute | solution.py:374
  98.2 6.9 %collective-permute-start.6 = (bf16[1,128,768]{2,1,0:T(8,128)(2,1)S(1)}, bf16[1,128,768]{2,1,0:T(8,128)(2,1)S(1)}, u32[]{:S(2)}, u32[]{:S(2)}) collective-permute-start(bf16[1,128,768]{2,1,0:T(8,128)(2,1)S(1)} %collective-permute-done.5), channel_id=1, source_target_pairs={{0,32},{32,64},{64,96},{96,0},{1,33},{33,65},{65,97},{97,1},{2,34}... | collective-permute-start | bytes 589832 | tf_op jit(solution)/shard_map/ppermute | solution.py:374

commit v7 on v6

--- a/solution.py
+++ b/solution.py
@@ -212,6 +212,8 @@
         (query_hbm, gates_hbm, grad_hbm, gain_hbm), (query_ref, gates_ref, grad_ref, gain_ref), sems, v_ref.shape[0]
     )
     lower = triangle(True)
+    for h in range(v_ref.shape[0]):
+        put_pair(state_ref, h, parts(decode(coded_ref, h)[0]))
     totals = [jnp.zeros((BLOCK, DK), F32)] * 2
 
     def turn(h):
@@ -219,8 +221,7 @@
         put_pair(q_ref, h, q_scaled)
         yield True
         scores = product(q_scaled, pair_of(k_ref, h), NT)
-        states = parts(decode(coded_ref, h)[0])
-        put_pair(state_ref, h, states)
+        states = pair_of(state_ref, h)
         yield True
         scores = parts(jnp.where(lower, scores, 0.0))
         put_pair(score_ref, h, scores)
@@ -301,13 +302,15 @@
 
 
 def value_grad_kernel(
-    value_part_hbm, k_hbm, coded_ref, first_ref, second_ref, third_ref, value_part_ref, k_ref, sems
+    value_part_hbm, k_hbm, coded_ref, first_ref, second_ref, third_ref, later_ref, value_part_ref, k_ref, sems
 ):
     heads = k_ref.shape[0]
     wait = start_copies((value_part_hbm, k_hbm), (value_part_ref, k_ref), sems, heads)
     for h in range(heads):
+        put_pair(later_ref, h, parts(decode(coded_ref, h)[0]))
+    for h in range(heads):
         wait(h)
-        v_grad = value_part_ref[h] + product(pair_of(k_ref, h), parts(decode(coded_ref, h)[0]), NT)
+        v_grad = value_part_ref[h] + product(pair_of(k_ref, h), pair_of(later_ref, h), NT)
         start = 0
         for ref in (first_ref, second_ref, third_ref):
             count = ref.shape[2] // DK
@@ -317,7 +320,7 @@
 
 
 def logit_grad_kernel(
-    logit_hbm, value_hbm, bound_hbm, kept_hbm, coded_ref, third_ref, logit_grad_ref,
+    logit_hbm, value_hbm, bound_hbm, kept_hbm, later_ref, third_ref, logit_grad_ref,
     logit_ref, value_ref, bound_ref, kept_ref, sems,
 ):
     heads = kept_ref.shape[0]
@@ -328,13 +331,13 @@
     ones_above = [jnp.where(triangle(False), 1.0, 0.0).astype(BF16)]
     for h in range(heads):
         wait(h)
-        later = decode(coded_ref, h)[0]
+        laters = pair_of(later_ref, h)
         shrink = kept_ref[h, 1]
         bound = of_head(bound_ref, h)
         squashed = squash(of_head(logit_ref, h))
         forget = forget_of(squashed, bound)
-        log_later = jnp.sum(kept_ref[h, 2] * later, axis=0, keepdims=True)
-        k_part = shrink * product([of_head(value_ref, h)], parts(later), NN)
+        log_later = jnp.sum(kept_ref[h, 2] * sum_of(laters), axis=0, keepdims=True)
+        k_part = shrink * product([of_head(value_ref, h)], laters, NN)
         log_grad = log_later - product(ones_above, parts((1.0 - forget) * k_part, 2), NN)
         logit_grad = (kept_ref[h, 0] + log_grad) / forget - k_part
         put_head(logit_grad_ref, h, (logit_grad * (1.0 - bound) * squashed * (1.0 - squashed)).astype(BF16))
@@ -417,14 +420,14 @@
     (sent,) = call(states_after_kernel, "states_after", [exchange(sent), decay], [coded])
     arrived = exchange(sent)
     arrived, early = lax.optimization_barrier((arrived, early))
-    first, second, third = call(
-        value_grad_kernel, "value_grad", [arrived], [first, second, third], streamed=[value_part, k_kept],
+    first, second, third, laters = call(
+        value_grad_kernel, "value_grad", [arrived], [first, second, third, pair], streamed=[value_part, k_kept],
         scratch=buffers(square, pair),
     )
     first = to_section(first, 1)
     second = to_section(second, -1)
     (rest,) = call(
-        logit_grad_kernel, "logit_grad", [arrived, third], [rest],
+        logit_grad_kernel, "logit_grad", [laters, third], [rest],
         streamed=[forget_logits, values, bound, kept_now], scratch=buffers(whole, whole, bound, kept),
     )
     first, second = lax.optimization_barrier((first, second))

time: 107 us -> 107 us (level)
  no operation moved by 1% of the time
where the time goes in v7:
time: 107 us; the launch traced here: 106 us
  blocking collectives  64.1 us (60%)
  Pallas kernels  18 us (17%)
  waiting for transfers between devices  15.9 us (15%)
  starting transfers between devices  7.57 us (7%)
    all_to_all x4, blocking collectives, exchange(): return lax.all_to_all(x, 'ctx', 0, 0)  64.1 us
    pallas_call x7, Pallas kernels, call(): pl.pallas_call(kernel, out_shape=[*outs, *[pltpu.HBM(x.shape, x.dtype) fo...  16 us
    ppermute x6, waiting for transfers between devices, to_section(): return lax.ppermute(x, 'pipe', [(i, (i + by) % size) for i in range(size)])  14.8 us
    ppermute x6, starting transfers between devices, to_section(): return lax.ppermute(x, 'pipe', [(i, (i + by) % size) for i in range(size)])  7.48 us
  transfers between devices with their start and end apart: 7, of which 6 were waited for; matrix products, arithmetic and copies ran while one was open for 0% of the time, Pallas kernels for 4%

profile of v7, /device:TPU:0, one launch (start us, length us, event | category | flops | bytes accessed | tf_op | source)
XLA Modules:
  0.0 106.4 jit_solution(12998576910727705492)
XLA Ops:
  0.6 2.5 %own_state.1 = (f32[16,128,128]{2,1,0:T(8,128)S(1)}, bf16[16,2,128,128]{3,2,1,0:T(8,128)(2,1)S(1)}, f32[16,128,128]{2,1,0:T(8,128)S(1)}, bf16[16,128,128]{2,1,0:T(8,128)(2,1)S(1)}, bf16[16,144,128]{2,1,0:T(8,128)(2,1)S(1)}) custom-call(bf16[1,128,2048]{2,1,0:T(8,128)(2,1)} %logit_hbm.3, bf16[1,128,2048]{2,1,0:T(8,128)(2,1)} %value_hbm.3, f32[1,1,2048]{2,1,0:T(1,128)} %bitcast.2), custom_call_target="tpu_custom_call" | custom-call | tf_op jit(solution)/shard_map/own_state/pallas_call | solution.py:105
  3.1 20.2 %all_to_all.20.coded_ref = bf16[16,144,128]{2,1,0:T(8,128)(2,1)S(1)} all-to-all(bf16[16,144,128]{2,1,0:T(8,128)(2,1)S(1)} %get-tuple-element.35), channel_id=1, replica_groups=mesh['pipe'=4,'ctx'=16,'tp'=2] {'ctx'}, dimensions={0} | all-to-all | bytes 1179648 | tf_op jit(solution)/shard_map/all_to_all | solution.py:381
  23.3 0.4 states_before.1
  23.7 14.2 %all_to_all.21.coded_ref = bf16[16,144,128]{2,1,0:T(8,128)(2,1)S(1)} all-to-all(bf16[16,144,128]{2,1,0:T(8,128)(2,1)S(1)} %get-tuple-element.36), channel_id=1, replica_groups=mesh['pipe'=4,'ctx'=16,'tp'=2] {'ctx'}, dimensions={0} | all-to-all | bytes 1179648 | tf_op jit(solution)/shard_map/all_to_all | solution.py:381
  37.9 3.0 %attended.1 = (bf16[16,2,128,128]{3,2,1,0:T(8,128)(2,1)S(1)}, bf16[16,2,128,128]{3,2,1,0:T(8,128)(2,1)S(1)}, f32[16,128,128]{2,1,0:T(8,128)S(1)}, f32[16,128,128...) custom-call(bf16[1,128,2048]{2,1,0:T(8,128)(2,1)} %query_hbm.1, ...), custom_call_target="tpu_custom_call" | custom-call | tf_op jit(solution)/shard_map/attended/pallas_call | solution.py:105
  40.9 0.1 collective-permute-start
  41.0 1.2 %collective-permute-done.other_ref = f32[16,128]{1,0:T(8,128)S(1)} collective-permute-done((f32[16,128]{1,0:T(8,128)S(1)}, f32[16,128]{1,0:T(8,128)S(1)}, u32[]{:S(2)}, u32[]{:S(2)}) %collective-permute-start) | collective-permute-done | bytes 8224 | tf_op jit(solution)/shard_map/ppermute | solution.py:413
  42.2 4.6 %early_grads.1 = (bf16[16,144,128]{2,1,0:T(8,128)(2,1)S(1)}, bf16[2,144,2048]{2,1,0:T(8,128)(2,1)S(1)}, f32[16,3,128,128]{3,2,1,0:T(8,128)}, f32[16,128,128]{2,1,0:T(8,128)}, bf16[16,2,128,128]{3,2,1,0:T(8,128)(2,1)}) custom-call(f32[16,128]{1,0:T(8,128)S(1)} %get-tuple-element.40.mine_ref, f32[16,128]{1,0:T(8,128)S(1)} %collective-permute-done.other_ref, ...), custom_call_target="tpu_custom_call" | custom-call | tf_op jit(solution)/shard_map/early_grads/pallas_call | solution.py:105
  46.7 2.8 %collective-permute-start.1 = (bf16[2,144,2048]{2,1,0:T(8,128)(2,1)S(1)}, bf16[2,144,2048]{2,1,0:T(8,128)(2,1)S(1)}, u32[]{:S(2)}, u32[]{:S(2)}) collective-permute-start(bf16[2,144,2048]{2,1,0:T(8,128)(2,1)S(1)} %get-tuple-element.50), channel_id=1, source_target_pairs={{0,96},{32,0},{64,32},{96,64},{1,97},{33,1},{65,33},{97,65},{2,98}... | collective-permute-start | bytes 3538952 | tf_op jit(solution)/shard_map/ppermute | solution.py:377
  49.6 15.4 %all_to_all.22.coded_ref = bf16[16,144,128]{2,1,0:T(8,128)(2,1)S(1)} all-to-all(bf16[16,144,128]{2,1,0:T(8,128)(2,1)S(1)} %get-tuple-element.48), channel_id=1, replica_groups=mesh['pipe'=4,'ctx'=16,'tp'=2] {'ctx'}, dimensions={0} | all-to-all | bytes 1179648 | tf_op jit(solution)/shard_map/all_to_all | solution.py:381
  65.0 0.4 states_after.1
  65.4 14.3 %all_to_all.23.coded_ref = bf16[16,144,128]{2,1,0:T(8,128)(2,1)S(1)} all-to-all(bf16[16,144,128]{2,1,0:T(8,128)(2,1)S(1)} %states_after.1), channel_id=1, replica_groups=mesh['pipe'=4,'ctx'=16,'tp'=2] {'ctx'}, dimensions={0} | all-to-all | bytes 1179648 | tf_op jit(solution)/shard_map/all_to_all | solution.py:381
  79.7 0.0 collective-permute-done.1.refs_0_
  79.7 2.2 %value_grad.1 = (bf16[1,128,768]{2,1,0:T(8,128)(2,1)S(1)}, bf16[1,128,1024]{2,1,0:T(8,128)(2,1)S(1)}, bf16[1,128,256]{2,1,0:T(8,128)(2,1)S(1)}, bf16[16,2,128,128]{3,2,1,0:T(8,128)(2,1)S(1)}) custom-call(f32[16,128,128]{2,1,0:T(8,128)} %get-tuple-element.54.value_part_hbm, bf16[16,2,128,128]{3,2,1,0:T(8,128)(2,1)} %get-tuple-element.55.k_hbm, ...), custom_call_target="tpu_custom_call" | custom-call | tf_op jit(solution)/shard_map/value_grad/pallas_call | solution.py:105
  81.8 0.9 collective-permute-start.4
  82.8 1.2 %collective-permute-start.3 = (bf16[1,128,768]{2,1,0:T(8,128)(2,1)S(1)}, bf16[1,128,768]{2,1,0:T(8,128)(2,1)S(1)}, u32[]{:S(2)}, u32[]{:S(2)}) collective-permute-start(bf16[1,128,768]{2,1,0:T(8,128)(2,1)S(1)} %get-tuple-element.59), channel_id=1, source_target_pairs={{0,32},{32,64},{64,96},{96,0},{1,33},{33,65},{65,97},{97,1},{2,34}... | collective-permute-start | bytes 589832 | tf_op jit(solution)/shard_map/ppermute | solution.py:377
  83.9 3.0 %logit_grad.1 = bf16[1,128,2304]{2,1,0:T(8,128)(2,1)S(1)} custom-call(bf16[1,128,2048]{2,1,0:T(8,128)(2,1)} %logit_hbm.3, bf16[1,128,2048]{2,1,0:T(8,128)(2,1)} %value_hbm.3, f32[1,1,2048]{2,1,0:T(1,128)} %bitcast.3, f32[16,3,128,128]{3,2,1,0:T(8,128)} %get-tuple-element.53.kept_hbm, bf16[16,2,128,128]{3,2,1,0:T(8,128)(2,1)S(1)} %get-tuple-element.57.later_ref, ...), custom_call_target="tpu_custom_call" | custom-call | tf_op jit(solution)/shard_map/logit_grad/pallas_call | solution.py:105
  87.0 2.1 %collective-permute-start.2 = (bf16[1,128,2304]{2,1,0:T(8,128)(2,1)S(1)}, bf16[1,128,2304]{2,1,0:T(8,128)(2,1)S(1)}, u32[]{:S(2)}, u32[]{:S(2)}) collective-permute-start(bf16[1,128,2304]{2,1,0:T(8,128)(2,1)S(1)} %logit_grad.1), channel_id=1, source_target_pairs={{0,96},{32,0},{64,32},{96,64},{1,97},{33,1},{65,33},{97,65},{2,98}... | collective-permute-start | bytes 1769480 | tf_op jit(solution)/shard_map/ppermute | solution.py:377
  89.1 0.6 collective-permute-done.3
  89.7 0.3 collective-permute-done.4.refs_2_
  90.0 0.4 collective-permute-start.5
  90.4 8.0 %collective-permute-done.5 = bf16[1,128,768]{2,1,0:T(8,128)(2,1)S(1)} collective-permute-done((bf16[1,128,768]{2,1,0:T(8,128)(2,1)S(1)}, bf16[1,128,768]{2,1,0:T(8,128)(2,1)S(1)}, u32[]{:S(2)}, u32[]{:S(2)}) %collective-permute-start.5) | collective-permute-done | bytes 196640 | tf_op jit(solution)/shard_map/ppermute | solution.py:377
  98.4 0.0 collective-permute-start.6
  98.4 1.0 deliver.2
  99.4 1.6 %collective-permute-done.2.refs_0_ = bf16[1,128,2304]{2,1,0:T(8,128)(2,1)S(1)} collective-permute-done((bf16[1,128,2304]{2,1,0:T(8,128)(2,1)S(1)}, bf16[1,128,2304]{2,1,0:T(8,128)(2,1)S(1)}, u32[]{:S(2)}, u32[]{:S(2)}) %collective-permute-start.2) | collective-permute-done | bytes 589856 | tf_op jit(solution)/shard_map/ppermute | solution.py:377
  100.9 4.3 %collective-permute-done.6.refs_1_ = bf16[1,128,768]{2,1,0:T(8,128)(2,1)S(1)} collective-permute-done((bf16[1,128,768]{2,1,0:T(8,128)(2,1)S(1)}, bf16[1,128,768]{2,1,0:T(8,128)(2,1)S(1)}, u32[]{:S(2)}, u32[]{:S(2)}) %collective-permute-start.6) | collective-permute-done | bytes 196640 | tf_op jit(solution)/shard_map/ppermute | solution.py:377
  105.3 1.0 deliver.3
Async XLA Ops:
  40.9 1.3 %collective-permute-start = (f32[16,128]{1,0:T(8,128)S(1)}, f32[16,128]{1,0:T(8,128)S(1)}, u32[]{:S(2)}, u32[]{:S(2)}) collective-permute-start(f32[16,128]{1,0:T(8,128)S(1)} %get-tuple-element.40.mine_ref), channel_id=1, source_target_pairs={{0,1},{1,0},{2,3},{3,2},{4,5},{5,4},{6,7},{7,6},{8,9},{9,8},{10,11... | collective-permute-start | bytes 24584 | tf_op jit(solution)/shard_map/ppermute | solution.py:413
  46.7 32.9 %collective-permute-start.1 = (bf16[2,144,2048]{2,1,0:T(8,128)(2,1)S(1)}, bf16[2,144,2048]{2,1,0:T(8,128)(2,1)S(1)}, u32[]{:S(2)}, u32[]{:S(2)}) collective-permute-start(bf16[2,144,2048]{2,1,0:T(8,128)(2,1)S(1)} %get-tuple-element.50), channel_id=1, source_target_pairs={{0,96},{32,0},{64,32},{96,64},{1,97},{33,1},{65,33},{97,65},{2,98}... | collective-permute-start | bytes 3538952 | tf_op jit(solution)/shard_map/ppermute | solution.py:377
  81.8 8.2 %collective-permute-start.4 = (bf16[1,128,1024]{2,1,0:T(8,128)(2,1)S(1)}, bf16[1,128,1024]{2,1,0:T(8,128)(2,1)S(1)}, u32[]{:S(2)}, u32[]{:S(2)}) collective-permute-start(bf16[1,128,1024]{2,1,0:T(8,128)(2,1)S(1)} %get-tuple-element.60), channel_id=1, source_target_pairs={{0,96},{32,0},{64,32},{96,64},{1,97},{33,1},{65,33},{97,65},{2,98}... | collective-permute-start | bytes 786440 | tf_op jit(solution)/shard_map/ppermute | solution.py:377
  82.8 6.9 %collective-permute-start.3 = (bf16[1,128,768]{2,1,0:T(8,128)(2,1)S(1)}, bf16[1,128,768]{2,1,0:T(8,128)(2,1)S(1)}, u32[]{:S(2)}, u32[]{:S(2)}) collective-permute-start(bf16[1,128,768]{2,1,0:T(8,128)(2,1)S(1)} %get-tuple-element.59), channel_id=1, source_target_pairs={{0,32},{32,64},{64,96},{96,0},{1,33},{33,65},{65,97},{97,1},{2,34}... | collective-permute-start | bytes 589832 | tf_op jit(solution)/shard_map/ppermute | solution.py:377
  87.0 14.0 %collective-permute-start.2 = (bf16[1,128,2304]{2,1,0:T(8,128)(2,1)S(1)}, bf16[1,128,2304]{2,1,0:T(8,128)(2,1)S(1)}, u32[]{:S(2)}, u32[]{:S(2)}) collective-permute-start(bf16[1,128,2304]{2,1,0:T(8,128)(2,1)S(1)} %logit_grad.1), channel_id=1, source_target_pairs={{0,96},{32,0},{64,32},{96,64},{1,97},{33,1},{65,33},{97,65},{2,98}... | collective-permute-start | bytes 1769480 | tf_op jit(solution)/shard_map/ppermute | solution.py:377
  90.0 8.4 %collective-permute-start.5 = (bf16[1,128,768]{2,1,0:T(8,128)(2,1)S(1)}, bf16[1,128,768]{2,1,0:T(8,128)(2,1)S(1)}, u32[]{:S(2)}, u32[]{:S(2)}) collective-permute-start(bf16[1,128,768]{2,1,0:T(8,128)(2,1)S(1)} %collective-permute-done.3), channel_id=1, source_target_pairs={{0,32},{32,64},{64,96},{96,0},{1,33},{33,65},{65,97},{97,1},{2,34}... | collective-permute-start | bytes 589832 | tf_op jit(solution)/shard_map/ppermute | solution.py:377
  98.4 6.9 %collective-permute-start.6 = (bf16[1,128,768]{2,1,0:T(8,128)(2,1)S(1)}, bf16[1,128,768]{2,1,0:T(8,128)(2,1)S(1)}, u32[]{:S(2)}, u32[]{:S(2)}) collective-permute-start(bf16[1,128,768]{2,1,0:T(8,128)(2,1)S(1)} %collective-permute-done.5), channel_id=1, source_target_pairs={{0,32},{32,64},{64,96},{96,0},{1,33},{33,65},{65,97},{97,1},{2,34}... | collective-permute-start | bytes 589832 | tf_op jit(solution)/shard_map/ppermute | solution.py:377
